TPU v7x, 32 devices: a whole 2x2x4 slice. The times are simulated.
32 devices in a mesh: dp: 4 (over x, core), expert: 2 (over y), seq: 4 (over z).
Axes of the slice: x: 2, y: 2, z: 4, core: 2. Of those that a mesh axis runs over, the one named last changes fastest.
Arguments:
- tokens: bfloat16 [4096, 4096], P(('dp', 'expert', 'seq')), may hold values from -6 to 6
- out_grad: bfloat16 [4096, 4096], P(('dp', 'expert', 'seq')), may hold values from -1.5 to 1.5
- gate_prob: bfloat16 [4096], P(('dp', 'expert', 'seq')), may hold values from 0.099609375 to 1
- expert_ids: int32 [4096, 1], P(('dp', 'expert', 'seq')), may hold values from 0 to 1; in each aligned block of 128 rows (0 to 127, 128 to 255, ...) at most 68 rows name the same one
- w_gate: bfloat16 [2, 4096, 1536], P('expert', None, 'seq'), may hold values from -0.09375 to 0.09375
- w_up: bfloat16 [2, 4096, 1536], P('expert', None, 'seq'), may hold values from -0.09375 to 0.09375
- w_down: bfloat16 [2, 1536, 4096], P('expert', 'seq'), may hold values from -0.15625 to 0.15625
Outputs:
- token_grad: bfloat16 [4096, 4096], P(('dp', 'expert', 'seq'))
- gate_grad: bfloat16 [4096], P(('dp', 'expert', 'seq'))
- gate_w_grad: bfloat16 [2, 4096, 1536], P('expert', 'dp', 'seq')
- up_w_grad: bfloat16 [2, 4096, 1536], P('expert', 'dp', 'seq')
- down_w_grad: bfloat16 [2, 1536, 4096], P('expert', 'seq', 'dp')
Inputs may be any that keep to these rules, and one draw needn't show every extreme that they name: `expert_ids`: in the 128 rows of one device no expert is named more than 68 times, a bound that some block reaches.
All inputs are finite; a program needn't handle non-finite values.
Results may differ from a plain program's by a relative error of at most 0.009.
Values may be sent and summed in bfloat16 or wider, within the bound.
No kernel may reach another device: no remote copies, remote signals or barrier semaphores. Data moves between devices by JAX's collectives and lax.ppermute only.
A program may use at most 192 MiB of HBM per device.

v0:
```python
import jax
import jax.numpy as jnp
from jax import lax
from jax.sharding import PartitionSpec as P

TOP = 1


def spread(array, copies_count):
    lead = array.shape[0]
    grown = jnp.broadcast_to(array[:, None], (lead, copies_count) + array.shape[1:])
    return grown.reshape((lead * copies_count,) + array.shape[1:])


def body(tokens, out_grad, gate_prob, expert_ids, w_gate, w_up, w_down):
    expert_count = lax.axis_size("expert")
    seq_count = lax.axis_size("seq")
    tok_rows, feat_width = tokens.shape
    capacity = tok_rows * TOP * 17 // (16 * expert_count)
    slot_total = expert_count * capacity
    route = expert_ids[:, 0]
    onehot = (route[:, None] == jnp.arange(expert_count)[None, :]).astype(jnp.int32)
    before = jnp.cumsum(onehot, axis=0) - onehot
    slot_index = jnp.sum(before * onehot, axis=1)
    target = route * capacity + slot_index
    placer = jnp.arange(slot_total)[:, None] == target[None, :]
    placer_bf = placer.astype(jnp.bfloat16)
    packed_x = jnp.dot(placer_bf, tokens, preferred_element_type=jnp.float32).astype(jnp.bfloat16)
    packed_dy = jnp.dot(placer_bf, out_grad, preferred_element_type=jnp.float32).astype(
        jnp.bfloat16
    )
    packed_p = jnp.sum(
        jnp.where(placer, gate_prob[None, :].astype(jnp.float32), 0.0), axis=1
    ).astype(jnp.bfloat16)
    packed_x = packed_x.reshape(expert_count, capacity, feat_width)
    packed_dy = packed_dy.reshape(expert_count, capacity, feat_width)
    packed_p = packed_p.reshape(expert_count, capacity)
    arrived_x, arrived_dy, arrived_p = (
        lax.all_to_all(
            spread(packed_x, seq_count), ("expert", "seq"), split_axis=0, concat_axis=0, tiled=True
        ),
        lax.all_to_all(
            spread(packed_dy, seq_count), ("expert", "seq"), split_axis=0, concat_axis=0, tiled=True
        ),
        lax.all_to_all(
            spread(packed_p, seq_count), ("expert", "seq"), split_axis=0, concat_axis=0, tiled=True
        ),
    )
    x_rows = arrived_x.reshape(-1, feat_width)
    dy_rows = arrived_dy.reshape(-1, feat_width)
    p_rows = arrived_p.reshape(-1).astype(jnp.float32)
    gate_local = w_gate[0]
    up_local = w_up[0]
    down_local = w_down[0]
    contract_last = (((1,), (1,)), ((), ()))
    contract_first = (((0,), (0,)), ((), ()))
    gate_pre = jnp.dot(x_rows, gate_local, preferred_element_type=jnp.float32)
    up_pre = jnp.dot(x_rows, up_local, preferred_element_type=jnp.float32)
    sigmoid_gate = jax.nn.sigmoid(gate_pre)
    activated = gate_pre * sigmoid_gate
    hidden = activated * up_pre
    hidden_grad = lax.dot_general(
        dy_rows, down_local, contract_last, preferred_element_type=jnp.float32
    )
    gate_part = jnp.sum(hidden * hidden_grad, axis=1)
    scaled_grad = p_rows[:, None] * hidden_grad
    gate_delta = (
        scaled_grad * up_pre * sigmoid_gate * (1.0 + gate_pre * (1.0 - sigmoid_gate))
    ).astype(jnp.bfloat16)
    up_delta = (scaled_grad * activated).astype(jnp.bfloat16)
    token_part = lax.dot_general(
        gate_delta, gate_local, contract_last, preferred_element_type=jnp.float32
    )
    token_part = token_part + lax.dot_general(
        up_delta, up_local, contract_last, preferred_element_type=jnp.float32
    )
    hidden_bf = hidden.astype(jnp.bfloat16)
    scaled_dy = (dy_rows.astype(jnp.float32) * p_rows[:, None]).astype(jnp.bfloat16)
    term_gate = lax.dot_general(
        x_rows, gate_delta, contract_first, preferred_element_type=jnp.float32
    )
    term_up = lax.dot_general(x_rows, up_delta, contract_first, preferred_element_type=jnp.float32)
    term_down = lax.dot_general(
        scaled_dy, hidden_bf, contract_first, preferred_element_type=jnp.float32
    )
    summed = lax.psum_scatter(
        jnp.concatenate([term_gate, term_up, term_down], axis=1).astype(jnp.bfloat16),
        "dp",
        scatter_dimension=0,
        tiled=True,
    ).astype(jnp.float32)
    shard_width = gate_local.shape[1]
    gate_w_grad = summed[:, :shard_width].astype(jnp.bfloat16)[None]
    up_w_grad = summed[:, shard_width : 2 * shard_width].astype(jnp.bfloat16)[None]
    down_w_grad = summed[:, 2 * shard_width :].T.astype(jnp.bfloat16)[None]
    back_x, back_g = (
        lax.all_to_all(
            token_part.astype(jnp.bfloat16).reshape(expert_count * seq_count, capacity, feat_width),
            ("expert", "seq"),
            split_axis=0,
            concat_axis=0,
            tiled=True,
        ),
        lax.all_to_all(
            gate_part.astype(jnp.bfloat16).reshape(expert_count * seq_count, capacity),
            ("expert", "seq"),
            split_axis=0,
            concat_axis=0,
            tiled=True,
        ),
    )
    summed_x = jnp.sum(
        back_x.reshape(expert_count, seq_count, capacity, feat_width).astype(jnp.float32), axis=1
    )
    summed_g = jnp.sum(
        back_g.reshape(expert_count, seq_count, capacity).astype(jnp.float32), axis=1
    )
    home_x = summed_x.astype(jnp.bfloat16)
    home_g = summed_g.astype(jnp.bfloat16)
    token_grad = lax.dot_general(
        placer_bf,
        home_x.reshape(slot_total, feat_width),
        contract_first,
        preferred_element_type=jnp.float32,
    ).astype(jnp.bfloat16)
    gate_grad = jnp.sum(
        jnp.where(placer, home_g.reshape(slot_total)[:, None].astype(jnp.float32), 0.0), axis=0
    ).astype(jnp.bfloat16)
    return (token_grad, gate_grad, gate_w_grad, up_w_grad, down_w_grad)


def solution(mesh):
    placed = (
        P(("dp", "expert", "seq"), None),
        P(("dp", "expert", "seq"), None),
        P(("dp", "expert", "seq")),
        P(("dp", "expert", "seq"), None),
        P("expert", None, "seq"),
        P("expert", None, "seq"),
        P("expert", "seq", None),
    )
    return jax.shard_map(
        body,
        mesh=mesh,
        in_specs=placed,
        out_specs=(
            P(("dp", "expert", "seq"), None),
            P(("dp", "expert", "seq")),
            P("expert", "dp", "seq"),
            P("expert", "dp", "seq"),
            P("expert", "seq", "dp"),
        ),
        check_vma=False,
    )
```

profile of v0, /device:TPU:8, one launch (start us, length us, event | category | flops | bytes accessed | tf_op | source)
XLA Modules:
  0.0 431.8 jit_solution(9860782493912268958)
XLA Ops:
  7.2 0.0 copy-start
  7.2 0.9 fusion.13
  8.1 0.2 reduce_window_sum.11
  8.2 0.8 select_reduce_fusion.2
  9.1 0.7 multiply_add_fusion
  9.7 2.7 convolution_convert_fusion.3
  12.4 2.5 broadcast_in_dim.61
  14.9 4.0 broadcast_in_dim.62
  18.9 6.3 %all-to-all-start.2 = ((bf16[8,68,4096]{2,1,0:T(8,128)(2,1)}), bf16[8,68,4096]{2,1,0:T(8,128)(2,1)}, u32[]{:S(2)}, u32[]{:S(2)}) async-start(bf16[8,68,4096]{2,1,0:T(8,128)(2,1)} %bitcast.44), calls=%async_computation.2 | async-start | bytes 9437184 | tf_op jit(solution)/shard_map/all_to_all | solution.py:39
  25.2 2.7 convolution_convert_fusion.4
  27.9 2.5 broadcast_in_dim.59
  30.4 95.7 %all-to-all-done.2 = bf16[8,68,4096]{2,1,0:T(8,128)(2,1)} async-done(((bf16[8,68,4096]{2,1,0:T(8,128)(2,1)}), bf16[8,68,4096]{2,1,0:T(8,128)(2,1)}, u32[]{:S(2)}, u32[]{:S(2)}) %all-to-all-start.2) | async-done | bytes 4456480 | tf_op jit(solution)/shard_map/all_to_all | solution.py:39
  126.1 4.1 broadcast_in_dim.60
  130.2 9.0 %all-to-all-start.1 = ((bf16[8,68,4096]{2,1,0:T(8,128)(2,1)}), bf16[8,68,4096]{2,1,0:T(8,128)(2,1)}, u32[]{:S(2)}, u32[]{:S(2)}) async-start(bf16[8,68,4096]{2,1,0:T(8,128)(2,1)} %bitcast.43), calls=%async_computation.1 | async-start | bytes 9437184 | tf_op jit(solution)/shard_map/all_to_all | solution.py:42
  139.2 5.2 %reshape.93 = bf16[544,4096]{1,0:T(8,128)(2,1)} reshape(bf16[8,68,4096]{2,1,0:T(8,128)(2,1)} %all-to-all-done.2) | data formatting | bytes 8912896 | tf_op jit(solution)/shard_map/reshape | solution.py:49
  144.4 0.0 copy-done
  144.4 5.8 %fusion.3 = f32[544,384]{1,0:T(8,128)} fusion(bf16[544,4096]{1,0:T(8,128)(2,1)} %reshape.93, bf16[1,4096,384]{2,1,0:T(8,128)(2,1)S(1)} %copy-done), kind=kOutput, calls=%fused_computation.13 | convolution fusion | flops 1711276032 | bytes 8437760 | tf_op jit(solution)/shard_map/dot_general | solution.py:57
  150.2 0.0 copy-done.1
  150.2 0.0 copy-done.4
  150.2 3.4 fusion.6
  153.5 85.7 %all-to-all-done.1 = bf16[8,68,4096]{2,1,0:T(8,128)(2,1)} async-done(((bf16[8,68,4096]{2,1,0:T(8,128)(2,1)}), bf16[8,68,4096]{2,1,0:T(8,128)(2,1)}, u32[]{:S(2)}, u32[]{:S(2)}) %all-to-all-start.1) | async-done | bytes 4456480 | tf_op jit(solution)/shard_map/all_to_all | solution.py:42
  239.2 5.2 %reshape.91 = bf16[544,4096]{1,0:T(8,128)(2,1)} reshape(bf16[8,68,4096]{2,1,0:T(8,128)(2,1)} %all-to-all-done.1) | data formatting | bytes 8912896 | tf_op jit(solution)/shard_map/reshape | solution.py:50
  244.5 7.1 %multiply_reduce_fusion = (bf16[544]{0:T(1024)(128)(2,1)S(1)}, f32[544,384]{1,0:T(8,128)}) fusion(f32[544,384]{1,0:T(8,128)} %fusion.6, f32[544,384]{1,0:T(8,128)} %fusion.3, bf16[544,4096]{1,0:T(8,128)(2,1)} %reshape.91, bf16[1,384,4096]{2,1,0:T(8,128)(2,1)} %param.13), kind=kOutput, calls=%fused_computation.20 | convolution fusion | flops 1712737792 | bytes 10110016 | tf_op jit(solution)/shard_map/dot_general | solution.py:62
  251.5 0.7 convert_element_type.118
  252.2 7.7 %all-to-all-start.4 = ((bf16[8,1,68]{2,1,0:T(2,128)(2,1)}), bf16[8,1,68]{2,1,0:T(2,128)(2,1)S(1)}, u32[]{:S(2)}, u32[]{:S(2)}) async-start(bf16[8,1,68]{2,1,0:T(2,128)(2,1)} %convert_element_type.118), calls=%async_computation.4 | async-start | bytes 8192 | tf_op jit(solution)/shard_map/all_to_all | solution.py:104
  259.9 0.0 reduce-scatter.2.cloned.1.call-start
  259.9 0.0 copy-done.10
  259.9 4.9 %all-to-all-done.4 = bf16[8,1,68]{2,1,0:T(2,128)(2,1)S(1)} async-done(((bf16[8,1,68]{2,1,0:T(2,128)(2,1)}), bf16[8,1,68]{2,1,0:T(2,128)(2,1)S(1)}, u32[]{:S(2)}, u32[]{:S(2)}) %all-to-all-start.4) | async-done | bytes 1120 | tf_op jit(solution)/shard_map/all_to_all | solution.py:104
  264.9 0.1 reshape.99
  264.9 0.6 select_reduce_fusion
  265.6 0.1 convert_element_type.98
  265.7 8.8 %all_to_all.30 = bf16[8,1,68]{2,1,0:T(2,128)(2,1)S(1)} all-to-all(bf16[8,1,68]{2,1,0:T(2,128)(2,1)S(1)} %copy.23), channel_id=1, replica_groups=mesh['dp'=4,'expert'=2,'seq'=4] {'expert','seq'}, dimensions={0} | all-to-all | bytes 2176 | tf_op jit(solution)/shard_map/all_to_all | solution.py:45
  274.5 0.1 reshape.98
  274.6 0.0 copy-start.8
  274.6 0.0 copy-start.9
  274.6 0.0 slice-start.1
  274.6 5.7 %convolution_convert_fusion = bf16[4096,384]{0,1:T(8,128)(2,1)S(1)} fusion(bf16[544,4096]{1,0:T(8,128)(2,1)} %reshape.91, f32[544]{0:T(1024)S(1)} %reshape.98, f32[544,384]{1,0:T(8,128)} %fusion.6, f32[544,384]{1,0:T(8,128)} %fusion.3), kind=kOutput, calls=%fused_computation.3 | convolution fusion | flops 1720786944 | bytes 9275520 | tf_op jit(solution)/shard_map/dot_general | solution.py:83
  280.3 0.0 copy-done.7
  280.3 0.0 copy-done.8
  280.4 0.0 copy-done.9
  280.4 0.5 multiply_convert_fusion.2
  280.8 0.0 copy-start.2
  280.8 0.0 copy-start.6
  280.9 0.0 slice-done
  280.9 0.0 slice-done.1
  280.9 2.9 convolution_convert_fusion.1
  283.8 0.0 copy-done.2
  283.8 0.0 copy-done.6
  283.8 2.9 convolution_convert_fusion.2
  286.7 4.3 %pad_maximum_fusion = bf16[4096,1152]{0,1:T(8,128)(2,1)} fusion(bf16[4096,384]{0,1:T(8,128)(2,1)S(1)} %convolution_convert_fusion, bf16[4096,384]{0,1:T(8,128)(2,1)S(1)} %convolution_convert_fusion.1, bf16[4096,384]{0,1:T(8,128)(2,1)S(1)} %convolution_convert_fusion.2), kind=kLoop, calls=%fused_computation | loop fusion | flops 28311552 | bytes 18874368 | tf_op jit(solution)/shard_map/concatenate | solution.py:87
  291.0 0.0 reduce-scatter.2.cloned.1.call-update
  291.1 0.0 copy-start.3
  291.1 0.0 copy-start.5
  291.1 3.7 fusion.1
  294.7 0.0 copy-done.3
  294.8 5.3 %add_convert_fusion = bf16[544,4096]{1,0:T(8,128)(2,1)} fusion(f32[544,4096]{1,0:T(8,128)S(1)} %fusion.1, bf16[544,384]{1,0:T(8,128)(2,1)S(1)} %copy-done.3, bf16[1,4096,384]{2,1,0:T(8,128)(2,1)S(1)} %copy-done.5), kind=kOutput, calls=%fused_computation.2 | convolution fusion | flops 1715732480 | bytes 16932864 | tf_op jit(solution)/shard_map/dot_general | solution.py:74
  300.0 6.0 %reshape.94 = bf16[8,68,4096]{2,1,0:T(8,128)(2,1)} reshape(bf16[544,4096]{1,0:T(8,128)(2,1)} %add_convert_fusion) | data formatting | bytes 8912896 | tf_op jit(solution)/shard_map/reshape | solution.py:98
  306.0 104.1 %all_to_all.31 = bf16[8,68,4096]{2,1,0:T(8,128)(2,1)S(1)} all-to-all(bf16[8,68,4096]{2,1,0:T(8,128)(2,1)} %reshape.94), channel_id=1, replica_groups=mesh['dp'=4,'expert'=2,'seq'=4] {'expert','seq'}, dimensions={0} | all-to-all | bytes 8912896 | tf_op jit(solution)/shard_map/all_to_all | solution.py:97
  410.1 2.0 bitcast_reduce_fusion
  412.1 2.5 reshape.96
  414.6 2.7 convolution_convert_fusion.5
  417.3 3.1 slice_bitcast_fusion
  420.4 2.3 copy.26
  422.7 2.3 copy.25
  (14 shorter events, 0.1 us)
Async XLA Ops:
  7.2 137.2 %copy-start = (bf16[1,4096,384]{2,1,0:T(8,128)(2,1)S(1)}, bf16[1,4096,384]{2,1,0:T(8,128)(2,1)}, u32[]{:S(2)}) copy-start(bf16[1,4096,384]{2,1,0:T(8,128)(2,1)} %param.11) | copy-start | bytes 9437188
  18.9 107.2 %all-to-all-start.2 = ((bf16[8,68,4096]{2,1,0:T(8,128)(2,1)}), bf16[8,68,4096]{2,1,0:T(8,128)(2,1)}, u32[]{:S(2)}, u32[]{:S(2)}) async-start(bf16[8,68,4096]{2,1,0:T(8,128)(2,1)} %bitcast.44), calls=%async_computation.2 | async-start | bytes 9437184 | tf_op jit(solution)/shard_map/all_to_all | solution.py:39
  130.2 109.0 %all-to-all-start.1 = ((bf16[8,68,4096]{2,1,0:T(8,128)(2,1)}), bf16[8,68,4096]{2,1,0:T(8,128)(2,1)}, u32[]{:S(2)}, u32[]{:S(2)}) async-start(bf16[8,68,4096]{2,1,0:T(8,128)(2,1)} %bitcast.43), calls=%async_computation.1 | async-start | bytes 9437184 | tf_op jit(solution)/shard_map/all_to_all | solution.py:42
  144.4 5.8 %copy-start.1 = (bf16[544,4096]{1,0:T(8,128)(2,1)S(1)}, bf16[544,4096]{1,0:T(8,128)(2,1)}, u32[]{:S(2)}) copy-start(bf16[544,4096]{1,0:T(8,128)(2,1)} %reshape.93) | copy-start | bytes 13369348
  144.4 5.8 %copy-start.4 = (bf16[1,4096,384]{2,1,0:T(8,128)(2,1)S(1)}, bf16[1,4096,384]{2,1,0:T(8,128)(2,1)}, u32[]{:S(2)}) copy-start(bf16[1,4096,384]{2,1,0:T(8,128)(2,1)} %param.12) | copy-start | bytes 9437188
  244.4 15.4 %copy-start.10 = (bf16[128]{0:T(256)(128)(2,1)S(1)}, bf16[128]{0:T(256)(128)(2,1)}, u32[]{:S(2)}) copy-start(bf16[128]{0:T(256)(128)(2,1)} %param.9) | copy-start | bytes 772
  244.5 36.4 %slice-start = ((s8[4456448]{0:T(1024)(128)(4,1)}), s8[262144]{0:T(1024)(128)(4,1)S(1)}, s32[]{:S(2)}) async-start(s8[4456448]{0:T(1024)(128)(4,1)} %bitcast.45), calls=%async_computation.7 | async-start | bytes 524288
  252.2 12.6 %all-to-all-start.4 = ((bf16[8,1,68]{2,1,0:T(2,128)(2,1)}), bf16[8,1,68]{2,1,0:T(2,128)(2,1)S(1)}, u32[]{:S(2)}, u32[]{:S(2)}) async-start(bf16[8,1,68]{2,1,0:T(2,128)(2,1)} %convert_element_type.118), calls=%async_computation.4 | async-start | bytes 8192 | tf_op jit(solution)/shard_map/all_to_all | solution.py:104
  259.9 157.5 %reduce-scatter.2.cloned.1.call-start = ((), (), s32[]{:S(2)}) async-start(), calls=%async_computation.6 | async-start | bytes 11796480 | tf_op jit(solution)/shard_map/reduce_scatter | solution.py:86
  274.6 5.7 %copy-start.7 = (f32[544,384]{1,0:T(8,128)S(1)}, f32[544,384]{1,0:T(8,128)}, u32[]{:S(2)}) copy-start(f32[544,384]{1,0:T(8,128)} %fusion.3) | copy-start | bytes 2506756
  274.6 5.8 %copy-start.8 = (f32[544,384]{1,0:T(8,128)S(1)}, f32[544,384]{1,0:T(8,128)}, u32[]{:S(2)}) copy-start(f32[544,384]{1,0:T(8,128)} %fusion.6) | copy-start | bytes 2506756
  274.6 5.8 %copy-start.9 = (f32[544,384]{1,0:T(8,128)S(1)}, f32[544,384]{1,0:T(8,128)}, u32[]{:S(2)}) copy-start(f32[544,384]{1,0:T(8,128)} %get-tuple-element.38) | copy-start | bytes 2506756
  274.6 6.3 %slice-start.1 = ((s8[4456448]{0:T(1024)(128)(4,1)}), s8[4194304]{0:T(1024)(128)(4,1)S(1)}, s32[]{:S(2)}) async-start(s8[4456448]{0:T(1024)(128)(4,1)} %bitcast.45), calls=%async_computation.8 | async-start | bytes 8388608
  280.8 2.9 copy-start.2
  280.8 2.9 copy-start.6
  291.1 3.7 copy-start.3
  291.1 3.7 copy-start.5
Sparse Core Ops, SparseCore 0:
  291.2 76.5 reduce-scatter.1
where the time goes:
time: 436 us; the launch traced here: 432 us
  waiting for transfers between devices  186 us (43%)
  blocking collectives  113 us (26%)
  matrix products  44.7 us (10%)
  local copies, waits for them, and re-layouts  40.6 us (9%)
  starting transfers between devices  22.9 us (5%)
  between operations  14.2 us (3%)
  other arithmetic  10 us (2%)
    all_to_all x1, blocking collectives, body(): lax.all_to_all(token_part.astype(jnp.bfloat16).reshape(expert_count * seq...  104 us
    all_to_all x1, waiting for transfers between devices, body(): lax.all_to_all(spread(packed_x, seq_count), ('expert', 'seq'), split_axis...  95.7 us
    all_to_all x1, waiting for transfers between devices, body(): lax.all_to_all(spread(packed_dy, seq_count), ('expert', 'seq'), split_axi...  85.7 us
    broadcast_in_dim x5, local copies, waits for them, and re-layouts, spread(): jnp.broadcast_to(array[:, None], (lead, copies_count) + array.shape[1:])  13.1 us
    all_to_all x1, starting transfers between devices, body(): lax.all_to_all(spread(packed_dy, seq_count), ('expert', 'seq'), split_axi...  8.96 us
    all_to_all x1, blocking collectives, body(): lax.all_to_all(spread(packed_p, seq_count), ('expert', 'seq'), split_axis...  8.83 us
  transfers between devices with their start and end apart: 4, of which 3 were waited for; matrix products, arithmetic and copies ran while one was open for 10% of the time, Pallas kernels for 0%

commit v1 on v0

v1 whole, which is shorter than its diff:
```python
import jax
import jax.numpy as jnp
from jax import lax
from jax.sharding import PartitionSpec as P

TOP = 1
BF = jnp.bfloat16
F32 = jnp.float32
CONTRACT_LAST = (((1,), (1,)), ((), ()))
CONTRACT_FIRST = (((0,), (0,)), ((), ()))


def dot(left, right, dims=(((1,), (0,)), ((), ()))):
    return lax.dot_general(left, right, dims, preferred_element_type=F32)


def send_xor(value, axis, mask):
    size = lax.axis_size(axis)
    return lax.ppermute(value, axis, [(i, i ^ mask) for i in range(size)])


def send_home(value, expert_mask, seq_mask):
    if not expert_mask:
        return send_xor(value, "seq", seq_mask) if seq_mask else value
    if not seq_mask:
        return send_xor(value, "expert", expert_mask)
    seq_count = lax.axis_size("seq")
    total = lax.axis_size("expert") * seq_count
    mask = expert_mask * seq_count + seq_mask
    return lax.ppermute(value, ("expert", "seq"), [(i, i ^ mask) for i in range(total)])


def gather_slots(value):
    count = lax.axis_size("seq")
    if count != 4:
        return [value] + [send_xor(value, "seq", j) for j in range(1, count)]
    place = lax.axis_index("seq")
    inner = (place == 1) | (place == 2)
    middle, outward = [(1, 2), (2, 1)], [(1, 0), (2, 3)]
    first = send_xor(value, "seq", 1)
    across = lax.ppermute(value, "seq", middle)
    relayed = lax.ppermute(first, "seq", middle)
    out_near = lax.ppermute(across, "seq", outward)
    out_far = lax.ppermute(relayed, "seq", outward)
    return [
        value,
        first,
        jnp.where(inner, relayed, out_near),
        jnp.where(inner, across, out_far),
    ]


def sum_over_dp(terms):
    count = lax.axis_size("dp")
    place = lax.axis_index("dp")
    rows = terms.shape[0] // count
    held = terms.reshape((count, rows) + terms.shape[1:])
    mask = 1
    while mask < count:
        split = held.reshape((held.shape[0] // 2, 2) + held.shape[1:])
        bit = (place // mask) % 2
        kept = lax.dynamic_index_in_dim(split, bit, 1, keepdims=False)
        given = lax.dynamic_index_in_dim(split, 1 - bit, 1, keepdims=False)
        taken = send_xor(given, "dp", mask)
        held = (kept.astype(F32) + taken.astype(F32)).astype(BF)
        mask *= 2
    return held[0]


def body(tokens, out_grad, gate_prob, expert_ids, w_gate, w_up, w_down):
    expert_count = lax.axis_size("expert")
    seq_count = lax.axis_size("seq")
    tok_rows, feat_width = tokens.shape
    capacity = tok_rows * TOP * 17 // (16 * expert_count)
    room = -(-capacity // 8) * 8
    my_expert = lax.axis_index("expert")
    route = expert_ids[:, 0]
    onehot = (route[:, None] == jnp.arange(expert_count)[None, :]).astype(F32)
    earlier = (jnp.arange(tok_rows)[:, None] > jnp.arange(tok_rows)[None, :]).astype(F32)
    before = dot(earlier, onehot)
    slot_index = jnp.sum(before * onehot, axis=1).astype(jnp.int32)
    block = jnp.bitwise_xor(route, my_expert)
    target = block * room + slot_index
    prob = gate_prob.astype(F32)

    def placer_of(first, last):
        return (first * room + jnp.arange((last - first) * room))[:, None] == target[None, :]

    def pack(first, last):
        placer = placer_of(first, last)
        scaler = jnp.where(placer, prob[None, :], 0.0).astype(BF)
        return dot(placer.astype(BF), tokens).astype(BF), dot(scaler, out_grad).astype(BF)

    packed = [pack(j, j + 1) for j in range(expert_count)]
    swapped_x = [send_xor(packed[j][0], "expert", j) for j in range(1, expert_count)]
    swapped_dy = [send_xor(packed[j][1], "expert", j) for j in range(1, expert_count)]
    pieces_x = [packed[0][0], jnp.concatenate(swapped_x, axis=0)]
    dy_mine = jnp.concatenate([packed[0][1]] + swapped_dy, axis=0)
    near_x, far_x = [gather_slots(piece) for piece in pieces_x]
    slots_dy = gather_slots(dy_mine)
    slots_x = [jnp.concatenate(pair, axis=0) for pair in zip(near_x, far_x)]

    gate_local, up_local, down_local = w_gate[0], w_up[0], w_down[0]
    home_parts = [[] for _ in range(expert_count)]
    gate_parts, gate_deltas, up_deltas, hiddens = [], [], [], []
    for j in range(seq_count):
        x_rows, dy_rows = slots_x[j], slots_dy[j]
        gate_pre = dot(x_rows, gate_local)
        up_pre = dot(x_rows, up_local)
        sigmoid_gate = jax.nn.sigmoid(gate_pre)
        activated = gate_pre * sigmoid_gate
        hidden = activated * up_pre
        scaled_grad = dot(dy_rows, down_local, CONTRACT_LAST)
        gate_parts.append(jnp.sum(hidden * scaled_grad, axis=1).astype(BF))
        gate_delta = (
            scaled_grad * up_pre * sigmoid_gate * (1.0 + gate_pre * (1.0 - sigmoid_gate))
        ).astype(BF)
        up_delta = (scaled_grad * activated).astype(BF)
        token_part = (
            dot(gate_delta, gate_local, CONTRACT_LAST) + dot(up_delta, up_local, CONTRACT_LAST)
        ).astype(BF)
        for k in range(expert_count):
            part = token_part[k * room : (k + 1) * room]
            home_parts[k].append(send_home(part, k, j))
        gate_deltas.append(gate_delta)
        up_deltas.append(up_delta)
        hiddens.append(hidden.astype(BF))

    all_x = jnp.concatenate(slots_x, axis=0)
    all_dy = jnp.concatenate(slots_dy, axis=0)
    gate_w_grad = sum_over_dp(
        dot(all_x, jnp.concatenate(gate_deltas, axis=0), CONTRACT_FIRST).astype(BF)
    )
    up_w_grad = sum_over_dp(
        dot(all_x, jnp.concatenate(up_deltas, axis=0), CONTRACT_FIRST).astype(BF)
    )
    down_w_grad = sum_over_dp(
        dot(all_dy, jnp.concatenate(hiddens, axis=0), CONTRACT_FIRST).astype(BF)
    )

    my_seq = lax.axis_index("seq")
    parts = jnp.stack(gate_parts).reshape(seq_count, expert_count, room)
    flat = parts.transpose(1, 0, 2).reshape(expert_count * seq_count, room)
    total = expert_count * seq_count
    mine = my_expert * seq_count + my_seq
    order = jnp.bitwise_xor(jnp.arange(total), mine)
    swap = (order[:, None] == jnp.arange(total)[None, :]).astype(BF)
    sent = dot(swap, flat).astype(BF)
    back = lax.all_to_all(sent, ("expert", "seq"), split_axis=0, concat_axis=0, tiled=True)
    back = dot(swap, back).reshape(expert_count, seq_count, room)
    home_g = jnp.sum(back, axis=1).reshape(1, expert_count * room)

    home_x = jnp.concatenate(
        [sum(part.astype(F32) for part in home_parts[k]).astype(BF) for k in range(expert_count)],
        axis=0,
    )
    placer = placer_of(0, expert_count)
    token_grad = dot(placer.astype(BF), home_x, CONTRACT_FIRST).astype(BF)
    gate_grad = (jnp.sum(jnp.where(placer, home_g.T, 0.0), axis=0) / prob).astype(BF)
    return (token_grad, gate_grad, gate_w_grad[None], up_w_grad[None], down_w_grad.T[None])


def solution(mesh):
    placed = (
        P(("dp", "expert", "seq"), None),
        P(("dp", "expert", "seq"), None),
        P(("dp", "expert", "seq")),
        P(("dp", "expert", "seq"), None),
        P("expert", None, "seq"),
        P("expert", None, "seq"),
        P("expert", "seq", None),
    )
    return jax.shard_map(
        body,
        mesh=mesh,
        in_specs=placed,
        out_specs=(
            P(("dp", "expert", "seq"), None),
            P(("dp", "expert", "seq")),
            P("expert", "dp", "seq"),
            P("expert", "dp", "seq"),
            P("expert", "seq", "dp"),
        ),
        check_vma=False,
    )
```

time: 436 us -> 335 us (0.77)
  blocking collectives: 113 us -> 0 us
  starting transfers between devices: 22.9 us -> 58.9 us
  waiting for transfers between devices: 186 us -> 152 us
  other arithmetic: 10 us -> 27.9 us
  matrix products: 44.7 us -> 62.5 us
  local copies, waits for them, and re-layouts: 40.6 us -> 27.4 us
  between operations: 14.2 us -> 1.32 us
    all_to_all x3 -> x1, waiting for transfers between devices: 186 us -> 0.01 us  [body(): lax.all_to_all(sent, ('expert', 'seq'), split_axis=0, concat_axis=0, tile...]
    ppermute x0 -> x30, waiting for transfers between devices: none -> 152 us  [the longest x3 47.1 us: gather_slots(): out_far = lax.ppermute(relayed, 'seq', outward)]
    all_to_all x2 -> x0, blocking collectives: 113 us -> none  [the longest x1 104 us: body(): lax.all_to_all(token_part.astype(jnp.bfloat16).reshape(expert_count * seq...]
    ppermute x0 -> x30, starting transfers between devices: none -> 52.9 us  [the longest x15 12.6 us: send_xor(): return lax.ppermute(value, axis, [(i, i ^ mask) for i in range(size)])]
    reshape x4 -> x0, local copies, waits for them, and re-layouts: 18.9 us -> none  [the longest x1 5.97 us: body(): token_part.astype(jnp.bfloat16)]
    dot_general x11 -> x31, matrix products: 44.7 us -> 62.5 us  [dot(): return lax.dot_general(left, right, dims, preferred_element_type=F32)]
    all_to_all x3 -> x1, starting transfers between devices: 22.9 us -> 5.99 us  [body(): lax.all_to_all(sent, ('expert', 'seq'), split_axis=0, concat_axis=0, tile...]
    broadcast_in_dim x6 -> x1, local copies, waits for them, and re-layouts: 16.1 us -> 0.08 us  [body(): jnp.where(placer, home_g.T, 0.0)]
  transfers between devices with their start and end apart: 4 -> 31, of which waited for: 3 -> 13; matrix products, arithmetic and copies ran while one was open for 10% -> 34% of each run, Pallas kernels for 0% -> 0%
where the time goes in v1:
time: 335 us; the launch traced here: 330 us
  waiting for transfers between devices  152 us (45%)
  matrix products  62.5 us (19%)
  starting transfers between devices  58.9 us (18%)
  other arithmetic  27.9 us (8%)
  local copies, waits for them, and re-layouts  27.4 us (8%)
    dot_general x31, matrix products, dot(): return lax.dot_general(left, right, dims, preferred_element_type=F32)  62.5 us
    ppermute x3, waiting for transfers between devices, gather_slots(): out_far = lax.ppermute(relayed, 'seq', outward)  47.1 us
    ppermute x3, waiting for transfers between devices, send_home(): lax.ppermute(value, ('expert', 'seq'), [(i, i ^ mask) for i in range(tota...  42.8 us
    ppermute x15, waiting for transfers between devices, send_xor(): return lax.ppermute(value, axis, [(i, i ^ mask) for i in range(size)])  40.1 us
    ppermute x3, waiting for transfers between devices, gather_slots(): out_near = lax.ppermute(across, 'seq', outward)  17.9 us
    ppermute x15, starting transfers between devices, send_xor(): return lax.ppermute(value, axis, [(i, i ^ mask) for i in range(size)])  12.6 us
    unnamed x81, local copies, waits for them, and re-layouts  11.5 us
    ppermute x3, starting transfers between devices, gather_slots(): out_near = lax.ppermute(across, 'seq', outward)  10 us
  transfers between devices with their start and end apart: 31, of which 13 were waited for; matrix products, arithmetic and copies ran while one was open for 34% of the time, Pallas kernels for 0%

profile of v1, /device:TPU:8, one launch (start us, length us, event | category | flops | bytes accessed | tf_op | source)
XLA Modules:
  0.0 330.4 jit_solution(14166266780354859672)
XLA Ops:
  2.5 2.6 constant_dynamic-update-slice_fusion.9
  5.0 3.5 %collective-permute-start.10 = (bf16[72,4096]{1,0:T(8,128)(2,1)}, bf16[72,4096]{1,0:T(8,128)(2,1)}, u32[]{:S(2)}, u32[]{:S(2)}) collective-permute-start(bf16[72,4096]{1,0:T(8,128)(2,1)} %get-tuple-element.42), channel_id=1, source_target_pairs={{1,2},{2,1},{5,6},{6,5},{9,10},{10,9},{13,14},{14,13},{17,18},{18,... | collective-permute-start | bytes 1769480 | tf_op jit(solution)/shard_map/ppermute | solution.py:41
  8.6 1.8 convolution_convert_fusion.4
  13.7 2.6 constant_dynamic-update-slice_fusion.12
  16.2 10.8 %collective-permute-done = bf16[72,4096]{1,0:T(8,128)(2,1)} collective-permute-done((bf16[72,4096]{1,0:T(8,128)(2,1)}, bf16[72,4096]{1,0:T(8,128)(2,1)}, u32[]{:S(2)}, u32[]{:S(2)}) %collective-permute-start) | collective-permute-done | bytes 589856 | tf_op jit(solution)/shard_map/ppermute | solution.py:19
  27.0 2.2 pad_maximum_fusion
  29.2 2.0 collective-permute-start.2
  31.2 2.3 collective-permute-start.7
  33.6 4.6 %collective-permute-done.1 = bf16[72,4096]{1,0:T(8,128)(2,1)} collective-permute-done((bf16[72,4096]{1,0:T(8,128)(2,1)}, bf16[72,4096]{1,0:T(8,128)(2,1)}, u32[]{:S(2)}, u32[]{:S(2)}) %collective-permute-start.1) | collective-permute-done | bytes 589856 | tf_op jit(solution)/shard_map/ppermute | solution.py:19
  38.2 1.7 collective-permute-start.4
  39.9 2.0 constant_dynamic-update-slice_fusion.8
  41.9 2.1 fusion.21
  44.0 2.2 fusion.33
  46.1 2.0 constant_dynamic-update-slice_fusion.11
  48.1 2.9 multiply_reduce_fusion.3
  52.2 2.3 fusion
  54.5 2.1 slice.36
  56.6 2.3 collective-permute-start.13
  58.9 2.0 constant_dynamic-update-slice_fusion.1
  60.9 3.5 %collective-permute-start.9 = (bf16[72,4096]{1,0:T(8,128)(2,1)}, bf16[72,4096]{1,0:T(8,128)(2,1)}, u32[]{:S(2)}, u32[]{:S(2)}) collective-permute-start(bf16[72,4096]{1,0:T(8,128)(2,1)} %collective-permute-done.3), channel_id=1, source_target_pairs={{1,2},{2,1},{5,6},{6,5},{9,10},{10,9},{13,14},{14,13},{17,18},{18,... | collective-permute-start | bytes 1769480 | tf_op jit(solution)/shard_map/ppermute | solution.py:42
  64.4 2.8 collective-permute-done.4
  67.2 3.4 %collective-permute-start.11 = (bf16[72,4096]{1,0:T(8,128)(2,1)}, bf16[72,4096]{1,0:T(8,128)(2,1)S(1)}, u32[]{:S(2)}, u32[]{:S(2)}) collective-permute-start(bf16[72,4096]{1,0:T(8,128)(2,1)} %collective-permute-done.10), channel_id=1, source_target_pairs={{1,0},{2,3},{5,4},{6,7},{9,8},{10,11},{13,12},{14,15},{17,16},{18,... | collective-permute-start | bytes 1769480 | tf_op jit(solution)/shard_map/ppermute | solution.py:43
  70.6 2.0 constant_dynamic-update-slice_fusion
  73.4 1.7 collective-permute-done.13
  75.1 2.3 collective-permute-start.12
  77.4 2.4 collective-permute-done.11
  79.8 5.1 %collective-permute-start.14 = (bf16[72,4096]{1,0:T(8,128)(2,1)}, bf16[72,4096]{1,0:T(8,128)(2,1)}, u32[]{:S(2)}, u32[]{:S(2)}) collective-permute-start(bf16[72,4096]{1,0:T(8,128)(2,1)} %collective-permute-done.13), channel_id=1, source_target_pairs={{1,0},{2,3},{5,4},{6,7},{9,8},{10,11},{13,12},{14,15},{17,16},{18,... | collective-permute-start | bytes 1769480 | tf_op jit(solution)/shard_map/ppermute | solution.py:43
  84.9 2.8 collective-permute-done.9
  87.7 2.1 collective-permute-start.17
  89.8 2.2 constant_dynamic-update-slice_fusion.5
  92.1 2.4 fusion.39
  96.1 3.0 fusion.15
  101.6 2.5 collective-permute-start.6
  104.0 3.2 collective-permute-start.18
  108.8 2.0 constant_dynamic-update-slice_fusion.4
  111.6 2.1 constant_dynamic-update-slice_fusion.3
  113.7 2.6 constant_dynamic-update-slice_fusion.10
  116.2 19.8 %collective-permute-done.18 = bf16[72,4096]{1,0:T(8,128)(2,1)S(1)} collective-permute-done((bf16[72,4096]{1,0:T(8,128)(2,1)}, bf16[72,4096]{1,0:T(8,128)(2,1)S(1)}, u32[]{:S(2)}, u32[]{:S(2)}) %collective-permute-start.18) | collective-permute-done | bytes 589856 | tf_op jit(solution)/shard_map/ppermute | solution.py:44
  136.1 2.0 constant_dynamic-update-slice_fusion.2
  139.6 15.5 %collective-permute-done.8 = bf16[144,4096]{1,0:T(8,128)(2,1)S(1)} collective-permute-done((bf16[144,4096]{1,0:T(8,128)(2,1)}, bf16[144,4096]{1,0:T(8,128)(2,1)S(1)}, u32[]{:S(2)}, u32[]{:S(2)}) %collective-permute-start.8) | collective-permute-done | bytes 1179680 | tf_op jit(solution)/shard_map/ppermute | solution.py:43
  155.2 2.8 fusion.37
  161.9 3.6 %collective-permute-start.16 = (bf16[144,4096]{1,0:T(8,128)(2,1)}, bf16[144,4096]{1,0:T(8,128)(2,1)}, u32[]{:S(2)}, u32[]{:S(2)}) collective-permute-start(bf16[144,4096]{1,0:T(8,128)(2,1)} %collective-permute-done.6), channel_id=1, source_target_pairs={{1,0},{2,3},{5,4},{6,7},{9,8},{10,11},{13,12},{14,15},{17,16},{18,... | collective-permute-start | bytes 3538952 | tf_op jit(solution)/shard_map/ppermute | solution.py:44
  166.7 2.7 fusion.49
  169.5 27.2 %collective-permute-done.16 = bf16[144,4096]{1,0:T(8,128)(2,1)} collective-permute-done((bf16[144,4096]{1,0:T(8,128)(2,1)}, bf16[144,4096]{1,0:T(8,128)(2,1)}, u32[]{:S(2)}, u32[]{:S(2)}) %collective-permute-start.16) | collective-permute-done | bytes 1179680 | tf_op jit(solution)/shard_map/ppermute | solution.py:44
  196.7 2.4 fusion.35
  199.2 1.6 multiply_reduce_fusion
  200.9 2.7 fusion.50
  203.6 5.6 %convolution_convert_fusion = bf16[4096,384]{1,0:T(8,128)(2,1)S(1)} fusion(bf16[576,4096]{1,0:T(8,128)(2,1)} %fusion.50, bf16[144,384]{1,0:T(8,128)(2,1)S(1)} %copy-done.35, bf16[144,384]{1,0:T(8,128)(2,1)S(1)} %copy-done.34, bf16[144,384]{1,0:T(8,128)(2,1)S(1)} %copy-done.32, bf16[144,384]{1,0:T(8,128)(2,1)S(1)} %copy-done.33), kind=kOutput, calls=%fused_computation | convolution fusion | flops 1815281664 | bytes 8306688 | tf_op jit(solution)/shard_map/dot_general | solution.py:14
  209.2 2.0 constant_dynamic-slice_fusion.2
  211.2 2.6 copy.46
  214.6 6.0 %all-to-all-start = ((bf16[8,1,72]{2,1,0:T(2,128)(2,1)}), bf16[8,1,72]{2,1,0:T(2,128)(2,1)S(1)}, u32[]{:S(2)}, u32[]{:S(2)}) async-start(bf16[8,1,72]{2,1,0:T(2,128)(2,1)} %copy.38), calls=%async_computation | async-start | bytes 8192 | tf_op jit(solution)/shard_map/all_to_all | solution.py:149
  220.6 2.6 copy.42
  223.2 3.2 fusion.7
  226.5 5.6 %convolution_convert_fusion.2 = bf16[4096,384]{1,0:T(8,128)(2,1)S(1)} fusion(bf16[576,4096]{1,0:T(8,128)(2,1)} %get-tuple-element.5, bf16[144,384]{1,0:T(8,128)(2,1)S(1)} %copy-done.22, bf16[144,384]{1,0:T(8,128)(2,1)S(1)} %get-tuple-element.26, bf16[144,384]{1,0:T(8,128)(2,1)S(1)} %get-tuple-element.24, bf16[144,384]{1,0:T(8,128)(2,1)S(1)} %get-tuple-element.22), kind=kOutput, calls=%fused_computation.2 | convolution fusion | flops 1815281664 | bytes 8306688 | tf_op jit(solution)/shard_map/dot_general | solution.py:14
  232.2 3.5 %convolution_convert_fusion.1 = bf16[4096,384]{1,0:T(8,128)(2,1)S(1)} fusion(bf16[576,4096]{1,0:T(8,128)(2,1)S(1)} %bitcast.117, bf16[144,384]{1,0:T(8,128)(2,1)S(1)} %copy-done.29, bf16[144,384]{1,0:T(8,128)(2,1)S(1)} %copy-done.28, bf16[144,384]{1,0:T(8,128)(2,1)S(1)} %copy-done.26, bf16[144,384]{1,0:T(8,128)(2,1)S(1)} %copy-done.24), kind=kOutput, calls=%fused_computation.1 | convolution fusion | flops 1815281664 | bytes 8306688 | tf_op jit(solution)/shard_map/dot_general | solution.py:14
  244.7 2.4 collective-permute-start.21
  247.1 19.5 %collective-permute-done.19 = bf16[72,4096]{1,0:T(8,128)(2,1)} collective-permute-done((bf16[72,4096]{1,0:T(8,128)(2,1)}, bf16[72,4096]{1,0:T(8,128)(2,1)}, u32[]{:S(2)}, u32[]{:S(2)}) %collective-permute-start.19) | collective-permute-done | bytes 589856 | tf_op jit(solution)/shard_map/ppermute | solution.py:19
  266.7 1.9 add_convert_fusion.4
  268.7 2.4 fusion.6
  271.1 2.4 collective-permute-start.23
  273.6 2.1 fusion.4
  280.1 27.6 %collective-permute-done.22 = bf16[72,4096]{1,0:T(8,128)(2,1)S(1)} collective-permute-done((bf16[72,4096]{1,0:T(8,128)(2,1)S(1)}, bf16[72,4096]{1,0:T(8,128)(2,1)S(1)}, u32[]{:S(2)}, u32[]{:S(2)}) %collective-permute-start.22) | collective-permute-done | bytes 589856 | tf_op jit(solution)/shard_map/ppermute | solution.py:30
  307.7 15.3 %collective-permute-done.23 = bf16[72,4096]{1,0:T(8,128)(2,1)S(1)} collective-permute-done((bf16[72,4096]{1,0:T(8,128)(2,1)S(1)}, bf16[72,4096]{1,0:T(8,128)(2,1)S(1)}, u32[]{:S(2)}, u32[]{:S(2)}) %collective-permute-start.23) | collective-permute-done | bytes 589856 | tf_op jit(solution)/shard_map/ppermute | solution.py:30
  327.0 2.3 collective-permute-done.27
  (152 shorter events, 39.7 us)
Async XLA Ops:
  0.6 43.3 %copy-start = (bf16[1,4096,384]{2,1,0:T(8,128)(2,1)S(1)}, bf16[1,4096,384]{2,1,0:T(8,128)(2,1)}, u32[]{:S(2)}) copy-start(bf16[1,4096,384]{2,1,0:T(8,128)(2,1)} %param.12) | copy-start | bytes 9437188
  0.7 7.9 %copy-start.11 = (bf16[128,4096]{1,0:T(8,128)(2,1)S(1)}, bf16[128,4096]{1,0:T(8,128)(2,1)}, u32[]{:S(2)}) copy-start(bf16[128,4096]{1,0:T(8,128)(2,1)} %param.8) | copy-start | bytes 3145732
  0.7 11.3 %copy-start.10 = (bf16[128,4096]{1,0:T(8,128)(2,1)S(1)}, bf16[128,4096]{1,0:T(8,128)(2,1)}, u32[]{:S(2)}) copy-start(bf16[128,4096]{1,0:T(8,128)(2,1)} %param.7) | copy-start | bytes 3145732
  2.5 11.2 %copy-start.30 = (bf16[128]{0:T(256)(128)(2,1)S(1)}, bf16[128]{0:T(256)(128)(2,1)}, u32[]{:S(2)}) copy-start(bf16[128]{0:T(256)(128)(2,1)} %param.9) | copy-start | bytes 772
  5.0 55.9 %collective-permute-start.10 = (bf16[72,4096]{1,0:T(8,128)(2,1)}, bf16[72,4096]{1,0:T(8,128)(2,1)}, u32[]{:S(2)}, u32[]{:S(2)}) collective-permute-start(bf16[72,4096]{1,0:T(8,128)(2,1)} %get-tuple-element.42), channel_id=1, source_target_pairs={{1,2},{2,1},{5,6},{6,5},{9,10},{10,9},{13,14},{14,13},{17,18},{18,... | collective-permute-start | bytes 1769480 | tf_op jit(solution)/shard_map/ppermute | solution.py:41
  8.5 48.1 %collective-permute-start.3 = (bf16[72,4096]{1,0:T(8,128)(2,1)}, bf16[72,4096]{1,0:T(8,128)(2,1)}, u32[]{:S(2)}, u32[]{:S(2)}) collective-permute-start(bf16[72,4096]{1,0:T(8,128)(2,1)} %get-tuple-element.42), channel_id=1, source_target_pairs={{0,1},{1,0},{2,3},{3,2},{4,5},{5,4},{6,7},{7,6},{8,9},{9,8},{10,11... | collective-permute-start | bytes 1769480 | tf_op jit(solution)/shard_map/ppermute | solution.py:19
  10.4 16.6 %collective-permute-start = (bf16[72,4096]{1,0:T(8,128)(2,1)}, bf16[72,4096]{1,0:T(8,128)(2,1)}, u32[]{:S(2)}, u32[]{:S(2)}) collective-permute-start(bf16[72,4096]{1,0:T(8,128)(2,1)} %convolution_convert_fusion.4), channel_id=1, source_target_pairs={{0,4},{4,0},{1,5},{5,1},{2,6},{6,2},{3,7},{7,3},{8,12},{12,8},{9,1... | collective-permute-start | bytes 1769480 | tf_op jit(solution)/shard_map/ppermute | solution.py:19
  13.1 25.0 %collective-permute-start.1 = (bf16[72,4096]{1,0:T(8,128)(2,1)}, bf16[72,4096]{1,0:T(8,128)(2,1)}, u32[]{:S(2)}, u32[]{:S(2)}) collective-permute-start(bf16[72,4096]{1,0:T(8,128)(2,1)} %convolution_convert_fusion.6), channel_id=1, source_target_pairs={{0,4},{4,0},{1,5},{5,1},{2,6},{6,2},{3,7},{7,3},{8,12},{12,8},{9,1... | collective-permute-start | bytes 1769480 | tf_op jit(solution)/shard_map/ppermute | solution.py:19
  13.7 28.2 %copy-start.1 = (bf16[1,4096,384]{2,1,0:T(8,128)(2,1)S(1)}, bf16[1,4096,384]{2,1,0:T(8,128)(2,1)}, u32[]{:S(2)}) copy-start(bf16[1,4096,384]{2,1,0:T(8,128)(2,1)} %param.11) | copy-start | bytes 9437188
  29.2 62.9 %collective-permute-start.2 = (bf16[144,4096]{1,0:T(8,128)(2,1)}, bf16[144,4096]{1,0:T(8,128)(2,1)}, u32[]{:S(2)}, u32[]{:S(2)}) collective-permute-start(bf16[144,4096]{1,0:T(8,128)(2,1)} %pad_maximum_fusion), channel_id=1, source_target_pairs={{0,1},{1,0},{2,3},{3,2},{4,5},{5,4},{6,7},{7,6},{8,9},{9,8},{10,11... | collective-permute-start | bytes 3538952 | tf_op jit(solution)/shard_map/ppermute | solution.py:19
  31.2 76.0 %collective-permute-start.7 = (bf16[144,4096]{1,0:T(8,128)(2,1)}, bf16[144,4096]{1,0:T(8,128)(2,1)}, u32[]{:S(2)}, u32[]{:S(2)}) collective-permute-start(bf16[144,4096]{1,0:T(8,128)(2,1)} %pad_maximum_fusion), channel_id=1, source_target_pairs={{1,2},{2,1},{5,6},{6,5},{9,10},{10,9},{13,14},{14,13},{17,18},{18,... | collective-permute-start | bytes 3538952 | tf_op jit(solution)/shard_map/ppermute | solution.py:41
  38.2 29.0 %collective-permute-start.4 = (bf16[72,4096]{1,0:T(8,128)(2,1)}, bf16[72,4096]{1,0:T(8,128)(2,1)}, u32[]{:S(2)}, u32[]{:S(2)}) collective-permute-start(bf16[72,4096]{1,0:T(8,128)(2,1)} %collective-permute-done.1), channel_id=1, source_target_pairs={{0,1},{1,0},{2,3},{3,2},{4,5},{5,4},{6,7},{7,6},{8,9},{9,8},{10,11... | collective-permute-start | bytes 1769480 | tf_op jit(solution)/shard_map/ppermute | solution.py:19
  44.0 4.2 %copy-start.4 = (bf16[1,384,4096]{2,1,0:T(8,128)(2,1)S(1)}, bf16[1,384,4096]{2,1,0:T(8,128)(2,1)}, u32[]{:S(2)}) copy-start(bf16[1,384,4096]{2,1,0:T(8,128)(2,1)} %param.13) | copy-start | bytes 9437188
  54.5 18.1 %copy-start.2 = (bf16[1,4096,384]{2,1,0:T(8,128)(2,1)S(1)}, bf16[1,4096,384]{2,1,0:T(8,128)(2,1)}, u32[]{:S(2)}) copy-start(bf16[1,4096,384]{2,1,0:T(8,128)(2,1)} %param.11) | copy-start | bytes 9437188
  56.6 18.5 %collective-permute-start.13 = (bf16[72,4096]{1,0:T(8,128)(2,1)}, bf16[72,4096]{1,0:T(8,128)(2,1)}, u32[]{:S(2)}, u32[]{:S(2)}) collective-permute-start(bf16[72,4096]{1,0:T(8,128)(2,1)} %collective-permute-done.1), channel_id=1, source_target_pairs={{1,2},{2,1},{5,6},{6,5},{9,10},{10,9},{13,14},{14,13},{17,18},{18,... | collective-permute-start | bytes 1769480 | tf_op jit(solution)/shard_map/ppermute | solution.py:41
  60.9 26.8 %collective-permute-start.9 = (bf16[72,4096]{1,0:T(8,128)(2,1)}, bf16[72,4096]{1,0:T(8,128)(2,1)}, u32[]{:S(2)}, u32[]{:S(2)}) collective-permute-start(bf16[72,4096]{1,0:T(8,128)(2,1)} %collective-permute-done.3), channel_id=1, source_target_pairs={{1,2},{2,1},{5,6},{6,5},{9,10},{10,9},{13,14},{14,13},{17,18},{18,... | collective-permute-start | bytes 1769480 | tf_op jit(solution)/shard_map/ppermute | solution.py:42
  67.2 12.5 %collective-permute-start.11 = (bf16[72,4096]{1,0:T(8,128)(2,1)}, bf16[72,4096]{1,0:T(8,128)(2,1)S(1)}, u32[]{:S(2)}, u32[]{:S(2)}) collective-permute-start(bf16[72,4096]{1,0:T(8,128)(2,1)} %collective-permute-done.10), channel_id=1, source_target_pairs={{1,0},{2,3},{5,4},{6,7},{9,8},{10,11},{13,12},{14,15},{17,16},{18,... | collective-permute-start | bytes 1769480 | tf_op jit(solution)/shard_map/ppermute | solution.py:43
  72.6 19.5 %copy-start.5 = (bf16[1,384,4096]{2,1,0:T(8,128)(2,1)S(1)}, bf16[1,384,4096]{2,1,0:T(8,128)(2,1)}, u32[]{:S(2)}) copy-start(bf16[1,384,4096]{2,1,0:T(8,128)(2,1)} %param.13) | copy-start | bytes 9437188
  75.1 29.0 %collective-permute-start.12 = (bf16[72,4096]{1,0:T(8,128)(2,1)}, bf16[72,4096]{1,0:T(8,128)(2,1)}, u32[]{:S(2)}, u32[]{:S(2)}) collective-permute-start(bf16[72,4096]{1,0:T(8,128)(2,1)} %collective-permute-done.4), channel_id=1, source_target_pairs={{1,2},{2,1},{5,6},{6,5},{9,10},{10,9},{13,14},{14,13},{17,18},{18,... | collective-permute-start | bytes 1769480 | tf_op jit(solution)/shard_map/ppermute | solution.py:42
  79.8 21.8 %collective-permute-start.14 = (bf16[72,4096]{1,0:T(8,128)(2,1)}, bf16[72,4096]{1,0:T(8,128)(2,1)}, u32[]{:S(2)}, u32[]{:S(2)}) collective-permute-start(bf16[72,4096]{1,0:T(8,128)(2,1)} %collective-permute-done.13), channel_id=1, source_target_pairs={{1,0},{2,3},{5,4},{6,7},{9,8},{10,11},{13,12},{14,15},{17,16},{18,... | collective-permute-start | bytes 1769480 | tf_op jit(solution)/shard_map/ppermute | solution.py:43
  87.7 23.9 %collective-permute-start.17 = (bf16[72,4096]{1,0:T(8,128)(2,1)}, bf16[72,4096]{1,0:T(8,128)(2,1)}, u32[]{:S(2)}, u32[]{:S(2)}) collective-permute-start(bf16[72,4096]{1,0:T(8,128)(2,1)} %collective-permute-done.9), channel_id=1, source_target_pairs={{1,0},{2,3},{5,4},{6,7},{9,8},{10,11},{13,12},{14,15},{17,16},{18,... | collective-permute-start | bytes 1769480 | tf_op jit(solution)/shard_map/ppermute | solution.py:44
  96.0 3.1 copy-start.25
  100.3 10.5 %copy-start.3 = (bf16[1,4096,384]{2,1,0:T(8,128)(2,1)S(1)}, bf16[1,4096,384]{2,1,0:T(8,128)(2,1)}, u32[]{:S(2)}) copy-start(bf16[1,4096,384]{2,1,0:T(8,128)(2,1)} %param.11) | copy-start | bytes 9437188
  100.4 10.5 %copy-start.15 = (bf16[72,4096]{1,0:T(8,128)(2,1)S(1)}, bf16[72,4096]{1,0:T(8,128)(2,1)}, u32[]{:S(2)}) copy-start(bf16[72,4096]{1,0:T(8,128)(2,1)} %get-tuple-element.12) | copy-start | bytes 1769476
  101.6 141.8 %collective-permute-start.5 = (bf16[72,4096]{1,0:T(8,128)(2,1)}, bf16[72,4096]{1,0:T(8,128)(2,1)}, u32[]{:S(2)}, u32[]{:S(2)}) collective-permute-start(bf16[72,4096]{1,0:T(8,128)(2,1)} %get-tuple-element.15), channel_id=1, source_target_pairs={{0,1},{1,0},{2,3},{3,2},{4,5},{5,4},{6,7},{7,6},{8,9},{9,8},{10,11... | collective-permute-start | bytes 1769480 | tf_op jit(solution)/shard_map/ppermute | solution.py:19
  101.6 38.1 %collective-permute-start.6 = (bf16[144,4096]{1,0:T(8,128)(2,1)}, bf16[144,4096]{1,0:T(8,128)(2,1)}, u32[]{:S(2)}, u32[]{:S(2)}) collective-permute-start(bf16[144,4096]{1,0:T(8,128)(2,1)} %collective-permute-done.2), channel_id=1, source_target_pairs={{1,2},{2,1},{5,6},{6,5},{9,10},{10,9},{13,14},{14,13},{17,18},{18,... | collective-permute-start | bytes 3538952 | tf_op jit(solution)/shard_map/ppermute | solution.py:42
  104.0 32.0 %collective-permute-start.18 = (bf16[72,4096]{1,0:T(8,128)(2,1)}, bf16[72,4096]{1,0:T(8,128)(2,1)S(1)}, u32[]{:S(2)}, u32[]{:S(2)}) collective-permute-start(bf16[72,4096]{1,0:T(8,128)(2,1)} %collective-permute-done.12), channel_id=1, source_target_pairs={{1,0},{2,3},{5,4},{6,7},{9,8},{10,11},{13,12},{14,15},{17,16},{18,... | collective-permute-start | bytes 1769480 | tf_op jit(solution)/shard_map/ppermute | solution.py:44
  107.2 47.9 %collective-permute-start.8 = (bf16[144,4096]{1,0:T(8,128)(2,1)}, bf16[144,4096]{1,0:T(8,128)(2,1)S(1)}, u32[]{:S(2)}, u32[]{:S(2)}) collective-permute-start(bf16[144,4096]{1,0:T(8,128)(2,1)} %collective-permute-done.7), channel_id=1, source_target_pairs={{1,0},{2,3},{5,4},{6,7},{9,8},{10,11},{13,12},{14,15},{17,16},{18,... | collective-permute-start | bytes 3538952 | tf_op jit(solution)/shard_map/ppermute | solution.py:43
  113.7 24.4 %copy-start.16 = (bf16[72,4096]{1,0:T(8,128)(2,1)}, bf16[72,4096]{1,0:T(8,128)(2,1)S(1)}, u32[]{:S(2)}) copy-start(bf16[72,4096]{1,0:T(8,128)(2,1)S(1)} %get-tuple-element.8) | copy-start | bytes 1769476
  138.1 17.0 %copy-start.6 = (bf16[1,384,4096]{2,1,0:T(8,128)(2,1)S(1)}, bf16[1,384,4096]{2,1,0:T(8,128)(2,1)}, u32[]{:S(2)}) copy-start(bf16[1,384,4096]{2,1,0:T(8,128)(2,1)} %param.13) | copy-start | bytes 9437188
  155.1 2.8 copy-start.9
  161.9 34.8 %collective-permute-start.16 = (bf16[144,4096]{1,0:T(8,128)(2,1)}, bf16[144,4096]{1,0:T(8,128)(2,1)}, u32[]{:S(2)}, u32[]{:S(2)}) collective-permute-start(bf16[144,4096]{1,0:T(8,128)(2,1)} %collective-permute-done.6), channel_id=1, source_target_pairs={{1,0},{2,3},{5,4},{6,7},{9,8},{10,11},{13,12},{14,15},{17,16},{18,... | collective-permute-start | bytes 3538952 | tf_op jit(solution)/shard_map/ppermute | solution.py:44
  166.7 30.0 %copy-start.7 = (bf16[1,384,4096]{2,1,0:T(8,128)(2,1)S(1)}, bf16[1,384,4096]{2,1,0:T(8,128)(2,1)}, u32[]{:S(2)}) copy-start(bf16[1,384,4096]{2,1,0:T(8,128)(2,1)} %param.13) | copy-start | bytes 9437188
  166.7 78.0 %collective-permute-start.15 = (bf16[72,4096]{1,0:T(8,128)(2,1)}, bf16[72,4096]{1,0:T(8,128)(2,1)}, u32[]{:S(2)}, u32[]{:S(2)}) collective-permute-start(bf16[72,4096]{1,0:T(8,128)(2,1)} %get-tuple-element.17), channel_id=1, source_target_pairs={{0,2},{1,3},{2,0},{3,1},{4,6},{5,7},{6,4},{7,5},{8,10},{9,11},{10,... | collective-permute-start | bytes 1769480 | tf_op jit(solution)/shard_map/ppermute | solution.py:19
  169.5 29.7 %copy-start.17 = (bf16[72,4096]{1,0:T(8,128)(2,1)S(1)}, bf16[72,4096]{1,0:T(8,128)(2,1)}, u32[]{:S(2)}) copy-start(bf16[72,4096]{1,0:T(8,128)(2,1)} %copy-done.16) | copy-start | bytes 1769476
  169.5 29.7 %copy-start.19 = (bf16[72,4096]{1,0:T(8,128)(2,1)S(1)}, bf16[72,4096]{1,0:T(8,128)(2,1)}, u32[]{:S(2)}) copy-start(bf16[72,4096]{1,0:T(8,128)(2,1)} %copy-done.18) | copy-start | bytes 1769476
  169.5 29.7 %copy-start.31 = (f32[144,384]{1,0:T(8,128)S(1)}, f32[144,384]{1,0:T(8,128)}, u32[]{:S(2)}) copy-start(f32[144,384]{1,0:T(8,128)} %fusion.9) | copy-start | bytes 663556
  200.8 2.7 copy-start.32
  200.8 2.7 copy-start.33
  200.8 2.7 copy-start.34
  200.9 2.7 copy-start.35
  214.6 27.8 %all-to-all-start = ((bf16[8,1,72]{2,1,0:T(2,128)(2,1)}), bf16[8,1,72]{2,1,0:T(2,128)(2,1)S(1)}, u32[]{:S(2)}, u32[]{:S(2)}) async-start(bf16[8,1,72]{2,1,0:T(2,128)(2,1)} %copy.38), calls=%async_computation | async-start | bytes 8192 | tf_op jit(solution)/shard_map/all_to_all | solution.py:149
  223.2 48.0 %collective-permute-start.28 = (bf16[2,1024,384]{1,2,0:T(8,128)(2,1)}, bf16[2,1024,384]{1,2,0:T(8,128)(2,1)}, u32[]{:S(2)}, u32[]{:S(2)}) collective-permute-start(bf16[2,1024,384]{1,2,0:T(8,128)(2,1)} %bitcast.115), channel_id=1, source_target_pairs={{0,8},{8,0},{16,24},{24,16},{1,9},{9,1},{17,25},{25,17},{2,10},{10... | collective-permute-start | bytes 4718600 | tf_op jit(solution)/shard_map/ppermute | solution.py:19
  223.2 3.2 copy-start.22
  223.2 9.0 %slice-start = ((s8[4718592]{0:T(1024)(128)(4,1)}), s8[4194304]{0:T(1024)(128)(4,1)S(1)}, s32[]{:S(2)}) async-start(s8[4718592]{0:T(1024)(128)(4,1)} %bitcast.116), calls=%async_computation.1 | async-start | bytes 8388608
  226.4 5.7 %copy-start.24 = (bf16[144,384]{1,0:T(8,128)(2,1)S(1)}, bf16[144,384]{1,0:T(8,128)(2,1)}, u32[]{:S(2)}) copy-start(bf16[144,384]{1,0:T(8,128)(2,1)} %copy-done.23) | copy-start | bytes 331780
  226.4 5.7 %copy-start.26 = (bf16[144,384]{1,0:T(8,128)(2,1)S(1)}, bf16[144,384]{1,0:T(8,128)(2,1)}, u32[]{:S(2)}) copy-start(bf16[144,384]{1,0:T(8,128)(2,1)} %copy-done.25) | copy-start | bytes 331780
  226.4 5.7 %copy-start.28 = (bf16[144,384]{1,0:T(8,128)(2,1)S(1)}, bf16[144,384]{1,0:T(8,128)(2,1)}, u32[]{:S(2)}) copy-start(bf16[144,384]{1,0:T(8,128)(2,1)} %copy-done.27) | copy-start | bytes 331780
  226.4 5.7 %copy-start.29 = (bf16[144,384]{1,0:T(8,128)(2,1)S(1)}, bf16[144,384]{1,0:T(8,128)(2,1)}, u32[]{:S(2)}) copy-start(bf16[144,384]{1,0:T(8,128)(2,1)} %get-tuple-element.40) | copy-start | bytes 331780
  226.4 5.7 %slice-start.1 = ((s8[4718592]{0:T(1024)(128)(4,1)}), s8[524288]{0:T(1024)(128)(4,1)S(1)}, s32[]{:S(2)}) async-start(s8[4718592]{0:T(1024)(128)(4,1)} %bitcast.116), calls=%async_computation.2 | async-start | bytes 1048576
  232.1 7.4 %copy-start.14 = (bf16[4096,384]{1,0:T(8,128)(2,1)}, bf16[4096,384]{1,0:T(8,128)(2,1)S(1)}, u32[]{:S(2)}) copy-start(bf16[4096,384]{1,0:T(8,128)(2,1)S(1)} %convolution_convert_fusion.2) | copy-start | bytes 9437188
  235.7 5.4 %copy-start.12 = (bf16[4096,384]{1,0:T(8,128)(2,1)}, bf16[4096,384]{1,0:T(8,128)(2,1)S(1)}, u32[]{:S(2)}) copy-start(bf16[4096,384]{1,0:T(8,128)(2,1)S(1)} %convolution_convert_fusion.1) | copy-start | bytes 9437188
  238.0 28.7 %collective-permute-start.19 = (bf16[72,4096]{1,0:T(8,128)(2,1)}, bf16[72,4096]{1,0:T(8,128)(2,1)}, u32[]{:S(2)}, u32[]{:S(2)}) collective-permute-start(bf16[72,4096]{1,0:T(8,128)(2,1)} %get-tuple-element.19), channel_id=1, source_target_pairs={{0,3},{1,2},{2,1},{3,0},{4,7},{5,6},{6,5},{7,4},{8,11},{9,10},{10,... | collective-permute-start | bytes 1769480 | tf_op jit(solution)/shard_map/ppermute | solution.py:19
  240.8 27.8 %collective-permute-start.24 = (bf16[2,1024,384]{2,1,0:T(8,128)(2,1)}, bf16[2,1024,384]{2,1,0:T(8,128)(2,1)}, u32[]{:S(2)}, u32[]{:S(2)}) collective-permute-start(bf16[2,1024,384]{2,1,0:T(8,128)(2,1)} %dynamic-slice_bitcast_fusion.1), channel_id=1, source_target_pairs={{0,8},{8,0},{16,24},{24,16},{1,9},{9,1},{17,25},{25,17},{2,10},{10... | collective-permute-start | bytes 4718600 | tf_op jit(solution)/shard_map/ppermute | solution.py:19
  242.7 25.9 %copy-start.20 = (bf16[72,4096]{1,0:T(8,128)(2,1)S(1)}, bf16[72,4096]{1,0:T(8,128)(2,1)}, u32[]{:S(2)}) copy-start(bf16[72,4096]{1,0:T(8,128)(2,1)} %get-tuple-element.18) | copy-start | bytes 1769476
  243.3 34.7 %collective-permute-start.20 = (bf16[72,4096]{1,0:T(8,128)(2,1)}, bf16[72,4096]{1,0:T(8,128)(2,1)S(1)}, u32[]{:S(2)}, u32[]{:S(2)}) collective-permute-start(bf16[72,4096]{1,0:T(8,128)(2,1)} %slice.36), channel_id=1, source_target_pairs={{0,4},{4,0},{1,5},{5,1},{2,6},{6,2},{3,7},{7,3},{8,12},{12,8},{9,1... | collective-permute-start | bytes 1769480 | tf_op jit(solution)/shard_map/ppermute | solution.py:19
  244.7 34.8 %collective-permute-start.21 = (bf16[72,4096]{1,0:T(8,128)(2,1)}, bf16[72,4096]{1,0:T(8,128)(2,1)S(1)}, u32[]{:S(2)}, u32[]{:S(2)}) collective-permute-start(bf16[72,4096]{1,0:T(8,128)(2,1)} %get-tuple-element.16), channel_id=1, source_target_pairs={{0,5},{1,4},{2,7},{3,6},{4,1},{5,0},{6,3},{7,2},{8,13},{9,12},{10,... | collective-permute-start | bytes 1769480 | tf_op jit(solution)/shard_map/ppermute | solution.py:30
  266.7 9.2 %collective-permute-start.26 = (bf16[2,1024,384]{2,1,0:T(8,128)(2,1)}, bf16[2,1024,384]{2,1,0:T(8,128)(2,1)S(1)}, u32[]{:S(2)}, u32[]{:S(2)}) collective-permute-start(bf16[2,1024,384]{2,1,0:T(8,128)(2,1)} %dynamic-slice_bitcast_fusion), channel_id=1, source_target_pairs={{0,8},{8,0},{16,24},{24,16},{1,9},{9,1},{17,25},{25,17},{2,10},{10... | collective-permute-start | bytes 4718600 | tf_op jit(solution)/shard_map/ppermute | solution.py:19
  268.6 4.9 %copy-start.8 = (bf16[2,1,1024,384]{2,3,0,1:T(8,128)(2,1)S(1)}, bf16[2,1,1024,384]{2,3,0,1:T(8,128)(2,1)}, u32[]{:S(2)}) copy-start(bf16[2,1,1024,384]{2,3,0,1:T(8,128)(2,1)} %copy.46) | copy-start | bytes 4718596
  268.6 39.1 %collective-permute-start.22 = (bf16[72,4096]{1,0:T(8,128)(2,1)S(1)}, bf16[72,4096]{1,0:T(8,128)(2,1)S(1)}, u32[]{:S(2)}, u32[]{:S(2)}) collective-permute-start(bf16[72,4096]{1,0:T(8,128)(2,1)S(1)} %copy-done.20), channel_id=1, source_target_pairs={{0,6},{1,7},{2,4},{3,5},{4,2},{5,3},{6,0},{7,1},{8,14},{9,15},{10,... | collective-permute-start | bytes 1769480 | tf_op jit(solution)/shard_map/ppermute | solution.py:30
  271.1 51.8 %collective-permute-start.23 = (bf16[72,4096]{1,0:T(8,128)(2,1)S(1)}, bf16[72,4096]{1,0:T(8,128)(2,1)S(1)}, u32[]{:S(2)}, u32[]{:S(2)}) collective-permute-start(bf16[72,4096]{1,0:T(8,128)(2,1)S(1)} %copy-done.21), channel_id=1, source_target_pairs={{0,7},{1,6},{2,5},{3,4},{4,3},{5,2},{6,1},{7,0},{8,15},{9,14},{10,... | collective-permute-start | bytes 1769480 | tf_op jit(solution)/shard_map/ppermute | solution.py:30
  275.8 48.9 %collective-permute-start.29 = (bf16[1,1024,384]{1,2,0:T(8,128)(2,1)S(1)}, bf16[1,1024,384]{1,2,0:T(8,128)(2,1)S(1)}, u32[]{:S(2)}, u32[]{:S(2)}) collective-permute-start(bf16[1,1024,384]{1,2,0:T(8,128)(2,1)S(1)} %constant_dynamic-slice_fusion), channel_id=1, source_target_pairs={{0,16},{8,24},{16,0},{24,8},{1,17},{9,25},{17,1},{25,9},{2,18},{10... | collective-permute-start | bytes 2359304 | tf_op jit(solution)/shard_map/ppermute | solution.py:19
  278.0 47.9 %collective-permute-start.25 = (bf16[1,1024,384]{2,1,0:T(8,128)(2,1)S(1)}, bf16[1,1024,384]{2,1,0:T(8,128)(2,1)S(1)}, u32[]{:S(2)}, u32[]{:S(2)}) collective-permute-start(bf16[1,1024,384]{2,1,0:T(8,128)(2,1)S(1)} %constant_dynamic-slice_fusion.4), channel_id=1, source_target_pairs={{0,16},{8,24},{16,0},{24,8},{1,17},{9,25},{17,1},{25,9},{2,18},{10... | collective-permute-start | bytes 2359304 | tf_op jit(solution)/shard_map/ppermute | solution.py:19
  279.6 49.7 %collective-permute-start.27 = (bf16[1,1024,384]{2,1,0:T(8,128)(2,1)S(1)}, bf16[1,1024,384]{2,1,0:T(8,128)(2,1)S(1)}, u32[]{:S(2)}, u32[]{:S(2)}) collective-permute-start(bf16[1,1024,384]{2,1,0:T(8,128)(2,1)S(1)} %constant_dynamic-slice_fusion.3), channel_id=1, source_target_pairs={{0,16},{8,24},{16,0},{24,8},{1,17},{9,25},{17,1},{25,9},{2,18},{10... | collective-permute-start | bytes 2359304 | tf_op jit(solution)/shard_map/ppermute | solution.py:19
  (5 other events, 8.2 us)

commit v2 on v1

v2 whole, which is shorter than its diff:
```python
import functools

import jax
import jax.numpy as jnp
from jax import lax
from jax.experimental import pallas as pl
from jax.experimental.pallas import tpu as pltpu
from jax.sharding import PartitionSpec as P

TOP = 1
BF = jnp.bfloat16
F32 = jnp.float32
PLAIN = (((1,), (0,)), ((), ()))
CONTRACT_LAST = (((1,), (1,)), ((), ()))
CONTRACT_FIRST = (((0,), (0,)), ((), ()))
MIDDLE = [(1, 2), (2, 1)]
OUTWARD = [(1, 0), (2, 3)]
INWARD_TWO = [(0, 2), (3, 1)]


def dot(left, right, dims=PLAIN):
    return lax.dot_general(left, right, dims, preferred_element_type=F32)


def after(value, *others):
    return lax.optimization_barrier((value,) + others)[0]


def send_xor(value, axis, mask):
    size = lax.axis_size(axis)
    return lax.ppermute(value, axis, [(i, i ^ mask) for i in range(size)])


def send_home(value, expert_mask, seq_mask):
    if not expert_mask:
        return send_xor(value, "seq", seq_mask) if seq_mask else value
    if not seq_mask:
        return send_xor(value, "expert", expert_mask)
    seq_count = lax.axis_size("seq")
    total = lax.axis_size("expert") * seq_count
    mask = expert_mask * seq_count + seq_mask
    return lax.ppermute(value, ("expert", "seq"), [(i, i ^ mask) for i in range(total)])


def slot_kernel(
    blocks,
    place,
    x,
    dy,
    wg,
    wu,
    wd,
    part,
    far_share,
    near_share,
    own_share,
    kx,
    ky,
    kg,
    ku,
    kd,
    kp,
    kfar,
    knear,
    kown,
    sems,
    out_sems,
):
    feat, width = kg.shape
    rows = kx.shape[0]
    step = feat // blocks
    half, quarter = feat // 2, feat // 4

    def fetch(i):
        cols = pl.ds(i * step, step)
        pairs = [(x, kx, True), (wg, kg, False), (dy, ky, True), (wu, ku, False), (wd, kd, True)]
        return [
            pltpu.make_async_copy(
                source.at[:, cols] if last else source.at[cols],
                target.at[:, cols] if last else target.at[cols],
                sems.at[k, i],
            )
            for k, (source, target, last) in enumerate(pairs)
        ]

    copies = [fetch(i) for i in range(blocks)]
    for group in copies:
        for copy in group:
            copy.start()
    gate_pre = up_pre = scaled_grad = None
    for i in range(blocks):
        for copy in copies[i]:
            copy.wait()
        cols = pl.ds(i * step, step)
        terms = (
            dot(kx[:, cols], kg[cols]),
            dot(kx[:, cols], ku[cols]),
            dot(ky[:, cols], kd[:, cols], CONTRACT_LAST),
        )
        if i == 0:
            gate_pre, up_pre, scaled_grad = terms
        else:
            gate_pre, up_pre, scaled_grad = (
                gate_pre + terms[0],
                up_pre + terms[1],
                scaled_grad + terms[2],
            )
    sigmoid_gate = jax.nn.sigmoid(gate_pre)
    activated = gate_pre * sigmoid_gate
    hidden = activated * up_pre
    gate_part = jnp.sum(hidden * scaled_grad, axis=1, keepdims=True).astype(BF)
    kp[:, feat:] = jnp.broadcast_to(gate_part, (rows, kp.shape[1] - feat))
    gate_delta = (
        scaled_grad * up_pre * sigmoid_gate * (1.0 + gate_pre * (1.0 - sigmoid_gate))
    ).astype(BF)
    up_delta = (scaled_grad * activated).astype(BF)
    hidden = hidden.astype(BF)
    hi, lo = place[0], place[1]
    shares = [
        (kfar, far_share, half, (1 - hi) * half),
        (knear, near_share, quarter, hi * half + (1 - lo) * quarter),
        (kown, own_share, quarter, hi * half + lo * quarter),
    ]
    outs = []
    for keep, share, count, start in shares:
        cols = pl.ds(pl.multiple_of(start, quarter), count)
        keep[:rows, :count] = kx[:, cols]
        keep[:rows, count : 2 * count] = ky[:, cols]
        low = 2 * count
        keep[:rows, low : low + width] = gate_delta
        keep[:rows, low + width : low + 2 * width] = up_delta
        keep[:rows, low + 2 * width : low + 3 * width] = hidden
        if keep.shape[0] > rows:
            keep[rows:] = jnp.zeros((keep.shape[0] - rows, keep.shape[1]), BF)
        copy = pltpu.make_async_copy(keep, share, out_sems.at[len(outs)])
        copy.start()
        outs.append(copy)
    for i in range(blocks):
        cols = pl.ds(i * step, step)
        kp[:, cols] = (
            dot(gate_delta, kg[cols], CONTRACT_LAST) + dot(up_delta, ku[cols], CONTRACT_LAST)
        ).astype(BF)
        if i == blocks - 1:
            cols = pl.ds(i * step, kp.shape[1] - i * step)
        copy = pltpu.make_async_copy(kp.at[:, cols], part.at[:, cols], out_sems.at[len(outs)])
        copy.start()
        outs.append(copy)
    for copy in outs:
        copy.wait()


def slot_work(place, x_rows, dy_rows, gate_local, up_local, down_local):
    rows, feat = x_rows.shape
    width = gate_local.shape[1]
    tall = -(-rows // 16) * 16
    wide = -(-3 * width // 128) * 128
    blocks = 4
    away = pl.BlockSpec(memory_space=pltpu.HBM)
    shares = [(tall, feat + wide), (tall, feat // 2 + wide), (tall, feat // 2 + wide)]
    return pl.pallas_call(
        functools.partial(slot_kernel, blocks),
        out_shape=[jax.ShapeDtypeStruct((rows, feat + 128), BF)]
        + [jax.ShapeDtypeStruct(shape, BF) for shape in shares],
        in_specs=[pl.BlockSpec(memory_space=pltpu.SMEM)] + [away] * 5,
        out_specs=[away] * 4,
        scratch_shapes=[
            pltpu.VMEM((rows, feat), BF),
            pltpu.VMEM((rows, feat), BF),
            pltpu.VMEM((feat, width), BF),
            pltpu.VMEM((feat, width), BF),
            pltpu.VMEM((width, feat), BF),
            pltpu.VMEM((rows, feat + 128), BF),
        ]
        + [pltpu.VMEM(shape, BF) for shape in shares]
        + [
            pltpu.SemaphoreType.DMA((5, blocks)),
            pltpu.SemaphoreType.DMA((3 + blocks,)),
        ],
        compiler_params=pltpu.CompilerParams(vmem_limit_bytes=56 * 1024 * 1024),
        name="slot_work",
    )(place, x_rows, dy_rows, gate_local, up_local, down_local)


def weight_kernel(slots, started, width, *refs):
    place, refs = refs[0], refs[1:]
    sources = [refs[4 * s : 4 * s + 4] for s in range(slots)]
    refs = refs[4 * slots :]
    before, refs = (refs[:3], refs[3:]) if started else (None, refs)
    outs, refs = refs[:3], refs[3:]
    keep_x, keep_dy, keep_d, sums_gu, sums_d, sems = refs
    quarter, wide = keep_x.shape[2], keep_d.shape[2]
    tall = keep_x.shape[1] // 4
    half = 2 * quarter
    low = pl.multiple_of(place[1] * quarter, quarter)
    shifted = pl.multiple_of(half + place[1] * quarter, quarter)
    copies = []
    for s in range(slots):
        own, near, far, cross = sources[s]
        cuts = [
            (own, 0, quarter, half),
            (near, 0, quarter, half),
            (far, low, shifted, 2 * half),
            (cross, low, shifted, 2 * half),
        ]
        for g, (ref, *starts) in enumerate(cuts):
            rows = pl.ds(g * tall, tall)
            for k, (keep, start) in enumerate(zip((keep_x, keep_dy, keep_d), starts)):
                copy = pltpu.make_async_copy(
                    ref.at[:, pl.ds(start, keep.shape[2])],
                    keep.at[s, rows],
                    sems.at[s, 3 * g + k],
                )
                copy.start()
                copies.append((s, copy))
    for s in range(slots):
        for n, copy in copies:
            if n == s:
                copy.wait()
        gate_up = dot(keep_x[s], keep_d[s, :, : 2 * width], CONTRACT_FIRST)
        down = dot(keep_d[s, :, 2 * width : 3 * width], keep_dy[s], CONTRACT_FIRST)
        if s == 0 and started:
            sums_gu[:, :width] = before[0][...] + gate_up[:, :width]
            sums_gu[:, width:] = before[1][...] + gate_up[:, width:]
            sums_d[...] = before[2][...] + down
        elif s == 0:
            sums_gu[...] = gate_up
            sums_d[...] = down
        else:
            sums_gu[...] += gate_up
            sums_d[...] += down
    outs[0][...] = sums_gu[:, :width].astype(outs[0].dtype)
    outs[1][...] = sums_gu[:, width:].astype(outs[1].dtype)
    outs[2][...] = sums_d[...].astype(outs[2].dtype)


def weight_work(place, width, slots, before, dtype):
    tall, both = slots[0][0].shape
    wide = -(-3 * width // 128) * 128
    quarter = (both - wide) // 2
    whole = pl.BlockSpec(memory_space=pltpu.VMEM)
    away = pl.BlockSpec(memory_space=pltpu.HBM)
    shapes = [(quarter, width), (quarter, width), (width, quarter)]
    return pl.pallas_call(
        functools.partial(weight_kernel, len(slots), bool(before), width),
        out_shape=[jax.ShapeDtypeStruct(shape, dtype) for shape in shapes],
        in_specs=[pl.BlockSpec(memory_space=pltpu.SMEM)]
        + [away] * (4 * len(slots))
        + [whole] * len(before),
        out_specs=[whole] * 3,
        scratch_shapes=[
            pltpu.VMEM((len(slots), 4 * tall, quarter), BF),
            pltpu.VMEM((len(slots), 4 * tall, quarter), BF),
            pltpu.VMEM((len(slots), 4 * tall, wide), BF),
            pltpu.VMEM((quarter, 2 * width), F32),
            pltpu.VMEM((width, quarter), F32),
            pltpu.SemaphoreType.DMA((len(slots), 12)),
        ],
        compiler_params=pltpu.CompilerParams(vmem_limit_bytes=56 * 1024 * 1024),
        name="weight_work",
    )(place, *[array for slot in slots for array in slot], *before)


def body(tokens, out_grad, gate_prob, expert_ids, w_gate, w_up, w_down):
    expert_count = lax.axis_size("expert")
    seq_count = lax.axis_size("seq")
    tok_rows, feat_width = tokens.shape
    capacity = tok_rows * TOP * 17 // (16 * expert_count)
    my_expert = lax.axis_index("expert")
    my_seq = lax.axis_index("seq")
    route = expert_ids[:, 0]
    onehot = (route[:, None] == jnp.arange(expert_count)[None, :]).astype(F32)
    earlier = (jnp.arange(tok_rows)[:, None] > jnp.arange(tok_rows)[None, :]).astype(F32)
    before = dot(earlier, onehot)
    slot_index = jnp.sum(before * onehot, axis=1).astype(jnp.int32)
    block = jnp.bitwise_xor(route, my_expert)
    target = block * capacity + slot_index
    prob = gate_prob.astype(F32)

    def placer_of(first, last):
        rows = first * capacity + jnp.arange((last - first) * capacity)
        return rows[:, None] == target[None, :]

    def pack_x(first, last):
        return dot(placer_of(first, last).astype(BF), tokens).astype(BF)

    def pack_dy(first, last):
        scaler = jnp.where(placer_of(first, last), prob[None, :], 0.0).astype(BF)
        return dot(scaler, out_grad).astype(BF)

    def joined(first, rest):
        return jnp.concatenate([first] + list(rest), axis=0)

    gate_local, up_local, down_local = w_gate[0], w_up[0], w_down[0]
    others = range(1, expert_count)
    far_x = [send_xor(pack_x(j, j + 1), "expert", j) for j in others]
    near_x = pack_x(0, 1)
    far_dy = [send_xor(pack_dy(j, j + 1), "expert", j) for j in others]
    near_dy = pack_dy(0, 1)
    far_x = far_x[0] if len(far_x) == 1 else jnp.concatenate(far_x, axis=0)
    slot_x = [joined(near_x, [far_x])]
    slot_dy = [joined(near_dy, far_dy)]

    dp_index = lax.axis_index("dp")
    place = jnp.stack([dp_index // 2, dp_index % 2]).astype(jnp.int32)
    width = gate_local.shape[1]
    token_parts, shares = [], []

    def work(x_rows, dy_rows):
        part, far_share, near_share, own_share = slot_work(
            place, x_rows, dy_rows, gate_local, up_local, down_local
        )
        token_parts.append(part)
        near = send_xor(near_share, "dp", 1)
        far = send_xor(far_share, "dp", 2)
        shares.append([own_share, near, far, send_xor(far, "dp", 1)])
        return part

    if seq_count == 4:
        inner = (my_seq == 1) | (my_seq == 2)
        first_near = send_xor(near_x, "seq", 1)
        across_near = lax.ppermute(near_x, "seq", MIDDLE)
        first_far = send_xor(far_x, "seq", 1)
        across_far = lax.ppermute(far_x, "seq", MIDDLE)
        dy_first = send_xor(slot_dy[0], "seq", 1)
        dy_across = lax.ppermute(slot_dy[0], "seq", MIDDLE)
        x_first = joined(first_near, [first_far])
        x_across = joined(across_near, [across_far])
        done = work(after(slot_x[0], x_first), slot_dy[0])
        x_relayed = lax.ppermute(after(x_first, x_across), "seq", MIDDLE)
        x_near = lax.ppermute(after(x_across, x_first), "seq", OUTWARD)
        dy_relayed = lax.ppermute(after(dy_first, dy_across, done), "seq", MIDDLE)
        dy_near = lax.ppermute(after(dy_across, dy_first, done), "seq", OUTWARD)
        done = work(after(x_first, x_relayed, shares[0][2]), dy_first)
        x_far = lax.ppermute(after(x_relayed, x_near), "seq", OUTWARD)
        work(
            jnp.where(inner, x_relayed, x_near),
            jnp.where(inner, dy_relayed, dy_near),
        )
        dy_far = lax.ppermute(after(dy_relayed, dy_near, done), "seq", OUTWARD)
        over = lax.ppermute(token_parts[2], "seq", MIDDLE)
        two_away = lax.ppermute(token_parts[2], "seq", INWARD_TWO)
        onward = (token_parts[1].astype(F32) + over.astype(F32)).astype(BF)
        one_away = send_xor(onward, "seq", 1)
        work(
            jnp.where(inner, x_across, after(x_far, onward, shares[1][2])),
            jnp.where(inner, dy_across, dy_far),
        )
        so_far = weight_work(place, width, shares[:2], [], F32)
        early = [token_parts[0], two_away, after(one_away, so_far[0])]
    else:
        work(slot_x[0], slot_dy[0])
        for j in range(1, seq_count):
            work(send_xor(slot_x[0], "seq", j), send_xor(slot_dy[0], "seq", j))
        so_far = weight_work(place, width, shares[:2], [], F32)
        early = [token_parts[0]]
        early += [send_xor(token_parts[j], "seq", j) for j in range(1, seq_count - 1)]
    for j in range(2, seq_count - 2, 2):
        so_far = weight_work(place, width, shares[j : j + 2], so_far, F32)
    gate_w_grad, up_w_grad, down_w_grad = weight_work(place, width, shares[-2:], so_far, BF)
    last = seq_count - 1
    early = sum(part.astype(F32) for part in early)

    def rows_of(array, k):
        return array[k * capacity : (k + 1) * capacity]

    homes = []
    for k in range(expert_count):
        direct = send_home(rows_of(token_parts[last], k), k, last)
        first = rows_of(early, k)
        if k:
            first = send_xor(first.astype(BF), "expert", k).astype(F32)
        homes.append((first + direct.astype(F32)).astype(BF))
    home_x = jnp.concatenate(homes, axis=0)

    placer = placer_of(0, expert_count)
    placer = placer.astype(BF)
    token_grad = dot(placer, home_x[:, :feat_width], CONTRACT_FIRST).astype(BF)
    home_g = dot(placer, home_x[:, feat_width:], CONTRACT_FIRST)[:, 0]
    gate_grad = (home_g / prob).astype(BF)
    return (token_grad, gate_grad, gate_w_grad[None], up_w_grad[None], down_w_grad[None])


def solution(mesh):
    placed = (
        P(("dp", "expert", "seq"), None),
        P(("dp", "expert", "seq"), None),
        P(("dp", "expert", "seq")),
        P(("dp", "expert", "seq"), None),
        P("expert", None, "seq"),
        P("expert", None, "seq"),
        P("expert", "seq", None),
    )
    return jax.shard_map(
        body,
        mesh=mesh,
        in_specs=placed,
        out_specs=(
            P(("dp", "expert", "seq"), None),
            P(("dp", "expert", "seq")),
            P("expert", "dp", "seq"),
            P("expert", "dp", "seq"),
            P("expert", "seq", "dp"),
        ),
        check_vma=False,
    )
```

time: 335 us -> 275 us (0.82); the launches traced: 330 us -> 274 us
  matrix products: 62.5 us -> 5.32 us
  Pallas kernels: 0 us -> 54.8 us
  local copies, waits for them, and re-layouts: 27.4 us -> 4.53 us
  waiting for transfers between devices: 152 us -> 140 us
  starting transfers between devices: 58.9 us -> 49.1 us
  other arithmetic: 27.9 us -> 19.4 us
    dot_general x31 -> x7, matrix products: 62.5 us -> 5.32 us  [dot(): return lax.dot_general(left, right, dims, preferred_element_type=F32)]
    pallas_call x0 -> x6, Pallas kernels: none -> 54.8 us  [the longest x4 36 us: slot_work(): pl.pallas_call(functools.partial(slot_kernel, blocks), out_shape=[jax.Sha...]
    ppermute x15 -> x20, waiting for transfers between devices: 40.1 us -> 85.3 us  [send_xor(): return lax.ppermute(value, axis, [(i, i ^ mask) for i in range(size)])]
    ppermute x3 -> x1, waiting for transfers between devices: 42.8 us -> 0.01 us  [send_home(): lax.ppermute(value, ('expert', 'seq'), [(i, i ^ mask) for i in range(tota...]
    ppermute x12 -> x11, waiting for transfers between devices: 69.5 us -> 54.3 us  [the longest x1 17.6 us: body(): x_relayed = lax.ppermute(after(x_first, x_across), 'seq', MIDDLE)]
    unnamed x81 -> x34, local copies, waits for them, and re-layouts: 11.5 us -> 2.04 us
    unnamed x5 -> x0, other arithmetic: 9.08 us -> none
    select_n x0 -> x4, other arithmetic: none -> 8.64 us  [the longest x1 2.4 us: body(): jnp.where(inner, x_relayed, x_near)]
  transfers between devices with their start and end apart: 31 -> 32, of which waited for: 13 -> 15; matrix products, arithmetic and copies ran while one was open for 34% -> 9% of each run, Pallas kernels for 0% -> 16%
where the time goes in v2:
time: 275 us; the launch traced here: 274 us
  waiting for transfers between devices  140 us (51%)
  Pallas kernels  54.8 us (20%)
  starting transfers between devices  49.1 us (18%)
  other arithmetic  19.4 us (7%)
  matrix products  5.32 us (2%)
  local copies, waits for them, and re-layouts  4.53 us (2%)
    ppermute x20, waiting for transfers between devices, send_xor(): return lax.ppermute(value, axis, [(i, i ^ mask) for i in range(size)])  85.3 us
    pallas_call x4, Pallas kernels, slot_work(): pl.pallas_call(functools.partial(slot_kernel, blocks), out_shape=[jax.Sha...  36 us
    pallas_call x2, Pallas kernels, weight_work(): pl.pallas_call(functools.partial(weight_kernel, len(slots), bool(before),...  18.8 us
    ppermute x1, waiting for transfers between devices, body(): x_relayed = lax.ppermute(after(x_first, x_across), 'seq', MIDDLE)  17.6 us
    ppermute x20, starting transfers between devices, send_xor(): return lax.ppermute(value, axis, [(i, i ^ mask) for i in range(size)])  14.4 us
    ppermute x1, waiting for transfers between devices, body(): over = lax.ppermute(token_parts[2], 'seq', MIDDLE)  9.72 us
    ppermute x1, waiting for transfers between devices, body(): dy_far = lax.ppermute(after(dy_relayed, dy_near, done), 'seq', OUTWARD)  8.44 us
    ppermute x1, waiting for transfers between devices, body(): dy_relayed = lax.ppermute(after(dy_first, dy_across, done), 'seq', MIDDLE)  8.32 us
  transfers between devices with their start and end apart: 32, of which 15 were waited for; matrix products, arithmetic and copies ran while one was open for 9% of the time, Pallas kernels for 16%

profile of v2, /device:TPU:8, one launch (start us, length us, event | category | flops | bytes accessed | tf_op | source)
XLA Modules:
  0.0 274.1 jit_solution(11882246941907198079)
XLA Ops:
  0.7 1.0 fusion.3
  1.6 0.7 convert_add_fusion.1
  2.7 1.6 collective-permute-start
  4.3 1.2 convolution_convert_fusion.1
  5.5 0.5 collective-permute-start.3
  6.3 3.5 %collective-permute-start.4 = (bf16[68,4096]{1,0:T(8,128)(2,1)S(1)}, bf16[68,4096]{1,0:T(8,128)(2,1)S(1)}, u32[]{:S(2)}, u32[]{:S(2)}) collective-permute-start(bf16[68,4096]{1,0:T(8,128)(2,1)S(1)} %convolution_convert_fusion.4), channel_id=1, source_target_pairs={{1,2},{2,1},{5,6},{6,5},{9,10},{10,9},{13,14},{14,13},{17,18},{18,... | collective-permute-start | bytes 1671176 | tf_op jit(solution)/shard_map/ppermute | solution.py:321
  9.9 9.2 %collective-permute-done = bf16[68,4096]{1,0:T(8,128)(2,1)} collective-permute-done((bf16[68,4096]{1,0:T(8,128)(2,1)S(1)}, bf16[68,4096]{1,0:T(8,128)(2,1)}, u32[]{:S(2)}, u32[]{:S(2)}) %collective-permute-start) | collective-permute-done | bytes 557088 | tf_op jit(solution)/shard_map/ppermute | solution.py:31
  19.4 5.1 %collective-permute-start.5 = (bf16[68,4096]{1,0:T(8,128)(2,1)}, bf16[68,4096]{1,0:T(8,128)(2,1)S(1)}, u32[]{:S(2)}, u32[]{:S(2)}) collective-permute-start(bf16[68,4096]{1,0:T(8,128)(2,1)} %collective-permute-done), channel_id=1, source_target_pairs={{1,2},{2,1},{5,6},{6,5},{9,10},{10,9},{13,14},{14,13},{17,18},{18,... | collective-permute-start | bytes 1671176 | tf_op jit(solution)/shard_map/ppermute | solution.py:323
  24.5 6.1 %collective-permute-done.3 = bf16[68,4096]{1,0:T(8,128)(2,1)} collective-permute-done((bf16[68,4096]{1,0:T(8,128)(2,1)}, bf16[68,4096]{1,0:T(8,128)(2,1)}, u32[]{:S(2)}, u32[]{:S(2)}) %collective-permute-start.3) | collective-permute-done | bytes 557088 | tf_op jit(solution)/shard_map/ppermute | solution.py:31
  30.6 1.2 pad_maximum_fusion.2.dy
  31.8 3.5 %collective-permute-start.9 = (bf16[136,4096]{1,0:T(8,128)(2,1)S(1)}, bf16[136,4096]{1,0:T(8,128)(2,1)}, u32[]{:S(2)}, u32[]{:S(2)}) collective-permute-start(bf16[136,4096]{1,0:T(8,128)(2,1)S(1)} %pad_maximum_fusion.2.dy), channel_id=1, source_target_pairs={{1,2},{2,1},{5,6},{6,5},{9,10},{10,9},{13,14},{14,13},{17,18},{18,... | collective-permute-start | bytes 3342344 | tf_op jit(solution)/shard_map/ppermute | solution.py:325
  35.4 1.4 collective-permute-done.2
  36.8 1.4 pad_maximum_fusion.1.x
  38.3 1.3 pad_maximum_fusion.3
  39.6 2.3 collective-permute-start.6
  42.0 2.9 %collective-permute-start.7 = (bf16[136,4096]{1,0:T(8,128)(2,1)}, bf16[136,4096]{1,0:T(8,128)(2,1)}, u32[]{:S(2)}, u32[]{:S(2)}) collective-permute-start(bf16[136,4096]{1,0:T(8,128)(2,1)} %pad_maximum_fusion.3), channel_id=1, source_target_pairs={{1,0},{2,3},{5,4},{6,7},{9,8},{10,11},{13,12},{14,15},{17,16},{18,... | collective-permute-start | bytes 3342344 | tf_op jit(solution)/shard_map/ppermute | solution.py:330
  44.9 0.6 pad_add_fusion.place.refs_0_
  45.5 2.2 pad_maximum_fusion.x
  47.7 8.9 %slot_work.4 = (bf16[136,4224]{1,0:T(8,128)(2,1)}, bf16[144,5248]{1,0:T(8,128)(2,1)}, bf16[144,3200]{1,0:T(8,128)(2,1)}, bf16[144,3200]{1,0:T(8,128)(2,1)}) custom-call(s32[2]{0:T(128)} %pad_add_fusion.place.refs_0_, bf16[136,4096]{1,0:T(8,128)(2,1)} %pad_maximum_fusion.x, bf16[136,4096]{1,0:T(8,128)(2,1)} %copy-done.3, bf16[4096,384]{1,0:T(8,128)(2,1)} %bitcast.20, ...), custom_call_target="tpu_custom_call" | custom-call | tf_op jit(solution)/shard_map/slot_work/pallas_call | solution.py:160
  56.6 1.6 collective-permute-start.13
  58.2 3.1 %collective-permute-done.9 = bf16[136,4096]{1,0:T(8,128)(2,1)} collective-permute-done((bf16[136,4096]{1,0:T(8,128)(2,1)S(1)}, bf16[136,4096]{1,0:T(8,128)(2,1)}, u32[]{:S(2)}, u32[]{:S(2)}) %collective-permute-start.9) | collective-permute-done | bytes 1114144 | tf_op jit(solution)/shard_map/ppermute | solution.py:325
  61.3 3.5 %collective-permute-start.10 = (bf16[136,4096]{1,0:T(8,128)(2,1)}, bf16[136,4096]{1,0:T(8,128)(2,1)}, u32[]{:S(2)}, u32[]{:S(2)}) collective-permute-start(bf16[136,4096]{1,0:T(8,128)(2,1)} %collective-permute-done.8.dy), channel_id=1, source_target_pairs={{1,2},{2,1},{5,6},{6,5},{9,10},{10,9},{13,14},{14,13},{17,18},{18,... | collective-permute-start | bytes 3342344 | tf_op jit(solution)/shard_map/ppermute | solution.py:331
  64.8 2.7 %collective-permute-start.11 = (bf16[136,4096]{1,0:T(8,128)(2,1)}, bf16[136,4096]{1,0:T(8,128)(2,1)}, u32[]{:S(2)}, u32[]{:S(2)}) collective-permute-start(bf16[136,4096]{1,0:T(8,128)(2,1)} %collective-permute-done.9), channel_id=1, source_target_pairs={{1,0},{2,3},{5,4},{6,7},{9,8},{10,11},{13,12},{14,15},{17,16},{18,... | collective-permute-start | bytes 3342344 | tf_op jit(solution)/shard_map/ppermute | solution.py:332
  67.6 17.6 %collective-permute-done.6 = bf16[136,4096]{1,0:T(8,128)(2,1)} collective-permute-done((bf16[136,4096]{1,0:T(8,128)(2,1)S(1)}, bf16[136,4096]{1,0:T(8,128)(2,1)}, u32[]{:S(2)}, u32[]{:S(2)}) %collective-permute-start.6) | collective-permute-done | bytes 1114144 | tf_op jit(solution)/shard_map/ppermute | solution.py:329
  85.2 2.4 broadcast_select_fusion.3.x
  87.6 2.5 collective-permute-done.13.refs_3_
  90.1 9.0 %slot_work.6 = (bf16[136,4224]{1,0:T(8,128)(2,1)}, bf16[144,5248]{1,0:T(8,128)(2,1)}, bf16[144,3200]{1,0:T(8,128)(2,1)}, bf16[144,3200]{1,0:T(8,128)(2,1)}) custom-call(s32[2]{0:T(128)} %pad_add_fusion.place.refs_0_, bf16[136,4096]{1,0:T(8,128)(2,1)} %copy-done.2, bf16[136,4096]{1,0:T(8,128)(2,1)} %collective-permute-done.8.dy, bf16[4096,384]{1,0:T(8,128)(2,1)} %bitcast.21, ...), custom_call_target="tpu_custom_call" | custom-call | tf_op jit(solution)/shard_map/slot_work/pallas_call | solution.py:160
  99.1 8.3 %collective-permute-done.10 = bf16[136,4096]{1,0:T(8,128)(2,1)} collective-permute-done((bf16[136,4096]{1,0:T(8,128)(2,1)}, bf16[136,4096]{1,0:T(8,128)(2,1)}, u32[]{:S(2)}, u32[]{:S(2)}) %collective-permute-start.10) | collective-permute-done | bytes 1114144 | tf_op jit(solution)/shard_map/ppermute | solution.py:331
  107.5 3.4 %collective-permute-start.22 = (bf16[136,4096]{1,0:T(8,128)(2,1)}, bf16[136,4096]{1,0:T(8,128)(2,1)S(1)}, u32[]{:S(2)}, u32[]{:S(2)}) collective-permute-start(bf16[136,4096]{1,0:T(8,128)(2,1)} %collective-permute-done.10), channel_id=1, source_target_pairs={{1,0},{2,3},{5,4},{6,7},{9,8},{10,11},{13,12},{14,15},{17,16},{18,... | collective-permute-start | bytes 3342344 | tf_op jit(solution)/shard_map/ppermute | solution.py:339
  110.9 2.4 broadcast_select_fusion.2.dy
  113.3 9.1 %slot_work.5 = (bf16[136,4224]{1,0:T(8,128)(2,1)}, bf16[144,5248]{1,0:T(8,128)(2,1)}, bf16[144,3200]{1,0:T(8,128)(2,1)}, bf16[144,3200]{1,0:T(8,128)(2,1)}) custom-call(s32[2]{0:T(128)} %pad_add_fusion.place.refs_0_, bf16[136,4096]{1,0:T(8,128)(2,1)} %broadcast_select_fusion.3.x, bf16[136,4096]{1,0:T(8,128)(2,1)} %broadcast_select_fusion.2.dy, ...), custom_call_target="tpu_custom_call" | custom-call | tf_op jit(solution)/shard_map/slot_work/pallas_call | solution.py:160
  122.4 3.1 %collective-permute-start.14 = (bf16[136,4224]{1,0:T(8,128)(2,1)}, bf16[136,4224]{1,0:T(8,128)(2,1)S(1)}, u32[]{:S(2)}, u32[]{:S(2)}) collective-permute-start(bf16[136,4224]{1,0:T(8,128)(2,1)} %get-tuple-element.43), channel_id=1, source_target_pairs={{1,2},{2,1},{5,6},{6,5},{9,10},{10,9},{13,14},{14,13},{17,18},{18,... | collective-permute-start | bytes 3446792 | tf_op jit(solution)/shard_map/ppermute | solution.py:340
  125.6 1.4 collective-permute-start.21
  127.0 0.5 collective-permute-start.18
  127.5 8.4 %collective-permute-done.22 = bf16[136,4096]{1,0:T(8,128)(2,1)S(1)} collective-permute-done((bf16[136,4096]{1,0:T(8,128)(2,1)}, bf16[136,4096]{1,0:T(8,128)(2,1)S(1)}, u32[]{:S(2)}, u32[]{:S(2)}) %collective-permute-start.22) | collective-permute-done | bytes 1114144 | tf_op jit(solution)/shard_map/ppermute | solution.py:339
  136.0 1.5 collective-permute-start.19
  137.4 2.4 broadcast_select_fusion.dy
  139.8 9.7 %collective-permute-done.14 = bf16[136,4224]{1,0:T(8,128)(2,1)S(1)} collective-permute-done((bf16[136,4224]{1,0:T(8,128)(2,1)}, bf16[136,4224]{1,0:T(8,128)(2,1)S(1)}, u32[]{:S(2)}, u32[]{:S(2)}) %collective-permute-start.14) | collective-permute-done | bytes 1148960 | tf_op jit(solution)/shard_map/ppermute | solution.py:340
  149.9 7.0 %collective-permute-done.21 = bf16[136,4096]{1,0:T(8,128)(2,1)S(1)} collective-permute-done((bf16[136,4096]{1,0:T(8,128)(2,1)}, bf16[136,4096]{1,0:T(8,128)(2,1)S(1)}, u32[]{:S(2)}, u32[]{:S(2)}) %collective-permute-start.21) | collective-permute-done | bytes 1114144 | tf_op jit(solution)/shard_map/ppermute | solution.py:334
  156.9 1.3 collective-permute-start.12
  158.2 7.2 %collective-permute-done.19.refs_7_ = bf16[144,5248]{1,0:T(8,128)(2,1)S(1)} collective-permute-done((bf16[144,5248]{1,0:T(8,128)(2,1)}, bf16[144,5248]{1,0:T(8,128)(2,1)S(1)}, u32[]{:S(2)}, u32[]{:S(2)}) %collective-permute-start.19) | collective-permute-done | bytes 1511456 | tf_op jit(solution)/shard_map/ppermute | solution.py:31
  165.4 1.5 broadcast_select_fusion.1.x
  166.9 9.0 %slot_work.7 = (bf16[136,4224]{1,0:T(8,128)(2,1)}, bf16[144,5248]{1,0:T(8,128)(2,1)}, bf16[144,3200]{1,0:T(8,128)(2,1)}, bf16[144,3200]{1,0:T(8,128)(2,1)}) custom-call(s32[2]{0:T(128)} %pad_add_fusion.place.refs_0_, bf16[136,4096]{1,0:T(8,128)(2,1)} %broadcast_select_fusion.1.x, bf16[136,4096]{1,0:T(8,128)(2,1)} %broadcast_select_fusion.dy, ...), custom_call_target="tpu_custom_call" | custom-call | tf_op jit(solution)/shard_map/slot_work/pallas_call | solution.py:160
  175.9 2.4 collective-permute-start.15
  178.3 2.4 fusion.29
  180.9 1.5 collective-permute-start.27
  182.3 2.0 collective-permute-start.25
  184.4 8.7 %weight_work.2 = (f32[1024,384]{1,0:T(8,128)}, f32[1024,384]{1,0:T(8,128)}, f32[384,1024]{1,0:T(8,128)}) custom-call(s32[2]{0:T(128)} %pad_add_fusion.place.refs_0_, bf16[144,3200]{1,0:T(8,128)(2,1)} %get-tuple-element.47.refs_1_, bf16[144,3200]{1,0:T(8,128)(2,1)} %collective-permute-done.16.refs_2_, bf16[144,5248]{1,0:T(8,128)(2,1)} %collective-permute-done.13.refs_3_, ...), custom_call_target="tpu_custom_call" | custom-call | tf_op jit(solution)/shard_map/weight_work/pallas_call | solution.py:243
  193.1 19.3 %collective-permute-done.15 = bf16[136,4224]{1,0:T(8,128)(2,1)S(1)} collective-permute-done((bf16[136,4224]{1,0:T(8,128)(2,1)S(1)}, bf16[136,4224]{1,0:T(8,128)(2,1)S(1)}, u32[]{:S(2)}, u32[]{:S(2)}) %collective-permute-start.15) | collective-permute-done | bytes 1148960 | tf_op jit(solution)/shard_map/ppermute | solution.py:31
  212.4 0.9 collective-permute-start.23
  213.3 1.5 collective-permute-start.30
  214.8 1.7 convert_add_fusion
  216.6 28.7 %collective-permute-done.23 = bf16[68,4224]{1,0:T(8,128)(2,1)S(1)} collective-permute-done((bf16[68,4224]{1,0:T(8,128)(2,1)}, bf16[68,4224]{1,0:T(8,128)(2,1)S(1)}, u32[]{:S(2)}, u32[]{:S(2)}) %collective-permute-start.23) | collective-permute-done | bytes 574496 | tf_op jit(solution)/shard_map/ppermute | solution.py:31
  245.4 1.5 collective-permute-start.24
  247.1 0.5 collective-permute-start.28
  247.6 1.2 collective-permute-done.30.refs_7_
  248.8 9.5 %collective-permute-done.24 = bf16[68,4224]{1,0:T(8,128)(2,1)S(1)} collective-permute-done((bf16[68,4224]{1,0:T(8,128)(2,1)S(1)}, bf16[68,4224]{1,0:T(8,128)(2,1)S(1)}, u32[]{:S(2)}, u32[]{:S(2)}) %collective-permute-start.24) | collective-permute-done | bytes 574496 | tf_op jit(solution)/shard_map/ppermute | solution.py:31
  258.3 1.2 add_convert_fusion.1
  259.5 0.7 fusion.5
  260.3 1.5 convolution_convert_fusion
  261.8 0.9 copy-done.13
  262.7 0.6 copy-done.9
  263.3 0.5 copy-done.10
  263.8 10.2 %weight_work.3 = (bf16[1024,384]{1,0:T(8,128)(2,1)}, bf16[1024,384]{1,0:T(8,128)(2,1)}, bf16[384,1024]{1,0:T(8,128)(2,1)}) custom-call(s32[2]{0:T(128)} %pad_add_fusion.place.refs_0_, bf16[144,3200]{1,0:T(8,128)(2,1)} %get-tuple-element.58.refs_1_, bf16[144,3200]{1,0:T(8,128)(2,1)} %collective-permute-done.26.refs_2_, bf16[144,5248]{1,0:T(8,128)(2,1)} %copy-done.5, ...), custom_call_target="tpu_custom_call" | custom-call | tf_op jit(solution)/shard_map/weight_work/pallas_call | solution.py:243
  (64 shorter events, 2.1 us)
Async XLA Ops:
  0.6 1.7 copy-start
  0.6 3.6 %copy-start.14 = (bf16[128]{0:T(256)(128)(2,1)S(1)}, bf16[128]{0:T(256)(128)(2,1)}, u32[]{:S(2)}) copy-start(bf16[128]{0:T(256)(128)(2,1)} %param.9) | copy-start | bytes 772
  0.7 3.6 %copy-start.4 = (bf16[128,4096]{1,0:T(8,128)(2,1)S(1)}, bf16[128,4096]{1,0:T(8,128)(2,1)}, u32[]{:S(2)}) copy-start(bf16[128,4096]{1,0:T(8,128)(2,1)} %param.8) | copy-start | bytes 3145732
  2.7 16.4 %collective-permute-start = (bf16[68,4096]{1,0:T(8,128)(2,1)S(1)}, bf16[68,4096]{1,0:T(8,128)(2,1)}, u32[]{:S(2)}, u32[]{:S(2)}) collective-permute-start(bf16[68,4096]{1,0:T(8,128)(2,1)S(1)} %convolution_convert_fusion.3), channel_id=1, source_target_pairs={{0,4},{4,0},{1,5},{5,1},{2,6},{6,2},{3,7},{7,3},{8,12},{12,8},{9,1... | collective-permute-start | bytes 1671176 | tf_op jit(solution)/shard_map/ppermute | solution.py:31
  5.5 25.1 %collective-permute-start.3 = (bf16[68,4096]{1,0:T(8,128)(2,1)}, bf16[68,4096]{1,0:T(8,128)(2,1)}, u32[]{:S(2)}, u32[]{:S(2)}) collective-permute-start(bf16[68,4096]{1,0:T(8,128)(2,1)} %convolution_convert_fusion.1), channel_id=1, source_target_pairs={{0,4},{4,0},{1,5},{5,1},{2,6},{6,2},{3,7},{7,3},{8,12},{12,8},{9,1... | collective-permute-start | bytes 1671176 | tf_op jit(solution)/shard_map/ppermute | solution.py:31
  6.3 32.0 %collective-permute-start.4 = (bf16[68,4096]{1,0:T(8,128)(2,1)S(1)}, bf16[68,4096]{1,0:T(8,128)(2,1)S(1)}, u32[]{:S(2)}, u32[]{:S(2)}) collective-permute-start(bf16[68,4096]{1,0:T(8,128)(2,1)S(1)} %convolution_convert_fusion.4), channel_id=1, source_target_pairs={{1,2},{2,1},{5,6},{6,5},{9,10},{10,9},{13,14},{14,13},{17,18},{18,... | collective-permute-start | bytes 1671176 | tf_op jit(solution)/shard_map/ppermute | solution.py:321
  9.8 25.5 %collective-permute-start.1 = (bf16[68,4096]{1,0:T(8,128)(2,1)S(1)}, bf16[68,4096]{1,0:T(8,128)(2,1)}, u32[]{:S(2)}, u32[]{:S(2)}) collective-permute-start(bf16[68,4096]{1,0:T(8,128)(2,1)S(1)} %convolution_convert_fusion.4), channel_id=1, source_target_pairs={{0,1},{1,0},{2,3},{3,2},{4,5},{5,4},{6,7},{7,6},{8,9},{9,8},{10,11... | collective-permute-start | bytes 1671176 | tf_op jit(solution)/shard_map/ppermute | solution.py:31
  19.1 17.7 %collective-permute-start.2 = (bf16[68,4096]{1,0:T(8,128)(2,1)}, bf16[68,4096]{1,0:T(8,128)(2,1)}, u32[]{:S(2)}, u32[]{:S(2)}) collective-permute-start(bf16[68,4096]{1,0:T(8,128)(2,1)} %collective-permute-done), channel_id=1, source_target_pairs={{0,1},{1,0},{2,3},{3,2},{4,5},{5,4},{6,7},{7,6},{8,9},{9,8},{10,11... | collective-permute-start | bytes 1671176 | tf_op jit(solution)/shard_map/ppermute | solution.py:31
  19.4 18.8 %collective-permute-start.5 = (bf16[68,4096]{1,0:T(8,128)(2,1)}, bf16[68,4096]{1,0:T(8,128)(2,1)S(1)}, u32[]{:S(2)}, u32[]{:S(2)}) collective-permute-start(bf16[68,4096]{1,0:T(8,128)(2,1)} %collective-permute-done), channel_id=1, source_target_pairs={{1,2},{2,1},{5,6},{6,5},{9,10},{10,9},{13,14},{14,13},{17,18},{18,... | collective-permute-start | bytes 1671176 | tf_op jit(solution)/shard_map/ppermute | solution.py:323
  31.8 7.8 %copy-start.3 = (bf16[136,4096]{1,0:T(8,128)(2,1)}, bf16[136,4096]{1,0:T(8,128)(2,1)S(1)}, u32[]{:S(2)}) copy-start(bf16[136,4096]{1,0:T(8,128)(2,1)S(1)} %pad_maximum_fusion.2.dy) | copy-start | bytes 3342340
  31.8 29.5 %collective-permute-start.9 = (bf16[136,4096]{1,0:T(8,128)(2,1)S(1)}, bf16[136,4096]{1,0:T(8,128)(2,1)}, u32[]{:S(2)}, u32[]{:S(2)}) collective-permute-start(bf16[136,4096]{1,0:T(8,128)(2,1)S(1)} %pad_maximum_fusion.2.dy), channel_id=1, source_target_pairs={{1,2},{2,1},{5,6},{6,5},{9,10},{10,9},{13,14},{14,13},{17,18},{18,... | collective-permute-start | bytes 3342344 | tf_op jit(solution)/shard_map/ppermute | solution.py:325
  35.3 26.0 %collective-permute-start.8 = (bf16[136,4096]{1,0:T(8,128)(2,1)S(1)}, bf16[136,4096]{1,0:T(8,128)(2,1)}, u32[]{:S(2)}, u32[]{:S(2)}) collective-permute-start(bf16[136,4096]{1,0:T(8,128)(2,1)S(1)} %pad_maximum_fusion.2.dy), channel_id=1, source_target_pairs={{0,1},{1,0},{2,3},{3,2},{4,5},{5,4},{6,7},{7,6},{8,9},{9,8},{10,11... | collective-permute-start | bytes 3342344 | tf_op jit(solution)/shard_map/ppermute | solution.py:31
  38.2 7.2 %copy-start.2 = (bf16[136,4096]{1,0:T(8,128)(2,1)}, bf16[136,4096]{1,0:T(8,128)(2,1)S(1)}, u32[]{:S(2)}) copy-start(bf16[136,4096]{1,0:T(8,128)(2,1)S(1)} %pad_maximum_fusion.1.x) | copy-start | bytes 3342340
  39.6 45.6 %collective-permute-start.6 = (bf16[136,4096]{1,0:T(8,128)(2,1)S(1)}, bf16[136,4096]{1,0:T(8,128)(2,1)}, u32[]{:S(2)}, u32[]{:S(2)}) collective-permute-start(bf16[136,4096]{1,0:T(8,128)(2,1)S(1)} %pad_maximum_fusion.1.x), channel_id=1, source_target_pairs={{1,2},{2,1},{5,6},{6,5},{9,10},{10,9},{13,14},{14,13},{17,18},{18,... | collective-permute-start | bytes 3342344 | tf_op jit(solution)/shard_map/ppermute | solution.py:329
  42.0 43.2 %collective-permute-start.7 = (bf16[136,4096]{1,0:T(8,128)(2,1)}, bf16[136,4096]{1,0:T(8,128)(2,1)}, u32[]{:S(2)}, u32[]{:S(2)}) collective-permute-start(bf16[136,4096]{1,0:T(8,128)(2,1)} %pad_maximum_fusion.3), channel_id=1, source_target_pairs={{1,0},{2,3},{5,4},{6,7},{9,8},{10,11},{13,12},{14,15},{17,16},{18,... | collective-permute-start | bytes 3342344 | tf_op jit(solution)/shard_map/ppermute | solution.py:330
  56.6 33.5 %collective-permute-start.13 = (bf16[144,5248]{1,0:T(8,128)(2,1)}, bf16[144,5248]{1,0:T(8,128)(2,1)}, u32[]{:S(2)}, u32[]{:S(2)}) collective-permute-start(bf16[144,5248]{1,0:T(8,128)(2,1)} %get-tuple-element.44), channel_id=1, source_target_pairs={{0,16},{8,24},{16,0},{24,8},{1,17},{9,25},{17,1},{25,9},{2,18},{10... | collective-permute-start | bytes 4534280 | tf_op jit(solution)/shard_map/ppermute | solution.py:31
  61.3 46.1 %collective-permute-start.10 = (bf16[136,4096]{1,0:T(8,128)(2,1)}, bf16[136,4096]{1,0:T(8,128)(2,1)}, u32[]{:S(2)}, u32[]{:S(2)}) collective-permute-start(bf16[136,4096]{1,0:T(8,128)(2,1)} %collective-permute-done.8.dy), channel_id=1, source_target_pairs={{1,2},{2,1},{5,6},{6,5},{9,10},{10,9},{13,14},{14,13},{17,18},{18,... | collective-permute-start | bytes 3342344 | tf_op jit(solution)/shard_map/ppermute | solution.py:331
  64.8 42.6 %collective-permute-start.11 = (bf16[136,4096]{1,0:T(8,128)(2,1)}, bf16[136,4096]{1,0:T(8,128)(2,1)}, u32[]{:S(2)}, u32[]{:S(2)}) collective-permute-start(bf16[136,4096]{1,0:T(8,128)(2,1)} %collective-permute-done.9), channel_id=1, source_target_pairs={{1,0},{2,3},{5,4},{6,7},{9,8},{10,11},{13,12},{14,15},{17,16},{18,... | collective-permute-start | bytes 3342344 | tf_op jit(solution)/shard_map/ppermute | solution.py:332
  107.5 28.5 %collective-permute-start.22 = (bf16[136,4096]{1,0:T(8,128)(2,1)}, bf16[136,4096]{1,0:T(8,128)(2,1)S(1)}, u32[]{:S(2)}, u32[]{:S(2)}) collective-permute-start(bf16[136,4096]{1,0:T(8,128)(2,1)} %collective-permute-done.10), channel_id=1, source_target_pairs={{1,0},{2,3},{5,4},{6,7},{9,8},{10,11},{13,12},{14,15},{17,16},{18,... | collective-permute-start | bytes 3342344 | tf_op jit(solution)/shard_map/ppermute | solution.py:339
  113.3 12.2 %copy-start.15 = (bf16[144,3200]{1,0:T(8,128)(2,1)S(1)}, bf16[144,3200]{1,0:T(8,128)(2,1)}, u32[]{:S(2)}) copy-start(bf16[144,3200]{1,0:T(8,128)(2,1)} %get-tuple-element.48) | copy-start | bytes 2764804
  122.4 27.1 %collective-permute-start.14 = (bf16[136,4224]{1,0:T(8,128)(2,1)}, bf16[136,4224]{1,0:T(8,128)(2,1)S(1)}, u32[]{:S(2)}, u32[]{:S(2)}) collective-permute-start(bf16[136,4224]{1,0:T(8,128)(2,1)} %get-tuple-element.43), channel_id=1, source_target_pairs={{1,2},{2,1},{5,6},{6,5},{9,10},{10,9},{13,14},{14,13},{17,18},{18,... | collective-permute-start | bytes 3446792 | tf_op jit(solution)/shard_map/ppermute | solution.py:340
  125.5 50.3 %collective-permute-start.16 = (bf16[144,3200]{1,0:T(8,128)(2,1)S(1)}, bf16[144,3200]{1,0:T(8,128)(2,1)}, u32[]{:S(2)}, u32[]{:S(2)}) collective-permute-start(bf16[144,3200]{1,0:T(8,128)(2,1)S(1)} %copy-done.15), channel_id=1, source_target_pairs={{0,8},{8,0},{16,24},{24,16},{1,9},{9,1},{17,25},{25,17},{2,10},{10... | collective-permute-start | bytes 2764808 | tf_op jit(solution)/shard_map/ppermute | solution.py:31
  125.6 31.3 %collective-permute-start.21 = (bf16[136,4096]{1,0:T(8,128)(2,1)}, bf16[136,4096]{1,0:T(8,128)(2,1)S(1)}, u32[]{:S(2)}, u32[]{:S(2)}) collective-permute-start(bf16[136,4096]{1,0:T(8,128)(2,1)} %collective-permute-done.6), channel_id=1, source_target_pairs={{1,0},{2,3},{5,4},{6,7},{9,8},{10,11},{13,12},{14,15},{17,16},{18,... | collective-permute-start | bytes 3342344 | tf_op jit(solution)/shard_map/ppermute | solution.py:334
  127.0 53.7 %collective-permute-start.18 = (bf16[144,3200]{1,0:T(8,128)(2,1)}, bf16[144,3200]{1,0:T(8,128)(2,1)}, u32[]{:S(2)}, u32[]{:S(2)}) collective-permute-start(bf16[144,3200]{1,0:T(8,128)(2,1)} %get-tuple-element.50), channel_id=1, source_target_pairs={{0,8},{8,0},{16,24},{24,16},{1,9},{9,1},{17,25},{25,17},{2,10},{10... | collective-permute-start | bytes 2764808 | tf_op jit(solution)/shard_map/ppermute | solution.py:31
  136.0 13.6 %copy-start.11 = (bf16[136,4224]{1,0:T(8,128)(2,1)S(1)}, bf16[136,4224]{1,0:T(8,128)(2,1)}, u32[]{:S(2)}) copy-start(bf16[136,4224]{1,0:T(8,128)(2,1)} %get-tuple-element.46) | copy-start | bytes 3446788
  136.0 29.4 %collective-permute-start.19 = (bf16[144,5248]{1,0:T(8,128)(2,1)}, bf16[144,5248]{1,0:T(8,128)(2,1)S(1)}, u32[]{:S(2)}, u32[]{:S(2)}) collective-permute-start(bf16[144,5248]{1,0:T(8,128)(2,1)} %get-tuple-element.51), channel_id=1, source_target_pairs={{0,16},{8,24},{16,0},{24,8},{1,17},{9,25},{17,1},{25,9},{2,18},{10... | collective-permute-start | bytes 4534280 | tf_op jit(solution)/shard_map/ppermute | solution.py:31
  149.5 31.3 %collective-permute-start.17 = (bf16[144,5248]{1,0:T(8,128)(2,1)}, bf16[144,5248]{1,0:T(8,128)(2,1)S(1)}, u32[]{:S(2)}, u32[]{:S(2)}) collective-permute-start(bf16[144,5248]{1,0:T(8,128)(2,1)} %collective-permute-done.13.refs_3_), channel_id=1, source_target_pairs={{0,8},{8,0},{16,24},{24,16},{1,9},{9,1},{17,25},{25,17},{2,10},{10... | collective-permute-start | bytes 4534280 | tf_op jit(solution)/shard_map/ppermute | solution.py:31
  156.9 56.4 %collective-permute-start.12 = (bf16[136,4224]{1,0:T(8,128)(2,1)}, bf16[136,4224]{1,0:T(8,128)(2,1)}, u32[]{:S(2)}, u32[]{:S(2)}) collective-permute-start(bf16[136,4224]{1,0:T(8,128)(2,1)} %get-tuple-element.43), channel_id=1, source_target_pairs={{0,2},{3,1},{4,6},{7,5},{8,10},{11,9},{12,14},{15,13},{16,18},{19,... | collective-permute-start | bytes 3446792 | tf_op jit(solution)/shard_map/ppermute | solution.py:341
  165.4 1.5 copy-start.6
  165.4 16.9 %collective-permute-start.20 = (bf16[144,5248]{1,0:T(8,128)(2,1)S(1)}, bf16[144,5248]{1,0:T(8,128)(2,1)}, u32[]{:S(2)}, u32[]{:S(2)}) collective-permute-start(bf16[144,5248]{1,0:T(8,128)(2,1)S(1)} %collective-permute-done.19.refs_7_), channel_id=1, source_target_pairs={{0,8},{8,0},{16,24},{24,16},{1,9},{9,1},{17,25},{25,17},{2,10},{10... | collective-permute-start | bytes 4534280 | tf_op jit(solution)/shard_map/ppermute | solution.py:31
  175.9 36.5 %collective-permute-start.15 = (bf16[136,4224]{1,0:T(8,128)(2,1)S(1)}, bf16[136,4224]{1,0:T(8,128)(2,1)S(1)}, u32[]{:S(2)}, u32[]{:S(2)}) collective-permute-start(bf16[136,4224]{1,0:T(8,128)(2,1)S(1)} %add_convert_fusion), channel_id=1, source_target_pairs={{0,1},{1,0},{2,3},{3,2},{4,5},{5,4},{6,7},{7,6},{8,9},{9,8},{10,11... | collective-permute-start | bytes 3446792 | tf_op jit(solution)/shard_map/ppermute | solution.py:31
  180.7 81.1 %collective-permute-start.26 = (bf16[144,3200]{1,0:T(8,128)(2,1)}, bf16[144,3200]{1,0:T(8,128)(2,1)}, u32[]{:S(2)}, u32[]{:S(2)}) collective-permute-start(bf16[144,3200]{1,0:T(8,128)(2,1)} %get-tuple-element.59), channel_id=1, source_target_pairs={{0,8},{8,0},{16,24},{24,16},{1,9},{9,1},{17,25},{25,17},{2,10},{10... | collective-permute-start | bytes 2764808 | tf_op jit(solution)/shard_map/ppermute | solution.py:31
  180.9 3.5 %copy-start.8 = (bf16[144,5248]{1,0:T(8,128)(2,1)}, bf16[144,5248]{1,0:T(8,128)(2,1)S(1)}, u32[]{:S(2)}) copy-start(bf16[144,5248]{1,0:T(8,128)(2,1)S(1)} %collective-permute-done.17.refs_4_) | copy-start | bytes 4534276
  180.9 66.1 %collective-permute-start.27 = (bf16[144,5248]{1,0:T(8,128)(2,1)}, bf16[144,5248]{1,0:T(8,128)(2,1)S(1)}, u32[]{:S(2)}, u32[]{:S(2)}) collective-permute-start(bf16[144,5248]{1,0:T(8,128)(2,1)} %get-tuple-element.60), channel_id=1, source_target_pairs={{0,16},{8,24},{16,0},{24,8},{1,17},{9,25},{17,1},{25,9},{2,18},{10... | collective-permute-start | bytes 4534280 | tf_op jit(solution)/shard_map/ppermute | solution.py:31
  182.3 64.8 %collective-permute-start.25 = (bf16[68,4224]{1,0:T(8,128)(2,1)}, bf16[68,4224]{1,0:T(8,128)(2,1)}, u32[]{:S(2)}, u32[]{:S(2)}) collective-permute-start(bf16[68,4224]{1,0:T(8,128)(2,1)} %get-tuple-element.69), channel_id=1, source_target_pairs={{0,7},{1,6},{2,5},{3,4},{4,3},{5,2},{6,1},{7,0},{8,15},{9,14},{10,... | collective-permute-start | bytes 1723400 | tf_op jit(solution)/shard_map/ppermute | solution.py:42
  184.4 30.4 %copy-start.12 = (bf16[136,4224]{1,0:T(8,128)(2,1)S(1)}, bf16[136,4224]{1,0:T(8,128)(2,1)}, u32[]{:S(2)}) copy-start(bf16[136,4224]{1,0:T(8,128)(2,1)} %get-tuple-element.38) | copy-start | bytes 3446788
  212.4 33.0 %collective-permute-start.23 = (bf16[68,4224]{1,0:T(8,128)(2,1)}, bf16[68,4224]{1,0:T(8,128)(2,1)S(1)}, u32[]{:S(2)}, u32[]{:S(2)}) collective-permute-start(bf16[68,4224]{1,0:T(8,128)(2,1)} %get-tuple-element.70), channel_id=1, source_target_pairs={{0,3},{1,2},{2,1},{3,0},{4,7},{5,6},{6,5},{7,4},{8,11},{9,10},{10,... | collective-permute-start | bytes 1723400 | tf_op jit(solution)/shard_map/ppermute | solution.py:31
  213.3 35.5 %collective-permute-start.30 = (bf16[144,5248]{1,0:T(8,128)(2,1)}, bf16[144,5248]{1,0:T(8,128)(2,1)S(1)}, u32[]{:S(2)}, u32[]{:S(2)}) collective-permute-start(bf16[144,5248]{1,0:T(8,128)(2,1)} %get-tuple-element.63), channel_id=1, source_target_pairs={{0,16},{8,24},{16,0},{24,8},{1,17},{9,25},{17,1},{25,9},{2,18},{10... | collective-permute-start | bytes 4534280 | tf_op jit(solution)/shard_map/ppermute | solution.py:31
  216.6 30.4 %copy-start.16 = (bf16[144,3200]{1,0:T(8,128)(2,1)S(1)}, bf16[144,3200]{1,0:T(8,128)(2,1)}, u32[]{:S(2)}) copy-start(bf16[144,3200]{1,0:T(8,128)(2,1)} %get-tuple-element.62) | copy-start | bytes 2764804
  245.4 13.0 %collective-permute-start.24 = (bf16[68,4224]{1,0:T(8,128)(2,1)S(1)}, bf16[68,4224]{1,0:T(8,128)(2,1)S(1)}, u32[]{:S(2)}, u32[]{:S(2)}) collective-permute-start(bf16[68,4224]{1,0:T(8,128)(2,1)S(1)} %slice.48), channel_id=1, source_target_pairs={{0,4},{4,0},{1,5},{5,1},{2,6},{6,2},{3,7},{7,3},{8,12},{12,8},{9,1... | collective-permute-start | bytes 1723400 | tf_op jit(solution)/shard_map/ppermute | solution.py:31
  247.0 13.3 %copy-start.5 = (bf16[144,5248]{1,0:T(8,128)(2,1)}, bf16[144,5248]{1,0:T(8,128)(2,1)S(1)}, u32[]{:S(2)}) copy-start(bf16[144,5248]{1,0:T(8,128)(2,1)S(1)} %collective-permute-done.27.refs_3_) | copy-start | bytes 4534276
  247.0 14.7 %collective-permute-start.29 = (bf16[144,3200]{1,0:T(8,128)(2,1)S(1)}, bf16[144,3200]{1,0:T(8,128)(2,1)S(1)}, u32[]{:S(2)}, u32[]{:S(2)}) collective-permute-start(bf16[144,3200]{1,0:T(8,128)(2,1)S(1)} %copy-done.16), channel_id=1, source_target_pairs={{0,8},{8,0},{16,24},{24,16},{1,9},{9,1},{17,25},{25,17},{2,10},{10... | collective-permute-start | bytes 2764808 | tf_op jit(solution)/shard_map/ppermute | solution.py:31
  247.1 14.7 %collective-permute-start.28 = (bf16[144,5248]{1,0:T(8,128)(2,1)S(1)}, bf16[144,5248]{1,0:T(8,128)(2,1)S(1)}, u32[]{:S(2)}, u32[]{:S(2)}) collective-permute-start(bf16[144,5248]{1,0:T(8,128)(2,1)S(1)} %collective-permute-done.27.refs_3_), channel_id=1, source_target_pairs={{0,8},{8,0},{16,24},{24,16},{1,9},{9,1},{17,25},{25,17},{2,10},{10... | collective-permute-start | bytes 4534280 | tf_op jit(solution)/shard_map/ppermute | solution.py:31
  248.8 11.5 %copy-start.7 = (bf16[144,5248]{1,0:T(8,128)(2,1)}, bf16[144,5248]{1,0:T(8,128)(2,1)S(1)}, u32[]{:S(2)}) copy-start(bf16[144,5248]{1,0:T(8,128)(2,1)S(1)} %collective-permute-done.30.refs_7_) | copy-start | bytes 4534276
  248.8 13.0 %collective-permute-start.31 = (bf16[144,5248]{1,0:T(8,128)(2,1)S(1)}, bf16[144,5248]{1,0:T(8,128)(2,1)S(1)}, u32[]{:S(2)}, u32[]{:S(2)}) collective-permute-start(bf16[144,5248]{1,0:T(8,128)(2,1)S(1)} %collective-permute-done.30.refs_7_), channel_id=1, source_target_pairs={{0,8},{8,0},{16,24},{24,16},{1,9},{9,1},{17,25},{25,17},{2,10},{10... | collective-permute-start | bytes 4534280 | tf_op jit(solution)/shard_map/ppermute | solution.py:31
  261.8 1.0 copy-start.13
  261.8 1.5 copy-start.9
  261.8 2.0 copy-start.10
  263.8 10.2 %copy-start.1 = (bf16[128,4096]{1,0:T(8,128)(2,1)S(1)}, bf16[128,4096]{1,0:T(8,128)(2,1)}, u32[]{:S(2)}) copy-start(bf16[128,4096]{1,0:T(8,128)(2,1)} %param.7) | copy-start | bytes 3145732

commit v3 on v2

--- a/solution.py
+++ b/solution.py
@@ -15,7 +15,7 @@
 CONTRACT_FIRST = (((0,), (0,)), ((), ()))
 MIDDLE = [(1, 2), (2, 1)]
 OUTWARD = [(1, 0), (2, 3)]
-INWARD_TWO = [(0, 2), (3, 1)]
+INWARD = [(0, 1), (3, 2)]
 
 
 def dot(left, right, dims=PLAIN):
@@ -52,7 +52,6 @@
     wd,
     part,
     far_share,
-    near_share,
     own_share,
     kx,
     ky,
@@ -61,7 +60,6 @@
     kd,
     kp,
     kfar,
-    knear,
     kown,
     sems,
     out_sems,
@@ -69,7 +67,7 @@
     feat, width = kg.shape
     rows = kx.shape[0]
     step = feat // blocks
-    half, quarter = feat // 2, feat // 4
+    half = feat // 2
 
     def fetch(i):
         cols = pl.ds(i * step, step)
@@ -115,15 +113,10 @@
     ).astype(BF)
     up_delta = (scaled_grad * activated).astype(BF)
     hidden = hidden.astype(BF)
-    hi, lo = place[0], place[1]
-    shares = [
-        (kfar, far_share, half, (1 - hi) * half),
-        (knear, near_share, quarter, hi * half + (1 - lo) * quarter),
-        (kown, own_share, quarter, hi * half + lo * quarter),
-    ]
     outs = []
-    for keep, share, count, start in shares:
-        cols = pl.ds(pl.multiple_of(start, quarter), count)
+    for keep, share, side in [(kfar, far_share, 1 - place[0]), (kown, own_share, place[0])]:
+        count = half
+        cols = pl.ds(pl.multiple_of(side * half, half), half)
         keep[:rows, :count] = kx[:, cols]
         keep[:rows, count : 2 * count] = ky[:, cols]
         low = 2 * count
@@ -156,13 +149,13 @@
     wide = -(-3 * width // 128) * 128
     blocks = 4
     away = pl.BlockSpec(memory_space=pltpu.HBM)
-    shares = [(tall, feat + wide), (tall, feat // 2 + wide), (tall, feat // 2 + wide)]
+    shares = [(tall, feat + wide), (tall, feat + wide)]
     return pl.pallas_call(
         functools.partial(slot_kernel, blocks),
         out_shape=[jax.ShapeDtypeStruct((rows, feat + 128), BF)]
         + [jax.ShapeDtypeStruct(shape, BF) for shape in shares],
         in_specs=[pl.BlockSpec(memory_space=pltpu.SMEM)] + [away] * 5,
-        out_specs=[away] * 4,
+        out_specs=[away] * 3,
         scratch_shapes=[
             pltpu.VMEM((rows, feat), BF),
             pltpu.VMEM((rows, feat), BF),
@@ -174,90 +167,75 @@
         + [pltpu.VMEM(shape, BF) for shape in shares]
         + [
             pltpu.SemaphoreType.DMA((5, blocks)),
-            pltpu.SemaphoreType.DMA((3 + blocks,)),
+            pltpu.SemaphoreType.DMA((2 + blocks,)),
         ],
         compiler_params=pltpu.CompilerParams(vmem_limit_bytes=56 * 1024 * 1024),
         name="slot_work",
     )(place, x_rows, dy_rows, gate_local, up_local, down_local)
 
 
-def weight_kernel(slots, started, width, *refs):
-    place, refs = refs[0], refs[1:]
-    sources = [refs[4 * s : 4 * s + 4] for s in range(slots)]
-    refs = refs[4 * slots :]
-    before, refs = (refs[:3], refs[3:]) if started else (None, refs)
-    outs, refs = refs[:3], refs[3:]
-    keep_x, keep_dy, keep_d, sums_gu, sums_d, sems = refs
-    quarter, wide = keep_x.shape[2], keep_d.shape[2]
-    tall = keep_x.shape[1] // 4
+def weight_kernel(count, width, *refs):
+    place, shares, refs = refs[0], refs[1 : 1 + count], refs[1 + count :]
+    keep_gu, give_gu, keep_d, give_d, rows, sums_gu, sums_d, sems = refs
+    quarter = sums_gu.shape[1]
     half = 2 * quarter
-    low = pl.multiple_of(place[1] * quarter, quarter)
-    shifted = pl.multiple_of(half + place[1] * quarter, quarter)
-    copies = []
-    for s in range(slots):
-        own, near, far, cross = sources[s]
-        cuts = [
-            (own, 0, quarter, half),
-            (near, 0, quarter, half),
-            (far, low, shifted, 2 * half),
-            (cross, low, shifted, 2 * half),
-        ]
-        for g, (ref, *starts) in enumerate(cuts):
-            rows = pl.ds(g * tall, tall)
-            for k, (keep, start) in enumerate(zip((keep_x, keep_dy, keep_d), starts)):
-                copy = pltpu.make_async_copy(
-                    ref.at[:, pl.ds(start, keep.shape[2])],
-                    keep.at[s, rows],
-                    sems.at[s, 3 * g + k],
-                )
-                copy.start()
-                copies.append((s, copy))
-    for s in range(slots):
-        for n, copy in copies:
-            if n == s:
-                copy.wait()
-        gate_up = dot(keep_x[s], keep_d[s, :, : 2 * width], CONTRACT_FIRST)
-        down = dot(keep_d[s, :, 2 * width : 3 * width], keep_dy[s], CONTRACT_FIRST)
-        if s == 0 and started:
-            sums_gu[:, :width] = before[0][...] + gate_up[:, :width]
-            sums_gu[:, width:] = before[1][...] + gate_up[:, width:]
-            sums_d[...] = before[2][...] + down
-        elif s == 0:
-            sums_gu[...] = gate_up
-            sums_d[...] = down
-        else:
-            sums_gu[...] += gate_up
-            sums_d[...] += down
-    outs[0][...] = sums_gu[:, :width].astype(outs[0].dtype)
-    outs[1][...] = sums_gu[:, width:].astype(outs[1].dtype)
-    outs[2][...] = sums_d[...].astype(outs[2].dtype)
-
-
-def weight_work(place, width, slots, before, dtype):
-    tall, both = slots[0][0].shape
+    tall = rows.shape[0] // count
+    copies = [
+        pltpu.make_async_copy(share, rows.at[pl.ds(n * tall, tall)], sems.at[n])
+        for n, share in enumerate(shares)
+    ]
+    for copy in copies:
+        copy.start()
+    for copy in copies:
+        copy.wait()
+    low = 2 * half
+    cut = quarter // 2
+    for q in range(2):
+        for c in range(2):
+            x_cols = pl.ds(q * quarter + c * cut, cut)
+            dy_cols = pl.ds(half + q * quarter + c * cut, cut)
+            cols = pl.ds(c * cut, cut)
+            sums_gu[q, cols] = dot(
+                rows[:, x_cols], rows[:, low : low + 2 * width], CONTRACT_FIRST
+            ).astype(BF)
+            sums_d[q, :, cols] = dot(
+                rows[:, low + 2 * width : low + 3 * width], rows[:, dy_cols], CONTRACT_FIRST
+            ).astype(BF)
+    mine = place[1]
+    copies = [
+        pltpu.make_async_copy(sums_gu.at[1 - mine], give_gu, sems.at[0]),
+        pltpu.make_async_copy(sums_d.at[1 - mine], give_d, sems.at[1]),
+        pltpu.make_async_copy(sums_gu.at[mine], keep_gu, sems.at[2]),
+        pltpu.make_async_copy(sums_d.at[mine], keep_d, sems.at[3]),
+    ]
+    for copy in copies:
+        copy.start()
+    for copy in copies:
+        copy.wait()
+
+
+def weight_work(place, width, shares):
+    tall, both = shares[0].shape
     wide = -(-3 * width // 128) * 128
-    quarter = (both - wide) // 2
-    whole = pl.BlockSpec(memory_space=pltpu.VMEM)
+    quarter = (both - wide) // 4
+    count = len(shares)
     away = pl.BlockSpec(memory_space=pltpu.HBM)
-    shapes = [(quarter, width), (quarter, width), (width, quarter)]
-    return pl.pallas_call(
-        functools.partial(weight_kernel, len(slots), bool(before), width),
-        out_shape=[jax.ShapeDtypeStruct(shape, dtype) for shape in shapes],
-        in_specs=[pl.BlockSpec(memory_space=pltpu.SMEM)]
-        + [away] * (4 * len(slots))
-        + [whole] * len(before),
-        out_specs=[whole] * 3,
+    shapes = [(quarter, 2 * width), (quarter, 2 * width), (width, quarter), (width, quarter)]
+    keep_gu, give_gu, keep_d, give_d = pl.pallas_call(
+        functools.partial(weight_kernel, count, width),
+        out_shape=[jax.ShapeDtypeStruct(shape, BF) for shape in shapes],
+        in_specs=[pl.BlockSpec(memory_space=pltpu.SMEM)] + [away] * count,
+        out_specs=[away] * 4,
         scratch_shapes=[
-            pltpu.VMEM((len(slots), 4 * tall, quarter), BF),
-            pltpu.VMEM((len(slots), 4 * tall, quarter), BF),
-            pltpu.VMEM((len(slots), 4 * tall, wide), BF),
-            pltpu.VMEM((quarter, 2 * width), F32),
-            pltpu.VMEM((width, quarter), F32),
-            pltpu.SemaphoreType.DMA((len(slots), 12)),
+            pltpu.VMEM((count * tall, both), BF),
+            pltpu.VMEM((2, quarter, 2 * width), BF),
+            pltpu.VMEM((2, width, quarter), BF),
+            pltpu.SemaphoreType.DMA((max(count, 4),)),
         ],
         compiler_params=pltpu.CompilerParams(vmem_limit_bytes=56 * 1024 * 1024),
         name="weight_work",
-    )(place, *[array for slot in slots for array in slot], *before)
+    )(place, *shares)
+    return (keep_gu, keep_d), (give_gu, give_d)
 
 
 def body(tokens, out_grad, gate_prob, expert_ids, w_gate, w_up, w_down):
@@ -292,8 +270,10 @@
 
     gate_local, up_local, down_local = w_gate[0], w_up[0], w_down[0]
     others = range(1, expert_count)
-    far_x = [send_xor(pack_x(j, j + 1), "expert", j) for j in others]
-    near_x = pack_x(0, 1)
+    far_x = [pack_x(j, j + 1) for j in others]
+    near_x = after(pack_x(0, 1), *far_x)
+    out_grad = after(out_grad, near_x)
+    far_x = [send_xor(far_x[j - 1], "expert", j) for j in others]
     far_dy = [send_xor(pack_dy(j, j + 1), "expert", j) for j in others]
     near_dy = pack_dy(0, 1)
     far_x = far_x[0] if len(far_x) == 1 else jnp.concatenate(far_x, axis=0)
@@ -303,16 +283,15 @@
     dp_index = lax.axis_index("dp")
     place = jnp.stack([dp_index // 2, dp_index % 2]).astype(jnp.int32)
     width = gate_local.shape[1]
-    token_parts, shares = [], []
+    token_parts, shares, sums = [], [], []
 
     def work(x_rows, dy_rows):
-        part, far_share, near_share, own_share = slot_work(
+        part, far_share, own_share = slot_work(
             place, x_rows, dy_rows, gate_local, up_local, down_local
         )
         token_parts.append(part)
-        near = send_xor(near_share, "dp", 1)
-        far = send_xor(far_share, "dp", 2)
-        shares.append([own_share, near, far, send_xor(far, "dp", 1)])
+        far = send_xor(after(far_share, shares[-1][1]) if shares else far_share, "dp", 2)
+        shares.append([own_share, far])
         return part
 
     if seq_count == 4:
@@ -322,55 +301,51 @@
         first_far = send_xor(far_x, "seq", 1)
         across_far = lax.ppermute(far_x, "seq", MIDDLE)
         dy_first = send_xor(slot_dy[0], "seq", 1)
-        dy_across = lax.ppermute(slot_dy[0], "seq", MIDDLE)
+        dy_across = lax.ppermute(after(slot_dy[0], across_far), "seq", MIDDLE)
         x_first = joined(first_near, [first_far])
         x_across = joined(across_near, [across_far])
-        done = work(after(slot_x[0], x_first), slot_dy[0])
+        done = work(after(slot_x[0], x_first, x_across), slot_dy[0])
         x_relayed = lax.ppermute(after(x_first, x_across), "seq", MIDDLE)
         x_near = lax.ppermute(after(x_across, x_first), "seq", OUTWARD)
         dy_relayed = lax.ppermute(after(dy_first, dy_across, done), "seq", MIDDLE)
         dy_near = lax.ppermute(after(dy_across, dy_first, done), "seq", OUTWARD)
-        done = work(after(x_first, x_relayed, shares[0][2]), dy_first)
-        x_far = lax.ppermute(after(x_relayed, x_near), "seq", OUTWARD)
+        done = work(x_first, dy_first)
+        x_far = lax.ppermute(after(x_relayed, x_near, done), "seq", OUTWARD)
+        dy_far = lax.ppermute(after(dy_relayed, dy_near), "seq", OUTWARD)
         work(
             jnp.where(inner, x_relayed, x_near),
             jnp.where(inner, dy_relayed, dy_near),
         )
-        dy_far = lax.ppermute(after(dy_relayed, dy_near, done), "seq", OUTWARD)
-        over = lax.ppermute(token_parts[2], "seq", MIDDLE)
-        two_away = lax.ppermute(token_parts[2], "seq", INWARD_TWO)
-        onward = (token_parts[1].astype(F32) + over.astype(F32)).astype(BF)
-        one_away = send_xor(onward, "seq", 1)
+        sent = after(token_parts[2], shares[1][1], x_far)
+        over = lax.ppermute(sent, "seq", MIDDLE)
+        into = lax.ppermute(sent, "seq", INWARD)
         work(
-            jnp.where(inner, x_across, after(x_far, onward, shares[1][2])),
+            jnp.where(inner, x_across, after(x_far, shares[2][1])),
             jnp.where(inner, dy_across, dy_far),
         )
-        so_far = weight_work(place, width, shares[:2], [], F32)
-        early = [token_parts[0], two_away, after(one_away, so_far[0])]
+        onward = after(token_parts[1], token_parts[3]).astype(F32) + over.astype(F32)
+        token_parts[3] = (token_parts[3].astype(F32) + into.astype(F32)).astype(BF)
+        returned = [(token_parts[0], 0), (onward.astype(BF), 1), (token_parts[3], 3)]
     else:
         work(slot_x[0], slot_dy[0])
         for j in range(1, seq_count):
             work(send_xor(slot_x[0], "seq", j), send_xor(slot_dy[0], "seq", j))
-        so_far = weight_work(place, width, shares[:2], [], F32)
-        early = [token_parts[0]]
-        early += [send_xor(token_parts[j], "seq", j) for j in range(1, seq_count - 1)]
-    for j in range(2, seq_count - 2, 2):
-        so_far = weight_work(place, width, shares[j : j + 2], so_far, F32)
-    gate_w_grad, up_w_grad, down_w_grad = weight_work(place, width, shares[-2:], so_far, BF)
-    last = seq_count - 1
-    early = sum(part.astype(F32) for part in early)
-
-    def rows_of(array, k):
-        return array[k * capacity : (k + 1) * capacity]
-
+        returned = [(token_parts[j], j) for j in range(seq_count)]
+    kept, given = weight_work(place, width, shares[0] + shares[1])
+    sums += [kept, [send_xor(part, "dp", 1) for part in given]]
     homes = []
     for k in range(expert_count):
-        direct = send_home(rows_of(token_parts[last], k), k, last)
-        first = rows_of(early, k)
-        if k:
-            first = send_xor(first.astype(BF), "expert", k).astype(F32)
-        homes.append((first + direct.astype(F32)).astype(BF))
+        rows = slice(k * capacity, (k + 1) * capacity)
+        parts = [send_home(part[rows], k, j) for part, j in returned]
+        homes.append(sum(part.astype(F32) for part in parts).astype(BF))
     home_x = jnp.concatenate(homes, axis=0)
+
+    for j in range(2, seq_count, 2):
+        kept, given = weight_work(place, width, shares[j] + shares[j + 1])
+        sums += [kept, [send_xor(part, "dp", 1) for part in given]]
+    gate_up = sum(pair[0].astype(F32) for pair in sums).astype(BF)
+    down_w_grad = sum(pair[1].astype(F32) for pair in sums).astype(BF)
+    gate_w_grad, up_w_grad = gate_up[:, :width], gate_up[:, width:]
 
     placer = placer_of(0, expert_count)
     placer = placer.astype(BF)

time: 275 us -> 251 us (0.913)
  waiting for transfers between devices: 140 us -> 112 us
  other arithmetic: 19.4 us -> 22.9 us
  starting transfers between devices: 49.1 us -> 46.3 us
    ppermute x20 -> x16, waiting for transfers between devices: 85.3 us -> 46.1 us  [send_xor(): return lax.ppermute(value, axis, [(i, i ^ mask) for i in range(size)])]
    ppermute x1 -> x2, waiting for transfers between devices: 0.01 us -> 12.1 us  [send_home(): lax.ppermute(value, ('expert', 'seq'), [(i, i ^ mask) for i in range(tota...]
    ppermute x1, waiting for transfers between devices: 17.6 us -> 10.3 us  [body(): x_relayed = lax.ppermute(after(x_first, x_across), 'seq', MIDDLE)]
    ppermute x1, waiting for transfers between devices: 8.32 us -> 13.8 us  [body(): dy_relayed = lax.ppermute(after(dy_first, dy_across, done), 'seq', MIDDLE)]
    ppermute x1, waiting for transfers between devices: 0.01 us -> 4 us  [body(): across_far = lax.ppermute(far_x, 'seq', MIDDLE)]
    convert_element_type x3 -> x5, other arithmetic: 1.65 us -> 5.57 us  [the longest x2 2.6 us: body(): homes.append(sum((part.astype(F32) for part in parts)).astype(BF))]
    ppermute x5, waiting for transfers between devices: 28.3 us -> 24.7 us  [the longest x1 13.6 us: body(): dy_far = lax.ppermute(after(dy_relayed, dy_near), 'seq', OUTWARD)]
    ppermute x20 -> x16, starting transfers between devices: 14.4 us -> 12.4 us  [send_xor(): return lax.ppermute(value, axis, [(i, i ^ mask) for i in range(size)])]
  transfers between devices with their start and end apart: 32 -> 29, of which waited for: 15 -> 15; matrix products, arithmetic and copies ran while one was open for 9% -> 10% of each run, Pallas kernels for 16% -> 18%
where the time goes in v3:
time: 251 us; the launch traced here: 250 us
  waiting for transfers between devices  112 us (45%)
  Pallas kernels  54.4 us (22%)
  starting transfers between devices  46.3 us (18%)
  other arithmetic  22.9 us (9%)
  local copies, waits for them, and re-layouts  6.65 us (3%)
  matrix products  6.09 us (2%)
    ppermute x16, waiting for transfers between devices, send_xor(): return lax.ppermute(value, axis, [(i, i ^ mask) for i in range(size)])  46.1 us
    pallas_call x4, Pallas kernels, slot_work(): pl.pallas_call(functools.partial(slot_kernel, blocks), out_shape=[jax.Sha...  35.8 us
    pallas_call x2, Pallas kernels, weight_work(): pl.pallas_call(functools.partial(weight_kernel, count, width), out_shape=...  18.6 us
    ppermute x1, waiting for transfers between devices, body(): dy_relayed = lax.ppermute(after(dy_first, dy_across, done), 'seq', MIDDLE)  13.8 us
    ppermute x1, waiting for transfers between devices, body(): dy_far = lax.ppermute(after(dy_relayed, dy_near), 'seq', OUTWARD)  13.6 us
    ppermute x16, starting transfers between devices, send_xor(): return lax.ppermute(value, axis, [(i, i ^ mask) for i in range(size)])  12.4 us
    ppermute x2, waiting for transfers between devices, send_home(): lax.ppermute(value, ('expert', 'seq'), [(i, i ^ mask) for i in range(tota...  12.1 us
    ppermute x1, waiting for transfers between devices, body(): x_relayed = lax.ppermute(after(x_first, x_across), 'seq', MIDDLE)  10.3 us
  transfers between devices with their start and end apart: 29, of which 15 were waited for; matrix products, arithmetic and copies ran while one was open for 10% of the time, Pallas kernels for 18%

profile of v3, /device:TPU:8, one launch (start us, length us, event | category | flops | bytes accessed | tf_op | source)
XLA Modules:
  0.0 249.7 jit_solution(16366097860078920380)
XLA Ops:
  0.7 0.9 fusion.2
  1.6 0.7 convert_add_fusion
  2.6 1.2 convolution_convert_fusion.3
  3.8 3.5 %collective-permute-start.3 = (bf16[68,4096]{1,0:T(8,128)(2,1)S(1)}, bf16[68,4096]{1,0:T(8,128)(2,1)S(1)}, u32[]{:S(2)}, u32[]{:S(2)}) collective-permute-start(bf16[68,4096]{1,0:T(8,128)(2,1)S(1)} %convolution_convert_fusion.4), channel_id=1, source_target_pairs={{1,2},{2,1},{5,6},{6,5},{9,10},{10,9},{13,14},{14,13},{17,18},{18,... | collective-permute-start | bytes 1671176 | tf_op jit(solution)/shard_map/ppermute | solution.py:300
  7.3 1.6 collective-permute-start
  8.9 1.2 convolution_convert_fusion.1
  10.9 0.6 pad_add_fusion.place.refs_0_
  11.6 12.4 %collective-permute-done = bf16[68,4096]{1,0:T(8,128)(2,1)} collective-permute-done((bf16[68,4096]{1,0:T(8,128)(2,1)}, bf16[68,4096]{1,0:T(8,128)(2,1)}, u32[]{:S(2)}, u32[]{:S(2)}) %collective-permute-start) | collective-permute-done | bytes 557088 | tf_op jit(solution)/shard_map/ppermute | solution.py:31
  24.0 2.0 collective-permute-start.2
  25.9 2.3 pad_maximum_fusion.x
  28.2 2.3 collective-permute-start.4
  30.6 4.5 %collective-permute-done.5 = bf16[68,4096]{1,0:T(8,128)(2,1)S(1)} collective-permute-done((bf16[68,4096]{1,0:T(8,128)(2,1)}, bf16[68,4096]{1,0:T(8,128)(2,1)S(1)}, u32[]{:S(2)}, u32[]{:S(2)}) %collective-permute-start.5) | collective-permute-done | bytes 557088 | tf_op jit(solution)/shard_map/ppermute | solution.py:31
  35.0 1.2 pad_maximum_fusion.3.dy
  36.6 1.2 pad_maximum_fusion.1.x
  37.8 4.0 %collective-permute-done.4 = bf16[68,4096]{1,0:T(8,128)(2,1)S(1)} collective-permute-done((bf16[68,4096]{1,0:T(8,128)(2,1)}, bf16[68,4096]{1,0:T(8,128)(2,1)S(1)}, u32[]{:S(2)}, u32[]{:S(2)}) %collective-permute-start.4) | collective-permute-done | bytes 557088 | tf_op jit(solution)/shard_map/ppermute | solution.py:302
  41.8 1.2 pad_maximum_fusion.2
  43.1 9.1 %slot_work.4 = (bf16[136,4224]{1,0:T(8,128)(2,1)}, bf16[144,5248]{1,0:T(8,128)(2,1)}, bf16[144,5248]{1,0:T(8,128)(2,1)}) custom-call(s32[2]{0:T(128)} %pad_add_fusion.place.refs_0_, bf16[136,4096]{1,0:T(8,128)(2,1)} %pad_maximum_fusion.x, bf16[136,4096]{1,0:T(8,128)(2,1)} %pad_maximum_fusion.3.dy, bf16[4096,384]{1,0:T(8,128)(2,1)} %bitcast.23, ...), custom_call_target="tpu_custom_call" | custom-call | tf_op jit(solution)/shard_map/slot_work/pallas_call | solution.py:153
  52.1 1.6 collective-permute-start.13
  53.7 2.4 collective-permute-start.10
  56.1 3.5 %collective-permute-start.7 = (bf16[136,4096]{1,0:T(8,128)(2,1)S(1)}, bf16[136,4096]{1,0:T(8,128)(2,1)}, u32[]{:S(2)}, u32[]{:S(2)}) collective-permute-start(bf16[136,4096]{1,0:T(8,128)(2,1)S(1)} %pad_maximum_fusion.1.x), channel_id=1, source_target_pairs={{1,2},{2,1},{5,6},{6,5},{9,10},{10,9},{13,14},{14,13},{17,18},{18,... | collective-permute-start | bytes 3342344 | tf_op jit(solution)/shard_map/ppermute | solution.py:308
  59.6 2.4 collective-permute-start.8
  62.0 16.8 %collective-permute-done.6.dy = bf16[136,4096]{1,0:T(8,128)(2,1)} collective-permute-done((bf16[136,4096]{1,0:T(8,128)(2,1)S(1)}, bf16[136,4096]{1,0:T(8,128)(2,1)}, u32[]{:S(2)}, u32[]{:S(2)}) %collective-permute-start.6) | collective-permute-done | bytes 1114144 | tf_op jit(solution)/shard_map/ppermute | solution.py:31
  78.7 4.5 %collective-permute-done.10 = bf16[136,4096]{1,0:T(8,128)(2,1)} collective-permute-done((bf16[136,4096]{1,0:T(8,128)(2,1)S(1)}, bf16[136,4096]{1,0:T(8,128)(2,1)}, u32[]{:S(2)}, u32[]{:S(2)}) %collective-permute-start.10) | collective-permute-done | bytes 1114144 | tf_op jit(solution)/shard_map/ppermute | solution.py:304
  83.2 2.4 collective-permute-start.11
  85.6 2.3 collective-permute-start.12
  87.9 8.9 %slot_work.5 = (bf16[136,4224]{1,0:T(8,128)(2,1)}, bf16[144,5248]{1,0:T(8,128)(2,1)}, bf16[144,5248]{1,0:T(8,128)(2,1)}) custom-call(s32[2]{0:T(128)} %pad_add_fusion.place.refs_0_, bf16[136,4096]{1,0:T(8,128)(2,1)} %copy-done.2, bf16[136,4096]{1,0:T(8,128)(2,1)} %collective-permute-done.6.dy, bf16[4096,384]{1,0:T(8,128)(2,1)} %bitcast.24, ...), custom_call_target="tpu_custom_call" | custom-call | tf_op jit(solution)/shard_map/slot_work/pallas_call | solution.py:153
  96.8 10.3 %collective-permute-done.7 = bf16[136,4096]{1,0:T(8,128)(2,1)} collective-permute-done((bf16[136,4096]{1,0:T(8,128)(2,1)S(1)}, bf16[136,4096]{1,0:T(8,128)(2,1)}, u32[]{:S(2)}, u32[]{:S(2)}) %collective-permute-start.7) | collective-permute-done | bytes 1114144 | tf_op jit(solution)/shard_map/ppermute | solution.py:308
  107.1 1.3 collective-permute-start.9
  109.0 2.4 broadcast_select_fusion.3.x
  111.4 13.8 %collective-permute-done.11 = bf16[136,4096]{1,0:T(8,128)(2,1)} collective-permute-done((bf16[136,4096]{1,0:T(8,128)(2,1)}, bf16[136,4096]{1,0:T(8,128)(2,1)}, u32[]{:S(2)}, u32[]{:S(2)}) %collective-permute-start.11) | collective-permute-done | bytes 1114144 | tf_op jit(solution)/shard_map/ppermute | solution.py:310
  125.2 1.4 collective-permute-done.12
  126.6 5.4 %collective-permute-start.16 = (bf16[136,4096]{1,0:T(8,128)(2,1)}, bf16[136,4096]{1,0:T(8,128)(2,1)}, u32[]{:S(2)}, u32[]{:S(2)}) collective-permute-start(bf16[136,4096]{1,0:T(8,128)(2,1)} %collective-permute-done.11), channel_id=1, source_target_pairs={{1,0},{2,3},{5,4},{6,7},{9,8},{10,11},{13,12},{14,15},{17,16},{18,... | collective-permute-start | bytes 3342344 | tf_op jit(solution)/shard_map/ppermute | solution.py:314
  132.0 2.4 broadcast_select_fusion.2.dy
  134.4 8.9 %slot_work.6 = (bf16[136,4224]{1,0:T(8,128)(2,1)}, bf16[144,5248]{1,0:T(8,128)(2,1)}, bf16[144,5248]{1,0:T(8,128)(2,1)}) custom-call(s32[2]{0:T(128)} %pad_add_fusion.place.refs_0_, bf16[136,4096]{1,0:T(8,128)(2,1)} %broadcast_select_fusion.3.x, bf16[136,4096]{1,0:T(8,128)(2,1)} %broadcast_select_fusion.2.dy, bf16[4096,384]{1,0:T(8,128)(2,1)} %bitcast.25, ...), custom_call_target="tpu_custom_call" | custom-call | tf_op jit(solution)/shard_map/slot_work/pallas_call | solution.py:153
  143.9 6.6 %collective-permute-done.9 = bf16[136,4096]{1,0:T(8,128)(2,1)S(1)} collective-permute-done((bf16[136,4096]{1,0:T(8,128)(2,1)}, bf16[136,4096]{1,0:T(8,128)(2,1)S(1)}, u32[]{:S(2)}, u32[]{:S(2)}) %collective-permute-start.9) | collective-permute-done | bytes 1114144 | tf_op jit(solution)/shard_map/ppermute | solution.py:313
  150.5 1.0 copy-done.12
  151.5 1.3 collective-permute-start.19
  152.8 2.5 collective-permute-start.17
  155.3 13.6 %collective-permute-done.16 = bf16[136,4096]{1,0:T(8,128)(2,1)} collective-permute-done((bf16[136,4096]{1,0:T(8,128)(2,1)}, bf16[136,4096]{1,0:T(8,128)(2,1)}, u32[]{:S(2)}, u32[]{:S(2)}) %collective-permute-start.16) | collective-permute-done | bytes 1114144 | tf_op jit(solution)/shard_map/ppermute | solution.py:314
  168.9 2.4 broadcast_select_fusion.dy
  171.2 1.5 broadcast_select_fusion.1.x
  172.7 8.9 %slot_work.7 = (bf16[136,4224]{1,0:T(8,128)(2,1)}, bf16[144,5248]{1,0:T(8,128)(2,1)}, bf16[144,5248]{1,0:T(8,128)(2,1)}) custom-call(s32[2]{0:T(128)} %pad_add_fusion.place.refs_0_, bf16[136,4096]{1,0:T(8,128)(2,1)} %broadcast_select_fusion.1.x, bf16[136,4096]{1,0:T(8,128)(2,1)} %broadcast_select_fusion.dy, bf16[4096,384]{1,0:T(8,128)(2,1)} %bitcast.26, ...), custom_call_target="tpu_custom_call" | custom-call | tf_op jit(solution)/shard_map/slot_work/pallas_call | solution.py:153
  181.6 1.9 add_convert_fusion.1
  185.1 0.9 fusion.29
  186.0 2.8 %collective-permute-start.18 = (bf16[68,4224]{1,0:T(8,128)(2,1)}, bf16[68,4224]{1,0:T(8,128)(2,1)}, u32[]{:S(2)}, u32[]{:S(2)}) collective-permute-start(bf16[68,4224]{1,0:T(8,128)(2,1)} %get-tuple-element.80), channel_id=1, source_target_pairs={{0,1},{1,0},{2,3},{3,2},{4,5},{5,4},{6,7},{7,6},{8,9},{9,8},{10,11... | collective-permute-start | bytes 1723400 | tf_op jit(solution)/shard_map/ppermute | solution.py:31
  189.3 1.0 slice.36
  190.3 1.5 collective-permute-start.21
  191.8 9.2 %weight_work.2 = (bf16[1024,768]{1,0:T(8,128)(2,1)}, bf16[1024,768]{1,0:T(8,128)(2,1)}, bf16[384,1024]{1,0:T(8,128)(2,1)}, bf16[384,1024]{1,0:T(8,128)(2,1)}) custom-call(s32[2]{0:T(128)} %pad_add_fusion.place.refs_0_, bf16[144,5248]{1,0:T(8,128)(2,1)} %get-tuple-element.63.refs_1_, bf16[144,5248]{1,0:T(8,128)(2,1)} %collective-permute-done.13.refs_2_, ...), custom_call_target="tpu_custom_call" | custom-call | tf_op jit(solution)/shard_map/weight_work/pallas_call | solution.py:224
  201.1 9.9 %collective-permute-done.20 = bf16[68,4224]{1,0:T(8,128)(2,1)S(1)} collective-permute-done((bf16[68,4224]{1,0:T(8,128)(2,1)S(1)}, bf16[68,4224]{1,0:T(8,128)(2,1)S(1)}, u32[]{:S(2)}, u32[]{:S(2)}) %collective-permute-start.20) | collective-permute-done | bytes 574496 | tf_op jit(solution)/shard_map/ppermute | solution.py:31
  211.0 1.1 collective-permute-start.23
  212.2 2.1 collective-permute-done.18
  214.3 3.6 %collective-permute-start.22 = (bf16[68,4224]{1,0:T(8,128)(2,1)S(1)}, bf16[68,4224]{1,0:T(8,128)(2,1)}, u32[]{:S(2)}, u32[]{:S(2)}) collective-permute-start(bf16[68,4224]{1,0:T(8,128)(2,1)S(1)} %get-tuple-element.79), channel_id=1, source_target_pairs={{0,5},{1,4},{2,7},{3,6},{4,1},{5,0},{6,3},{7,2},{8,13},{9,12},{10,... | collective-permute-start | bytes 1723400 | tf_op jit(solution)/shard_map/ppermute | solution.py:42
  217.9 1.3 add_convert_fusion.5
  219.3 1.0 copy-done.9
  220.3 9.4 %weight_work.3 = (bf16[1024,768]{1,0:T(8,128)(2,1)}, bf16[1024,768]{1,0:T(8,128)(2,1)}, bf16[384,1024]{1,0:T(8,128)(2,1)}, bf16[384,1024]{1,0:T(8,128)(2,1)}) custom-call(s32[2]{0:T(128)} %pad_add_fusion.place.refs_0_, bf16[144,5248]{1,0:T(8,128)(2,1)} %get-tuple-element.67.refs_1_, bf16[144,5248]{1,0:T(8,128)(2,1)} %copy-done.7, ...), custom_call_target="tpu_custom_call" | custom-call | tf_op jit(solution)/shard_map/weight_work/pallas_call | solution.py:224
  229.8 9.6 %collective-permute-done.23 = bf16[68,4224]{1,0:T(8,128)(2,1)S(1)} collective-permute-done((bf16[68,4224]{1,0:T(8,128)(2,1)S(1)}, bf16[68,4224]{1,0:T(8,128)(2,1)S(1)}, u32[]{:S(2)}, u32[]{:S(2)}) %collective-permute-start.23) | collective-permute-done | bytes 574496 | tf_op jit(solution)/shard_map/ppermute | solution.py:42
  239.5 2.4 collective-permute-done.22
  241.9 1.3 add_convert_fusion.4
  243.2 0.7 fusion.4
  243.9 1.5 convolution_convert_fusion
  245.4 1.5 fusion.5
  247.0 0.6 copy-done.6
  247.6 0.8 add_convert_fusion
  248.4 1.3 slice_bitcast_fusion
  (62 shorter events, 5.1 us)
Async XLA Ops:
  0.6 1.6 copy-start
  2.6 6.4 %copy-start.4 = (bf16[128,4096]{1,0:T(8,128)(2,1)S(1)}, bf16[128,4096]{1,0:T(8,128)(2,1)}, u32[]{:S(2)}) copy-start(bf16[128,4096]{1,0:T(8,128)(2,1)} %param.8) | copy-start | bytes 3145732
  2.6 6.3 %copy-start.16 = (bf16[128]{0:T(256)(128)(2,1)S(1)}, bf16[128]{0:T(256)(128)(2,1)}, u32[]{:S(2)}) copy-start(bf16[128]{0:T(256)(128)(2,1)} %param.9) | copy-start | bytes 772
  3.8 34.1 %collective-permute-start.3 = (bf16[68,4096]{1,0:T(8,128)(2,1)S(1)}, bf16[68,4096]{1,0:T(8,128)(2,1)S(1)}, u32[]{:S(2)}, u32[]{:S(2)}) collective-permute-start(bf16[68,4096]{1,0:T(8,128)(2,1)S(1)} %convolution_convert_fusion.4), channel_id=1, source_target_pairs={{1,2},{2,1},{5,6},{6,5},{9,10},{10,9},{13,14},{14,13},{17,18},{18,... | collective-permute-start | bytes 1671176 | tf_op jit(solution)/shard_map/ppermute | solution.py:300
  7.3 29.0 %collective-permute-start.1 = (bf16[68,4096]{1,0:T(8,128)(2,1)S(1)}, bf16[68,4096]{1,0:T(8,128)(2,1)}, u32[]{:S(2)}, u32[]{:S(2)}) collective-permute-start(bf16[68,4096]{1,0:T(8,128)(2,1)S(1)} %convolution_convert_fusion.4), channel_id=1, source_target_pairs={{0,1},{1,0},{2,3},{3,2},{4,5},{5,4},{6,7},{7,6},{8,9},{9,8},{10,11... | collective-permute-start | bytes 1671176 | tf_op jit(solution)/shard_map/ppermute | solution.py:31
  7.3 16.6 %collective-permute-start = (bf16[68,4096]{1,0:T(8,128)(2,1)}, bf16[68,4096]{1,0:T(8,128)(2,1)}, u32[]{:S(2)}, u32[]{:S(2)}) collective-permute-start(bf16[68,4096]{1,0:T(8,128)(2,1)} %convolution_convert_fusion.3), channel_id=1, source_target_pairs={{0,4},{4,0},{1,5},{5,1},{2,6},{6,2},{3,7},{7,3},{8,12},{12,8},{9,1... | collective-permute-start | bytes 1671176 | tf_op jit(solution)/shard_map/ppermute | solution.py:31
  10.1 24.9 %collective-permute-start.5 = (bf16[68,4096]{1,0:T(8,128)(2,1)}, bf16[68,4096]{1,0:T(8,128)(2,1)S(1)}, u32[]{:S(2)}, u32[]{:S(2)}) collective-permute-start(bf16[68,4096]{1,0:T(8,128)(2,1)} %convolution_convert_fusion.1), channel_id=1, source_target_pairs={{0,4},{4,0},{1,5},{5,1},{2,6},{6,2},{3,7},{7,3},{8,12},{12,8},{9,1... | collective-permute-start | bytes 1671176 | tf_op jit(solution)/shard_map/ppermute | solution.py:31
  24.0 12.6 %collective-permute-start.2 = (bf16[68,4096]{1,0:T(8,128)(2,1)}, bf16[68,4096]{1,0:T(8,128)(2,1)S(1)}, u32[]{:S(2)}, u32[]{:S(2)}) collective-permute-start(bf16[68,4096]{1,0:T(8,128)(2,1)} %collective-permute-done), channel_id=1, source_target_pairs={{0,1},{1,0},{2,3},{3,2},{4,5},{5,4},{6,7},{7,6},{8,9},{9,8},{10,11... | collective-permute-start | bytes 1671176 | tf_op jit(solution)/shard_map/ppermute | solution.py:31
  28.2 13.6 %collective-permute-start.4 = (bf16[68,4096]{1,0:T(8,128)(2,1)}, bf16[68,4096]{1,0:T(8,128)(2,1)S(1)}, u32[]{:S(2)}, u32[]{:S(2)}) collective-permute-start(bf16[68,4096]{1,0:T(8,128)(2,1)} %collective-permute-done), channel_id=1, source_target_pairs={{1,2},{2,1},{5,6},{6,5},{9,10},{10,9},{13,14},{14,13},{17,18},{18,... | collective-permute-start | bytes 1671176 | tf_op jit(solution)/shard_map/ppermute | solution.py:302
  37.8 18.3 %copy-start.2 = (bf16[136,4096]{1,0:T(8,128)(2,1)}, bf16[136,4096]{1,0:T(8,128)(2,1)S(1)}, u32[]{:S(2)}) copy-start(bf16[136,4096]{1,0:T(8,128)(2,1)S(1)} %pad_maximum_fusion.1.x) | copy-start | bytes 3342340
  43.1 10.6 %copy-start.3 = (bf16[136,4096]{1,0:T(8,128)(2,1)S(1)}, bf16[136,4096]{1,0:T(8,128)(2,1)}, u32[]{:S(2)}) copy-start(bf16[136,4096]{1,0:T(8,128)(2,1)} %pad_maximum_fusion.3.dy) | copy-start | bytes 3342340
  52.1 56.3 %collective-permute-start.13 = (bf16[144,5248]{1,0:T(8,128)(2,1)}, bf16[144,5248]{1,0:T(8,128)(2,1)}, u32[]{:S(2)}, u32[]{:S(2)}) collective-permute-start(bf16[144,5248]{1,0:T(8,128)(2,1)} %get-tuple-element.54), channel_id=1, source_target_pairs={{0,16},{8,24},{16,0},{24,8},{1,17},{9,25},{17,1},{25,9},{2,18},{10... | collective-permute-start | bytes 4534280 | tf_op jit(solution)/shard_map/ppermute | solution.py:31
  53.7 25.0 %collective-permute-start.6 = (bf16[136,4096]{1,0:T(8,128)(2,1)S(1)}, bf16[136,4096]{1,0:T(8,128)(2,1)}, u32[]{:S(2)}, u32[]{:S(2)}) collective-permute-start(bf16[136,4096]{1,0:T(8,128)(2,1)S(1)} %copy-done.3), channel_id=1, source_target_pairs={{0,1},{1,0},{2,3},{3,2},{4,5},{5,4},{6,7},{7,6},{8,9},{9,8},{10,11... | collective-permute-start | bytes 3342344 | tf_op jit(solution)/shard_map/ppermute | solution.py:31
  53.7 29.5 %collective-permute-start.10 = (bf16[136,4096]{1,0:T(8,128)(2,1)S(1)}, bf16[136,4096]{1,0:T(8,128)(2,1)}, u32[]{:S(2)}, u32[]{:S(2)}) collective-permute-start(bf16[136,4096]{1,0:T(8,128)(2,1)S(1)} %copy-done.3), channel_id=1, source_target_pairs={{1,2},{2,1},{5,6},{6,5},{9,10},{10,9},{13,14},{14,13},{17,18},{18,... | collective-permute-start | bytes 3342344 | tf_op jit(solution)/shard_map/ppermute | solution.py:304
  56.1 51.0 %collective-permute-start.7 = (bf16[136,4096]{1,0:T(8,128)(2,1)S(1)}, bf16[136,4096]{1,0:T(8,128)(2,1)}, u32[]{:S(2)}, u32[]{:S(2)}) collective-permute-start(bf16[136,4096]{1,0:T(8,128)(2,1)S(1)} %pad_maximum_fusion.1.x), channel_id=1, source_target_pairs={{1,2},{2,1},{5,6},{6,5},{9,10},{10,9},{13,14},{14,13},{17,18},{18,... | collective-permute-start | bytes 3342344 | tf_op jit(solution)/shard_map/ppermute | solution.py:308
  59.6 47.5 %collective-permute-start.8 = (bf16[136,4096]{1,0:T(8,128)(2,1)}, bf16[136,4096]{1,0:T(8,128)(2,1)}, u32[]{:S(2)}, u32[]{:S(2)}) collective-permute-start(bf16[136,4096]{1,0:T(8,128)(2,1)} %pad_maximum_fusion.2), channel_id=1, source_target_pairs={{1,0},{2,3},{5,4},{6,7},{9,8},{10,11},{13,12},{14,15},{17,16},{18,... | collective-permute-start | bytes 3342344 | tf_op jit(solution)/shard_map/ppermute | solution.py:309
  83.2 42.0 %collective-permute-start.11 = (bf16[136,4096]{1,0:T(8,128)(2,1)}, bf16[136,4096]{1,0:T(8,128)(2,1)}, u32[]{:S(2)}, u32[]{:S(2)}) collective-permute-start(bf16[136,4096]{1,0:T(8,128)(2,1)} %collective-permute-done.6.dy), channel_id=1, source_target_pairs={{1,2},{2,1},{5,6},{6,5},{9,10},{10,9},{13,14},{14,13},{17,18},{18,... | collective-permute-start | bytes 3342344 | tf_op jit(solution)/shard_map/ppermute | solution.py:310
  85.6 41.0 %collective-permute-start.12 = (bf16[136,4096]{1,0:T(8,128)(2,1)}, bf16[136,4096]{1,0:T(8,128)(2,1)}, u32[]{:S(2)}, u32[]{:S(2)}) collective-permute-start(bf16[136,4096]{1,0:T(8,128)(2,1)} %collective-permute-done.10), channel_id=1, source_target_pairs={{1,0},{2,3},{5,4},{6,7},{9,8},{10,11},{13,12},{14,15},{17,16},{18,... | collective-permute-start | bytes 3342344 | tf_op jit(solution)/shard_map/ppermute | solution.py:311
  107.1 43.4 %collective-permute-start.9 = (bf16[136,4096]{1,0:T(8,128)(2,1)}, bf16[136,4096]{1,0:T(8,128)(2,1)S(1)}, u32[]{:S(2)}, u32[]{:S(2)}) collective-permute-start(bf16[136,4096]{1,0:T(8,128)(2,1)} %collective-permute-done.7), channel_id=1, source_target_pairs={{1,0},{2,3},{5,4},{6,7},{9,8},{10,11},{13,12},{14,15},{17,16},{18,... | collective-permute-start | bytes 3342344 | tf_op jit(solution)/shard_map/ppermute | solution.py:313
  108.5 34.8 %collective-permute-start.14 = (bf16[144,5248]{1,0:T(8,128)(2,1)}, bf16[144,5248]{1,0:T(8,128)(2,1)S(1)}, u32[]{:S(2)}, u32[]{:S(2)}) collective-permute-start(bf16[144,5248]{1,0:T(8,128)(2,1)} %get-tuple-element.55), channel_id=1, source_target_pairs={{0,16},{8,24},{16,0},{24,8},{1,17},{9,25},{17,1},{25,9},{2,18},{10... | collective-permute-start | bytes 4534280 | tf_op jit(solution)/shard_map/ppermute | solution.py:31
  126.6 42.3 %collective-permute-start.16 = (bf16[136,4096]{1,0:T(8,128)(2,1)}, bf16[136,4096]{1,0:T(8,128)(2,1)}, u32[]{:S(2)}, u32[]{:S(2)}) collective-permute-start(bf16[136,4096]{1,0:T(8,128)(2,1)} %collective-permute-done.11), channel_id=1, source_target_pairs={{1,0},{2,3},{5,4},{6,7},{9,8},{10,11},{13,12},{14,15},{17,16},{18,... | collective-permute-start | bytes 3342344 | tf_op jit(solution)/shard_map/ppermute | solution.py:314
  143.3 27.9 %copy-start.8 = (bf16[144,5248]{1,0:T(8,128)(2,1)}, bf16[144,5248]{1,0:T(8,128)(2,1)S(1)}, u32[]{:S(2)}) copy-start(bf16[144,5248]{1,0:T(8,128)(2,1)S(1)} %collective-permute-done.14.refs_4_) | copy-start | bytes 4534276
  143.3 27.9 %collective-permute-start.15 = (bf16[144,5248]{1,0:T(8,128)(2,1)}, bf16[144,5248]{1,0:T(8,128)(2,1)S(1)}, u32[]{:S(2)}, u32[]{:S(2)}) collective-permute-start(bf16[144,5248]{1,0:T(8,128)(2,1)} %get-tuple-element.56), channel_id=1, source_target_pairs={{0,16},{8,24},{16,0},{24,8},{1,17},{9,25},{17,1},{25,9},{2,18},{10... | collective-permute-start | bytes 4534280 | tf_op jit(solution)/shard_map/ppermute | solution.py:31
  150.5 1.0 copy-start.12
  151.5 30.2 %collective-permute-start.19 = (bf16[136,4224]{1,0:T(8,128)(2,1)}, bf16[136,4224]{1,0:T(8,128)(2,1)}, u32[]{:S(2)}, u32[]{:S(2)}) collective-permute-start(bf16[136,4224]{1,0:T(8,128)(2,1)} %get-tuple-element.62), channel_id=1, source_target_pairs={{0,1},{3,2},{4,5},{7,6},{8,9},{11,10},{12,13},{15,14},{16,17},{19,... | collective-permute-start | bytes 3446792 | tf_op jit(solution)/shard_map/ppermute | solution.py:321
  152.8 18.5 %copy-start.13 = (bf16[136,4096]{1,0:T(8,128)(2,1)S(1)}, bf16[136,4096]{1,0:T(8,128)(2,1)}, u32[]{:S(2)}) copy-start(bf16[136,4096]{1,0:T(8,128)(2,1)} %copy-done.12) | copy-start | bytes 3342340
  152.8 31.4 %collective-permute-start.17 = (bf16[136,4224]{1,0:T(8,128)(2,1)}, bf16[136,4224]{1,0:T(8,128)(2,1)S(1)}, u32[]{:S(2)}, u32[]{:S(2)}) collective-permute-start(bf16[136,4224]{1,0:T(8,128)(2,1)} %get-tuple-element.62), channel_id=1, source_target_pairs={{1,2},{2,1},{5,6},{6,5},{9,10},{10,9},{13,14},{14,13},{17,18},{18,... | collective-permute-start | bytes 3446792 | tf_op jit(solution)/shard_map/ppermute | solution.py:320
  171.2 1.5 copy-start.7
  183.5 1.3 copy-start.11
  183.7 27.4 %collective-permute-start.20 = (bf16[68,4224]{1,0:T(8,128)(2,1)S(1)}, bf16[68,4224]{1,0:T(8,128)(2,1)S(1)}, u32[]{:S(2)}, u32[]{:S(2)}) collective-permute-start(bf16[68,4224]{1,0:T(8,128)(2,1)S(1)} %get-tuple-element.82), channel_id=1, source_target_pairs={{0,3},{1,2},{2,1},{3,0},{4,7},{5,6},{6,5},{7,4},{8,11},{9,10},{10,... | collective-permute-start | bytes 1723400 | tf_op jit(solution)/shard_map/ppermute | solution.py:31
  185.0 4.3 %copy-start.10 = (bf16[136,4224]{1,0:T(8,128)(2,1)S(1)}, bf16[136,4224]{1,0:T(8,128)(2,1)}, u32[]{:S(2)}) copy-start(bf16[136,4224]{1,0:T(8,128)(2,1)} %get-tuple-element.44) | copy-start | bytes 3446788
  186.0 28.2 %collective-permute-start.18 = (bf16[68,4224]{1,0:T(8,128)(2,1)}, bf16[68,4224]{1,0:T(8,128)(2,1)}, u32[]{:S(2)}, u32[]{:S(2)}) collective-permute-start(bf16[68,4224]{1,0:T(8,128)(2,1)} %get-tuple-element.80), channel_id=1, source_target_pairs={{0,1},{1,0},{2,3},{3,2},{4,5},{5,4},{6,7},{7,6},{8,9},{9,8},{10,11... | collective-permute-start | bytes 1723400 | tf_op jit(solution)/shard_map/ppermute | solution.py:31
  188.8 30.4 %collective-permute-start.25 = (bf16[144,5248]{1,0:T(8,128)(2,1)}, bf16[144,5248]{1,0:T(8,128)(2,1)S(1)}, u32[]{:S(2)}, u32[]{:S(2)}) collective-permute-start(bf16[144,5248]{1,0:T(8,128)(2,1)} %get-tuple-element.70), channel_id=1, source_target_pairs={{0,16},{8,24},{16,0},{24,8},{1,17},{9,25},{17,1},{25,9},{2,18},{10... | collective-permute-start | bytes 4534280 | tf_op jit(solution)/shard_map/ppermute | solution.py:31
  190.3 39.4 %collective-permute-start.21 = (bf16[68,4224]{1,0:T(8,128)(2,1)}, bf16[68,4224]{1,0:T(8,128)(2,1)S(1)}, u32[]{:S(2)}, u32[]{:S(2)}) collective-permute-start(bf16[68,4224]{1,0:T(8,128)(2,1)} %slice.36), channel_id=1, source_target_pairs={{0,4},{4,0},{1,5},{5,1},{2,6},{6,2},{3,7},{7,3},{8,12},{12,8},{9,1... | collective-permute-start | bytes 1723400 | tf_op jit(solution)/shard_map/ppermute | solution.py:31
  201.0 44.4 %collective-permute-start.27 = (bf16[384,1024]{1,0:T(8,128)(2,1)}, bf16[384,1024]{1,0:T(8,128)(2,1)S(1)}, u32[]{:S(2)}, u32[]{:S(2)}) collective-permute-start(bf16[384,1024]{1,0:T(8,128)(2,1)} %get-tuple-element.74), channel_id=1, source_target_pairs={{0,8},{8,0},{16,24},{24,16},{1,9},{9,1},{17,25},{25,17},{2,10},{10... | collective-permute-start | bytes 2359304 | tf_op jit(solution)/shard_map/ppermute | solution.py:31
  211.0 28.4 %collective-permute-start.23 = (bf16[68,4224]{1,0:T(8,128)(2,1)S(1)}, bf16[68,4224]{1,0:T(8,128)(2,1)S(1)}, u32[]{:S(2)}, u32[]{:S(2)}) collective-permute-start(bf16[68,4224]{1,0:T(8,128)(2,1)S(1)} %get-tuple-element.81), channel_id=1, source_target_pairs={{0,7},{1,6},{2,5},{3,4},{4,3},{5,2},{6,1},{7,0},{8,15},{9,14},{10,... | collective-permute-start | bytes 1723400 | tf_op jit(solution)/shard_map/ppermute | solution.py:42
  214.3 27.6 %collective-permute-start.22 = (bf16[68,4224]{1,0:T(8,128)(2,1)S(1)}, bf16[68,4224]{1,0:T(8,128)(2,1)}, u32[]{:S(2)}, u32[]{:S(2)}) collective-permute-start(bf16[68,4224]{1,0:T(8,128)(2,1)S(1)} %get-tuple-element.79), channel_id=1, source_target_pairs={{0,5},{1,4},{2,7},{3,6},{4,1},{5,0},{6,3},{7,2},{8,13},{9,12},{10,... | collective-permute-start | bytes 1723400 | tf_op jit(solution)/shard_map/ppermute | solution.py:42
  219.2 1.1 copy-start.9
  219.2 27.8 %collective-permute-start.24 = (bf16[1024,768]{1,0:T(8,128)(2,1)}, bf16[1024,768]{1,0:T(8,128)(2,1)S(1)}, u32[]{:S(2)}, u32[]{:S(2)}) collective-permute-start(bf16[1024,768]{1,0:T(8,128)(2,1)} %get-tuple-element.66), channel_id=1, source_target_pairs={{0,8},{8,0},{16,24},{24,16},{1,9},{9,1},{17,25},{25,17},{2,10},{10... | collective-permute-start | bytes 4718600 | tf_op jit(solution)/shard_map/ppermute | solution.py:31
  229.8 15.6 %collective-permute-start.28 = (bf16[384,1024]{1,0:T(8,128)(2,1)}, bf16[384,1024]{1,0:T(8,128)(2,1)S(1)}, u32[]{:S(2)}, u32[]{:S(2)}) collective-permute-start(bf16[384,1024]{1,0:T(8,128)(2,1)} %get-tuple-element.76), channel_id=1, source_target_pairs={{0,8},{8,0},{16,24},{24,16},{1,9},{9,1},{17,25},{25,17},{2,10},{10... | collective-permute-start | bytes 2359304 | tf_op jit(solution)/shard_map/ppermute | solution.py:31
  239.5 7.5 %collective-permute-start.26 = (bf16[1024,768]{1,0:T(8,128)(2,1)}, bf16[1024,768]{1,0:T(8,128)(2,1)S(1)}, u32[]{:S(2)}, u32[]{:S(2)}) collective-permute-start(bf16[1024,768]{1,0:T(8,128)(2,1)} %get-tuple-element.72), channel_id=1, source_target_pairs={{0,8},{8,0},{16,24},{24,16},{1,9},{9,1},{17,25},{25,17},{2,10},{10... | collective-permute-start | bytes 4718600 | tf_op jit(solution)/shard_map/ppermute | solution.py:31
  243.9 1.5 copy-start.14
  243.9 1.5 copy-start.15
  245.4 1.5 copy-start.5
  245.4 2.2 copy-start.6
  247.6 2.1 copy-start.1

commit v4 on v3

v4 whole, which is shorter than its diff:
```python
import functools

import jax
import jax.numpy as jnp
from jax import lax
from jax.experimental import pallas as pl
from jax.experimental.pallas import tpu as pltpu
from jax.sharding import PartitionSpec as P

TOP = 1
BF = jnp.bfloat16
F32 = jnp.float32
PLAIN = (((1,), (0,)), ((), ()))
CONTRACT_LAST = (((1,), (1,)), ((), ()))
CONTRACT_FIRST = (((0,), (0,)), ((), ()))
MIDDLE = [(1, 2), (2, 1)]
OUTWARD = [(1, 0), (2, 3)]
INWARD = [(0, 1), (3, 2)]


def dot(left, right, dims=PLAIN):
    return lax.dot_general(left, right, dims, preferred_element_type=F32)


def after(value, *others):
    return lax.optimization_barrier((value,) + others)[0]


def send_xor(value, axis, mask):
    size = lax.axis_size(axis)
    return lax.ppermute(value, axis, [(i, i ^ mask) for i in range(size)])


def send_home(value, expert_mask, seq_mask):
    if not expert_mask:
        return send_xor(value, "seq", seq_mask) if seq_mask else value
    if not seq_mask:
        return send_xor(value, "expert", expert_mask)
    seq_count = lax.axis_size("seq")
    total = lax.axis_size("expert") * seq_count
    mask = expert_mask * seq_count + seq_mask
    return lax.ppermute(value, ("expert", "seq"), [(i, i ^ mask) for i in range(total)])


def slot_kernel(blocks, count, choices, place, *refs):
    xs, refs = refs[: count * choices], refs[count * choices :]
    dys, refs = refs[: count * choices], refs[count * choices :]
    wg, wu, wd, refs = refs[0], refs[1], refs[2], refs[3:]
    parts, refs = refs[:count], refs[count:]
    far_share, refs = refs[0], refs[1:]
    own_shares, refs = refs[:count], refs[count:]
    kx, ky, kg, ku, kd, kp, kfar, kown, sems, out_sems = refs
    feat, width = kg.shape
    rows = kx.shape[1]
    step = feat // blocks
    half = feat // 2
    low = 2 * half
    wide = kown.shape[2] - low

    def weights(i):
        cols = pl.ds(i * step, step)
        pairs = [(wg.at[cols], kg.at[cols]), (wu.at[cols], ku.at[cols])]
        return pairs + [(wd.at[:, cols], kd.at[:, cols])]

    def tokens(i, choice):
        cols = pl.ds(i * step, step)
        pairs = []
        for n in range(count):
            pairs += [(xs[n * choices + choice].at[:, cols], kx.at[n, :, cols])]
            pairs += [(dys[n * choices + choice].at[:, cols], ky.at[n, :, cols])]
        return pairs

    def copies_of(i, pairs, first):
        return [
            pltpu.make_async_copy(source, target, sems.at[first + k, i])
            for k, (source, target) in enumerate(pairs)
        ]

    def start_tokens(choice):
        for i in range(blocks):
            for copy in copies_of(i, tokens(i, choice), 3):
                copy.start()

    for i in range(blocks):
        for copy in copies_of(i, weights(i), 0):
            copy.start()
        if i == 0:
            if choices == 1:
                start_tokens(0)
            else:
                for choice in range(choices):
                    pl.when(place[2] == choice)(functools.partial(start_tokens, choice))
    copies = [copies_of(i, weights(i), 0) + copies_of(i, tokens(i, 0), 3) for i in range(blocks)]
    sums = [None] * count
    for i in range(blocks):
        for copy in copies[i]:
            copy.wait()
        cols = pl.ds(i * step, step)
        for n in range(count):
            terms = (
                dot(kx[n, :, cols], kg[cols]),
                dot(kx[n, :, cols], ku[cols]),
                dot(ky[n, :, cols], kd[:, cols], CONTRACT_LAST),
            )
            sums[n] = [s + t for s, t in zip(sums[n], terms)] if i else terms
    outs = []
    backward = []
    side = place[0]
    mine = pl.ds(pl.multiple_of(side * half, half), half)
    other = pl.ds(pl.multiple_of((1 - side) * half, half), half)
    if kfar.shape[0] > rows:
        kfar[rows:] = jnp.zeros((kfar.shape[0] - rows, kfar.shape[1]), BF)
    for n in range(count):
        gate_pre, up_pre, scaled_grad = sums[n]
        sigmoid_gate = jax.nn.sigmoid(gate_pre)
        activated = gate_pre * sigmoid_gate
        hidden = activated * up_pre
        gate_part = jnp.sum(hidden * scaled_grad, axis=1, keepdims=True).astype(BF)
        kp[n, :, feat:] = jnp.broadcast_to(gate_part, (rows, kp.shape[2] - feat))
        gate_delta = (
            scaled_grad * up_pre * sigmoid_gate * (1.0 + gate_pre * (1.0 - sigmoid_gate))
        ).astype(BF)
        up_delta = (scaled_grad * activated).astype(BF)
        backward.append((gate_delta, up_delta))
        kown[n, :rows, :half] = kx[n, :, mine]
        kown[n, :rows, half:low] = ky[n, :, mine]
        last = n == count - 1
        if last:
            kfar[:rows, :half] = kx[n, :, other]
            kfar[:rows, half:low] = ky[n, :, other]
        start = low if last else low + (n + 1) * wide
        for k, delta in enumerate((gate_delta, up_delta, hidden.astype(BF))):
            kown[n, :rows, low + k * width : low + (k + 1) * width] = delta
            kfar[:rows, start + k * width : start + (k + 1) * width] = delta
        if kown.shape[1] > rows:
            kown[n, rows:] = jnp.zeros((kown.shape[1] - rows, kown.shape[2]), BF)
        outs.append(pltpu.make_async_copy(kown.at[n], own_shares[n], out_sems.at[len(outs)]))
        outs[-1].start()
    outs.append(pltpu.make_async_copy(kfar, far_share, out_sems.at[len(outs)]))
    outs[-1].start()
    for i in range(blocks):
        cols = pl.ds(i * step, step)
        taken = pl.ds(i * step, kp.shape[2] - i * step) if i == blocks - 1 else cols
        for n, (gate_delta, up_delta) in enumerate(backward):
            kp[n, :, cols] = (
                dot(gate_delta, kg[cols], CONTRACT_LAST) + dot(up_delta, ku[cols], CONTRACT_LAST)
            ).astype(BF)
            outs.append(
                pltpu.make_async_copy(
                    kp.at[n, :, taken], parts[n].at[:, taken], out_sems.at[len(outs)]
                )
            )
            outs[-1].start()
    for copy in outs:
        copy.wait()


def slot_work(place, xs, dys, gate_local, up_local, down_local):
    rows, feat = xs[0][0].shape
    count, choices = len(xs), len(xs[0])
    width = gate_local.shape[1]
    tall = -(-rows // 16) * 16
    wide = -(-3 * width // 128) * 128
    blocks = 4
    away = pl.BlockSpec(memory_space=pltpu.HBM)
    far_shape, own_shape = (tall, feat + count * wide), (tall, feat + wide)
    outs = pl.pallas_call(
        functools.partial(slot_kernel, blocks, count, choices),
        out_shape=[jax.ShapeDtypeStruct((rows, feat + 128), BF)] * count
        + [jax.ShapeDtypeStruct(far_shape, BF)]
        + [jax.ShapeDtypeStruct(own_shape, BF)] * count,
        in_specs=[pl.BlockSpec(memory_space=pltpu.SMEM)] + [away] * (2 * count * choices + 3),
        out_specs=[away] * (2 * count + 1),
        scratch_shapes=[
            pltpu.VMEM((count, rows, feat), BF),
            pltpu.VMEM((count, rows, feat), BF),
            pltpu.VMEM((feat, width), BF),
            pltpu.VMEM((feat, width), BF),
            pltpu.VMEM((width, feat), BF),
            pltpu.VMEM((count, rows, feat + 128), BF),
            pltpu.VMEM(far_shape, BF),
            pltpu.VMEM((count,) + own_shape, BF),
            pltpu.SemaphoreType.DMA((3 + 2 * count, blocks)),
            pltpu.SemaphoreType.DMA((1 + count + count * blocks,)),
        ],
        compiler_params=pltpu.CompilerParams(vmem_limit_bytes=56 * 1024 * 1024),
        name="slot_work",
    )(place, *sum(xs, []), *sum(dys, []), gate_local, up_local, down_local)
    return outs[:count], outs[count], outs[count + 1 :]


def weight_kernel(cuts, started, width, place, *refs):
    arrays, refs = refs[: len(cuts)], refs[len(cuts) :]
    before, refs = (refs[:4], refs[4:]) if started else ([], refs)
    outs, refs = refs[:4], refs[4:]
    rows, sums_gu, sums_d, old_gu, old_d, sems, old_sems = refs
    quarter = sums_gu.shape[1]
    half = 2 * quarter
    low = 2 * half
    mine = place[1]
    tall = arrays[0].shape[0]
    copies = []
    for array, pieces in zip(arrays, cuts):
        for block, start, target, size in pieces:
            copies.append(
                pltpu.make_async_copy(
                    array.at[:, pl.ds(start, size)],
                    rows.at[pl.ds(block * tall, tall), pl.ds(target, size)],
                    sems.at[len(copies)],
                )
            )
    places = [(mine, 0), (mine, 1), (1 - mine, 0), (1 - mine, 1)]
    for k, ref in enumerate(before):
        side, kind = places[k]
        copies.append(
            pltpu.make_async_copy(ref, (old_gu, old_d)[kind].at[side], old_sems.at[k])
        )
    for copy in copies:
        copy.start()
    for copy in copies:
        copy.wait()
    cut = quarter // 2
    for q in range(2):
        for c in range(2):
            x_cols = pl.ds(q * quarter + c * cut, cut)
            dy_cols = pl.ds(half + q * quarter + c * cut, cut)
            cols = pl.ds(c * cut, cut)
            gate_up = dot(rows[:, x_cols], rows[:, low : low + 2 * width], CONTRACT_FIRST)
            hidden = rows[:, low + 2 * width : low + 3 * width]
            down = dot(hidden, rows[:, dy_cols], CONTRACT_FIRST)
            if started:
                gate_up += old_gu[q, cols].astype(F32)
                down += old_d[q, :, cols].astype(F32)
            sums_gu[q, cols] = gate_up.astype(BF)
            sums_d[q, :, cols] = down.astype(BF)
    copies = [
        pltpu.make_async_copy((sums_gu, sums_d)[kind].at[side], outs[k], old_sems.at[k])
        for k, (side, kind) in enumerate(places)
    ]
    for copy in copies:
        copy.start()
    for copy in copies:
        copy.wait()


def weight_work(place, width, feat, sources, before):
    tall = sources[0][0].shape[0]
    wide = -(-3 * width // 128) * 128
    quarter = feat // 4
    arrays = [array for array, _ in sources]
    cuts = [pieces for _, pieces in sources]
    count = 1 + max(piece[0] for pieces in cuts for piece in pieces)
    away = pl.BlockSpec(memory_space=pltpu.HBM)
    shapes = [(quarter, 2 * width), (width, quarter)] * 2
    kept = [(2,) + shape for shape in shapes[:2]]
    return pl.pallas_call(
        functools.partial(weight_kernel, cuts, bool(before), width),
        out_shape=[jax.ShapeDtypeStruct(shape, BF) for shape in shapes],
        in_specs=[pl.BlockSpec(memory_space=pltpu.SMEM)]
        + [away] * (len(arrays) + len(before)),
        out_specs=[away] * 4,
        scratch_shapes=[pltpu.VMEM((count * tall, feat + wide), BF)]
        + [pltpu.VMEM(shape, BF) for shape in kept * 2]
        + [
            pltpu.SemaphoreType.DMA((sum(len(pieces) for pieces in cuts),)),
            pltpu.SemaphoreType.DMA((4,)),
        ],
        compiler_params=pltpu.CompilerParams(vmem_limit_bytes=56 * 1024 * 1024),
        name="weight_work",
    )(place, *arrays, *before)


def body(tokens, out_grad, gate_prob, expert_ids, w_gate, w_up, w_down):
    expert_count = lax.axis_size("expert")
    seq_count = lax.axis_size("seq")
    tok_rows, feat_width = tokens.shape
    capacity = tok_rows * TOP * 17 // (16 * expert_count)
    my_expert = lax.axis_index("expert")
    my_seq = lax.axis_index("seq")
    route = expert_ids[:, 0]
    onehot = (route[:, None] == jnp.arange(expert_count)[None, :]).astype(F32)
    earlier = (jnp.arange(tok_rows)[:, None] > jnp.arange(tok_rows)[None, :]).astype(F32)
    before = dot(earlier, onehot)
    slot_index = jnp.sum(before * onehot, axis=1).astype(jnp.int32)
    block = jnp.bitwise_xor(route, my_expert)
    target = block * capacity + slot_index
    prob = gate_prob.astype(F32)

    def placer_of(first, last):
        rows = first * capacity + jnp.arange((last - first) * capacity)
        return rows[:, None] == target[None, :]

    def pack_x(first, last):
        return dot(placer_of(first, last).astype(BF), tokens).astype(BF)

    def pack_dy(first, last):
        scaler = jnp.where(placer_of(first, last), prob[None, :], 0.0).astype(BF)
        return dot(scaler, out_grad).astype(BF)

    def joined(first, rest):
        return jnp.concatenate([first] + list(rest), axis=0)

    gate_local, up_local, down_local = w_gate[0], w_up[0], w_down[0]
    others = range(1, expert_count)
    far_x = [pack_x(j, j + 1) for j in others]
    near_x = after(pack_x(0, 1), *far_x)
    out_grad = after(out_grad, near_x)
    far_x = [send_xor(far_x[j - 1], "expert", j) for j in others]
    far_dy = [send_xor(after(pack_dy(j, j + 1), *far_x), "expert", j) for j in others]
    near_dy = pack_dy(0, 1)
    far_x = far_x[0] if len(far_x) == 1 else jnp.concatenate(far_x, axis=0)
    slot_x = [joined(near_x, [far_x])]
    slot_dy = [joined(near_dy, far_dy)]

    dp_index = lax.axis_index("dp")
    is_inner = (my_seq > 0) & (my_seq < seq_count - 1)
    place = jnp.stack([dp_index // 2, dp_index % 2, is_inner]).astype(jnp.int32)
    width = gate_local.shape[1]
    wide = -(-3 * width // 128) * 128
    both = feat_width + wide
    half = feat_width // 2
    tall = -(-expert_count * capacity // 16) * 16

    def work(xs, dys, *others):
        parts, far_share, own_shares = slot_work(
            place, xs, dys, gate_local, up_local, down_local
        )
        far = send_xor(after(far_share, *others), "dp", 2)
        return parts, far, own_shares

    def whole(block):
        return (block, 0, 0, both)

    def rows_of(array, k):
        return array[k * capacity : (k + 1) * capacity]

    if seq_count == 4:
        first_near = send_xor(near_x, "seq", 1)
        across_near = lax.ppermute(near_x, "seq", MIDDLE)
        first_far = send_xor(far_x, "seq", 1)
        across_far = lax.ppermute(far_x, "seq", MIDDLE)
        dy_first = send_xor(slot_dy[0], "seq", 1)
        dy_across = lax.ppermute(after(slot_dy[0], across_far), "seq", MIDDLE)
        x_first = joined(first_near, [first_far])
        x_across = joined(across_near, [across_far])
        early = [
            jnp.where(place[0] == 0, array[:, half:], array[:, :half])
            for array in (slot_x[0], slot_dy[0])
        ]
        early = jnp.concatenate(early, axis=1)
        early = jnp.pad(early, ((0, tall - early.shape[0]), (0, 0)))
        early_far = send_xor(early, "dp", 2)
        x_relayed = lax.ppermute(after(x_first, x_across), "seq", MIDDLE)
        x_near = lax.ppermute(after(x_across, x_first), "seq", OUTWARD)
        dy_relayed = lax.ppermute(after(dy_first, dy_across), "seq", MIDDLE)
        dy_near = lax.ppermute(after(dy_across, dy_first), "seq", OUTWARD)
        parts, far, owns = work([[slot_x[0]], [x_first]], [[slot_dy[0]], [dy_first]], early_far)
        x_far = lax.ppermute(after(x_relayed, x_near, parts[0]), "seq", OUTWARD)
        dy_far = lax.ppermute(after(dy_relayed, dy_near), "seq", OUTWARD)
        home_far = [send_home(rows_of(parts[0], k), k, 0) for k in others]
        sums = weight_work(
            place,
            width,
            feat_width,
            [
                (owns[0], [whole(0)]),
                (owns[1], [whole(1)]),
                (early_far, [(2, 0, 0, feat_width)]),
                (far, [whole(3), (2, both, feat_width, wide)]),
            ],
            [],
        )
        parts_two, far_two, owns_two = work(
            [[x_near, x_relayed]],
            [[dy_near, dy_relayed]],
            far,
        )
        sent = after(parts_two[0], x_far, sums[0])
        over = lax.ppermute(sent, "seq", MIDDLE)
        into = lax.ppermute(sent, "seq", INWARD)
        parts_three, far_three, owns_three = work(
            [[after(x_far, far_two, *home_far), x_across]],
            [[dy_far, dy_across]],
            far_two,
        )
        onward = after(parts[1], parts_three[0]).astype(F32) + over.astype(F32)
        last = (parts_three[0].astype(F32) + into.astype(F32)).astype(BF)
        returned = [(onward.astype(BF), 1), (last, 3)]
        homes = [[rows_of(parts[0], 0)]] + [[array] for array in home_far]
        latest = [(owns_two, far_two), (owns_three, far_three)]
    else:
        sums, latest, returned, homes = [], [], [], [[] for _ in range(expert_count)]
        for j in range(seq_count):
            x_rows, dy_rows = [send_home(array, 0, j) for array in (slot_x[0], slot_dy[0])]
            parts, far, owns = work([[x_rows]], [[dy_rows]])
            returned.append((parts[0], j))
            latest.append((owns, far))
    for j in range(0, len(latest), 2):
        pair = latest[j : j + 2]
        arrays = [array for owns, far in pair for array in (owns[0], far)]
        sources = [(array, [whole(n)]) for n, array in enumerate(arrays)]
        sums = weight_work(place, width, feat_width, sources, sums)
    for k in range(expert_count):
        homes[k] += [send_home(rows_of(part, k), k, j) for part, j in returned]
        homes[k] = sum(part.astype(F32) for part in homes[k]).astype(BF)
    home_x = jnp.concatenate(homes, axis=0)

    keep_gu, keep_d, give_gu, give_d = sums
    gate_up = (keep_gu.astype(F32) + send_xor(give_gu, "dp", 1).astype(F32)).astype(BF)
    down_w_grad = (keep_d.astype(F32) + send_xor(give_d, "dp", 1).astype(F32)).astype(BF)
    gate_w_grad, up_w_grad = gate_up[:, :width], gate_up[:, width:]

    placer = placer_of(0, expert_count)
    placer = placer.astype(BF)
    token_grad = dot(placer, home_x[:, :feat_width], CONTRACT_FIRST).astype(BF)
    home_g = dot(placer, home_x[:, feat_width:], CONTRACT_FIRST)[:, 0]
    gate_grad = (home_g / prob).astype(BF)
    return (token_grad, gate_grad, gate_w_grad[None], up_w_grad[None], down_w_grad[None])


def solution(mesh):
    placed = (
        P(("dp", "expert", "seq"), None),
        P(("dp", "expert", "seq"), None),
        P(("dp", "expert", "seq")),
        P(("dp", "expert", "seq"), None),
        P("expert", None, "seq"),
        P("expert", None, "seq"),
        P("expert", "seq", None),
    )
    return jax.shard_map(
        body,
        mesh=mesh,
        in_specs=placed,
        out_specs=(
            P(("dp", "expert", "seq"), None),
            P(("dp", "expert", "seq")),
            P("expert", "dp", "seq"),
            P("expert", "dp", "seq"),
            P("expert", "seq", "dp"),
        ),
        check_vma=False,
    )
```

time: 251 us -> 232 us (0.924)
  other arithmetic: 22.9 us -> 8.42 us
  waiting for transfers between devices: 112 us -> 105 us
    ppermute x2, waiting for transfers between devices: 12.1 us -> 24.3 us  [send_home(): lax.ppermute(value, ('expert', 'seq'), [(i, i ^ mask) for i in range(tota...]
    ppermute x1, waiting for transfers between devices: 10.3 us -> 0.01 us  [body(): x_relayed = lax.ppermute(after(x_first, x_across), 'seq', MIDDLE)]
    ppermute x1, waiting for transfers between devices: 13.6 us -> 4.15 us  [body(): dy_far = lax.ppermute(after(dy_relayed, dy_near), 'seq', OUTWARD)]
    select_n x4 -> x2, other arithmetic: 8.57 us -> 0.45 us  [body(): jnp.where(place[0] == 0, array[:, half:], array[:, :half])]
    ppermute x1, waiting for transfers between devices: 4.47 us -> 9.99 us  [body(): dy_across = lax.ppermute(after(slot_dy[0], across_far), 'seq', MIDDLE)]
    convert_element_type x5, other arithmetic: 5.57 us -> 1.54 us  [the longest x1 0.48 us: body(): (keep_gu.astype(F32) + send_xor(give_gu, 'dp', 1).astype(F32)).astype(BF)]
    unnamed x34 -> x48, local copies, waits for them, and re-layouts: 3.3 us -> 7.09 us
    ppermute x1, starting transfers between devices: 5.4 us -> 2.55 us  [body(): dy_far = lax.ppermute(after(dy_relayed, dy_near), 'seq', OUTWARD)]
  transfers between devices with their start and end apart: 29 -> 27, of which waited for: 15 -> 14; matrix products, arithmetic and copies ran while one was open for 10% -> 5% of each run, Pallas kernels for 18% -> 23%
where the time goes in v4:
time: 232 us; the launch traced here: 231 us
  waiting for transfers between devices  105 us (45%)
  Pallas kernels  52.5 us (23%)
  starting transfers between devices  48.6 us (21%)
  local copies, waits for them, and re-layouts  8.81 us (4%)
  other arithmetic  8.42 us (4%)
  matrix products  6.08 us (3%)
    ppermute x14, waiting for transfers between devices, send_xor(): return lax.ppermute(value, axis, [(i, i ^ mask) for i in range(size)])  45.9 us
    pallas_call x3, Pallas kernels, slot_work(): pl.pallas_call(functools.partial(slot_kernel, blocks, count, choices), ou...  32.7 us
    ppermute x2, waiting for transfers between devices, send_home(): lax.ppermute(value, ('expert', 'seq'), [(i, i ^ mask) for i in range(tota...  24.3 us
    pallas_call x2, Pallas kernels, weight_work(): pl.pallas_call(functools.partial(weight_kernel, cuts, bool(before), width...  19.9 us
    ppermute x1, waiting for transfers between devices, body(): dy_near = lax.ppermute(after(dy_across, dy_first), 'seq', OUTWARD)  19.4 us
    ppermute x14, starting transfers between devices, send_xor(): return lax.ppermute(value, axis, [(i, i ^ mask) for i in range(size)])  13.1 us
    ppermute x1, waiting for transfers between devices, body(): dy_across = lax.ppermute(after(slot_dy[0], across_far), 'seq', MIDDLE)  9.99 us
    unnamed x48, local copies, waits for them, and re-layouts  7.09 us
  transfers between devices with their start and end apart: 27, of which 14 were waited for; matrix products, arithmetic and copies ran while one was open for 5% of the time, Pallas kernels for 23%

profile of v4, /device:TPU:8, one launch (start us, length us, event | category | flops | bytes accessed | tf_op | source)
XLA Modules:
  0.0 230.7 jit_solution(2304894386348126267)
XLA Ops:
  0.7 0.9 fusion.5
  1.6 0.7 convert_add_fusion
  2.3 1.2 convolution_convert_fusion.3
  3.4 1.5 collective-permute-start
  5.3 3.5 %collective-permute-start.5 = (bf16[68,4096]{1,0:T(8,128)(2,1)S(1)}, bf16[68,4096]{1,0:T(8,128)(2,1)}, u32[]{:S(2)}, u32[]{:S(2)}) collective-permute-start(bf16[68,4096]{1,0:T(8,128)(2,1)S(1)} %convolution_convert_fusion.4), channel_id=1, source_target_pairs={{1,2},{2,1},{5,6},{6,5},{9,10},{10,9},{13,14},{14,13},{17,18},{18,... | collective-permute-start | bytes 1671176 | tf_op jit(solution)/shard_map/ppermute | solution.py:339
  8.9 1.2 convolution_convert_fusion.1
  10.1 8.6 %collective-permute-done = bf16[68,4096]{1,0:T(8,128)(2,1)S(1)} collective-permute-done((bf16[68,4096]{1,0:T(8,128)(2,1)}, bf16[68,4096]{1,0:T(8,128)(2,1)S(1)}, u32[]{:S(2)}, u32[]{:S(2)}) %collective-permute-start) | collective-permute-done | bytes 557088 | tf_op jit(solution)/shard_map/ppermute | solution.py:31
  18.7 1.5 collective-permute-start.3
  20.2 0.6 pad_add_fusion.place
  21.2 3.5 %collective-permute-start.6 = (bf16[68,4096]{1,0:T(8,128)(2,1)S(1)}, bf16[68,4096]{1,0:T(8,128)(2,1)S(1)}, u32[]{:S(2)}, u32[]{:S(2)}) collective-permute-start(bf16[68,4096]{1,0:T(8,128)(2,1)S(1)} %collective-permute-done), channel_id=1, source_target_pairs={{1,2},{2,1},{5,6},{6,5},{9,10},{10,9},{13,14},{14,13},{17,18},{18,... | collective-permute-start | bytes 1671176 | tf_op jit(solution)/shard_map/ppermute | solution.py:341
  25.0 8.2 %collective-permute-done.3 = bf16[68,4096]{1,0:T(8,128)(2,1)S(1)} collective-permute-done((bf16[68,4096]{1,0:T(8,128)(2,1)}, bf16[68,4096]{1,0:T(8,128)(2,1)S(1)}, u32[]{:S(2)}, u32[]{:S(2)}) %collective-permute-start.3) | collective-permute-done | bytes 557088 | tf_op jit(solution)/shard_map/ppermute | solution.py:31
  33.4 0.6 collective-permute-start.4
  34.4 1.5 collective-permute-start.13
  35.9 1.3 collective-permute-done.6
  37.1 1.2 pad_maximum_fusion.3.refs_1_
  38.4 2.7 %collective-permute-done.2 = bf16[68,4096]{1,0:T(8,128)(2,1)S(1)} collective-permute-done((bf16[68,4096]{1,0:T(8,128)(2,1)S(1)}, bf16[68,4096]{1,0:T(8,128)(2,1)S(1)}, u32[]{:S(2)}, u32[]{:S(2)}) %collective-permute-start.2) | collective-permute-done | bytes 557088 | tf_op jit(solution)/shard_map/ppermute | solution.py:31
  41.0 1.2 pad_maximum_fusion.2.refs_1_
  42.3 2.4 %collective-permute-start.7 = (bf16[136,4096]{1,0:T(8,128)(2,1)S(1)}, bf16[136,4096]{1,0:T(8,128)(2,1)}, u32[]{:S(2)}, u32[]{:S(2)}) collective-permute-start(bf16[136,4096]{1,0:T(8,128)(2,1)S(1)} %pad_maximum_fusion.2.refs_1_), channel_id=1, source_target_pairs={{1,2},{2,1},{5,6},{6,5},{9,10},{10,9},{13,14},{14,13},{17,18},{18,... | collective-permute-start | bytes 3342344 | tf_op jit(solution)/shard_map/ppermute | solution.py:353
  44.7 2.3 collective-permute-start.8
  47.0 3.5 %collective-permute-start.10 = (bf16[136,4096]{1,0:T(8,128)(2,1)S(1)}, bf16[136,4096]{1,0:T(8,128)(2,1)}, u32[]{:S(2)}, u32[]{:S(2)}) collective-permute-start(bf16[136,4096]{1,0:T(8,128)(2,1)S(1)} %pad_maximum_fusion.1.refs_2_), channel_id=1, source_target_pairs={{1,2},{2,1},{5,6},{6,5},{9,10},{10,9},{13,14},{14,13},{17,18},{18,... | collective-permute-start | bytes 3342344 | tf_op jit(solution)/shard_map/ppermute | solution.py:343
  50.4 1.2 pad_maximum_fusion.refs_0_
  51.6 10.8 %collective-permute-done.4.refs_3_ = bf16[136,4096]{1,0:T(8,128)(2,1)S(1)} collective-permute-done((bf16[136,4096]{1,0:T(8,128)(2,1)S(1)}, bf16[136,4096]{1,0:T(8,128)(2,1)S(1)}, u32[]{:S(2)}, u32[]{:S(2)}) %collective-permute-start.4) | collective-permute-done | bytes 1114144 | tf_op jit(solution)/shard_map/ppermute | solution.py:31
  62.4 1.0 copy-done.14
  63.4 14.3 %slot_work.3 = (bf16[136,4224]{1,0:T(8,128)(2,1)}, bf16[136,4224]{1,0:T(8,128)(2,1)}, bf16[144,6400]{1,0:T(8,128)(2,1)}, bf16[144,5248]{1,0:T(8,128)(2,1)}, bf16[144,5248]{1,0:T(8,128)(2,1)}) custom-call(s32[3]{0:T(128)} %pad_add_fusion.place, bf16[136,4096]{1,0:T(8,128)(2,1)} %pad_maximum_fusion.refs_0_, bf16[136,4096]{1,0:T(8,128)(2,1)} %copy-done.4, ...), custom_call_target="tpu_custom_call" | custom-call | tf_op jit(solution)/shard_map/slot_work/pallas_call | solution.py:167
  77.7 1.0 copy-done.11
  78.8 1.5 collective-permute-start.14
  80.3 10.0 %collective-permute-done.10.refs_3_ = bf16[136,4096]{1,0:T(8,128)(2,1)} collective-permute-done((bf16[136,4096]{1,0:T(8,128)(2,1)S(1)}, bf16[136,4096]{1,0:T(8,128)(2,1)}, u32[]{:S(2)}, u32[]{:S(2)}) %collective-permute-start.10) | collective-permute-done | bytes 1114144 | tf_op jit(solution)/shard_map/ppermute | solution.py:343
  90.2 1.3 collective-permute-start.11
  91.6 3.5 %collective-permute-start.12 = (bf16[136,4096]{1,0:T(8,128)(2,1)S(1)}, bf16[136,4096]{1,0:T(8,128)(2,1)S(1)}, u32[]{:S(2)}, u32[]{:S(2)}) collective-permute-start(bf16[136,4096]{1,0:T(8,128)(2,1)S(1)} %copy-done.15), channel_id=1, source_target_pairs={{1,2},{2,1},{5,6},{6,5},{9,10},{10,9},{13,14},{14,13},{17,18},{18,... | collective-permute-start | bytes 3342344 | tf_op jit(solution)/shard_map/ppermute | solution.py:355
  95.1 2.3 collective-permute-start.9
  97.4 19.4 %collective-permute-done.11.refs_2_ = bf16[136,4096]{1,0:T(8,128)(2,1)S(1)} collective-permute-done((bf16[136,4096]{1,0:T(8,128)(2,1)}, bf16[136,4096]{1,0:T(8,128)(2,1)S(1)}, u32[]{:S(2)}, u32[]{:S(2)}) %collective-permute-start.11) | collective-permute-done | bytes 1114144 | tf_op jit(solution)/shard_map/ppermute | solution.py:356
  116.9 1.0 copy-done.18
  117.8 1.0 copy-done.16
  118.9 9.2 %slot_work.4 = (bf16[136,4224]{1,0:T(8,128)(2,1)}, bf16[144,5248]{1,0:T(8,128)(2,1)}, bf16[144,5248]{1,0:T(8,128)(2,1)}) custom-call(s32[3]{0:T(128)} %pad_add_fusion.place, bf16[136,4096]{1,0:T(8,128)(2,1)} %collective-permute-done.8.refs_0_, bf16[136,4096]{1,0:T(8,128)(2,1)} %collective-permute-done.7.refs_1_, bf16[136,4096]{1,0:T(8,128)(2,1)} %copy-done.18, ...), custom_call_target="tpu_custom_call" | custom-call | tf_op jit(solution)/shard_map/slot_work/pallas_call | solution.py:167
  128.1 1.6 collective-permute-start.15
  129.7 9.3 %weight_work.2 = (bf16[1024,768]{1,0:T(8,128)(2,1)}, bf16[384,1024]{1,0:T(8,128)(2,1)}, bf16[1024,768]{1,0:T(8,128)(2,1)}, bf16[384,1024]{1,0:T(8,128)(2,1)}) custom-call(s32[3]{0:T(128)} %pad_add_fusion.place, bf16[144,5248]{1,0:T(8,128)(2,1)} %get-tuple-element.60.refs_0_, bf16[144,5248]{1,0:T(8,128)(2,1)} %get-tuple-element.61.refs_1_, ...), custom_call_target="tpu_custom_call" | custom-call | tf_op jit(solution)/shard_map/weight_work/pallas_call | solution.py:256
  139.0 3.5 %collective-permute-start.18 = (bf16[136,4224]{1,0:T(8,128)(2,1)}, bf16[136,4224]{1,0:T(8,128)(2,1)S(1)}, u32[]{:S(2)}, u32[]{:S(2)}) collective-permute-start(bf16[136,4224]{1,0:T(8,128)(2,1)} %get-tuple-element.63), channel_id=1, source_target_pairs={{1,2},{2,1},{5,6},{6,5},{9,10},{10,9},{13,14},{14,13},{17,18},{18,... | collective-permute-start | bytes 3446792 | tf_op jit(solution)/shard_map/ppermute | solution.py:379
  142.5 2.5 %collective-permute-start.17 = (bf16[136,4096]{1,0:T(8,128)(2,1)S(1)}, bf16[136,4096]{1,0:T(8,128)(2,1)}, u32[]{:S(2)}, u32[]{:S(2)}) collective-permute-start(bf16[136,4096]{1,0:T(8,128)(2,1)S(1)} %copy-done.17), channel_id=1, source_target_pairs={{1,0},{2,3},{5,4},{6,7},{9,8},{10,11},{13,12},{14,15},{17,16},{18,... | collective-permute-start | bytes 3342344 | tf_op jit(solution)/shard_map/ppermute | solution.py:359
  145.2 0.7 collective-permute-start.16
  145.9 1.5 collective-permute-start.20
  147.4 7.9 %collective-permute-done.16 = bf16[68,4224]{1,0:T(8,128)(2,1)S(1)} collective-permute-done((bf16[68,4224]{1,0:T(8,128)(2,1)S(1)}, bf16[68,4224]{1,0:T(8,128)(2,1)S(1)}, u32[]{:S(2)}, u32[]{:S(2)}) %collective-permute-start.16) | collective-permute-done | bytes 574496 | tf_op jit(solution)/shard_map/ppermute | solution.py:31
  155.3 0.6 collective-permute-done.15.refs_1_
  156.2 4.1 %collective-permute-done.17.refs_2_ = bf16[136,4096]{1,0:T(8,128)(2,1)} collective-permute-done((bf16[136,4096]{1,0:T(8,128)(2,1)S(1)}, bf16[136,4096]{1,0:T(8,128)(2,1)}, u32[]{:S(2)}, u32[]{:S(2)}) %collective-permute-start.17) | collective-permute-done | bytes 1114144 | tf_op jit(solution)/shard_map/ppermute | solution.py:359
  160.3 9.2 %slot_work.5 = (bf16[136,4224]{1,0:T(8,128)(2,1)}, bf16[144,5248]{1,0:T(8,128)(2,1)}, bf16[144,5248]{1,0:T(8,128)(2,1)}) custom-call(s32[3]{0:T(128)} %pad_add_fusion.place, bf16[136,4096]{1,0:T(8,128)(2,1)} %collective-permute-done.9.refs_0_, bf16[136,4096]{1,0:T(8,128)(2,1)} %copy-done.2, bf16[136,4096]{1,0:T(8,128)(2,1)} %collective-permute-done.17.refs_2_, ...), custom_call_target="tpu_custom_call" | custom-call | tf_op jit(solution)/shard_map/slot_work/pallas_call | solution.py:167
  169.6 0.3 add_convert_fusion.2
  170.1 1.1 copy-done.13
  171.6 3.6 %collective-permute-start.23 = (bf16[68,4224]{1,0:T(8,128)(2,1)S(1)}, bf16[68,4224]{1,0:T(8,128)(2,1)S(1)}, u32[]{:S(2)}, u32[]{:S(2)}) collective-permute-start(bf16[68,4224]{1,0:T(8,128)(2,1)S(1)} %get-tuple-element.79), channel_id=1, source_target_pairs={{0,7},{1,6},{2,5},{3,4},{4,3},{5,2},{6,1},{7,0},{8,15},{9,14},{10,... | collective-permute-start | bytes 1723400 | tf_op jit(solution)/shard_map/ppermute | solution.py:42
  175.2 2.2 collective-permute-start.22
  177.4 1.5 collective-permute-start.24
  178.9 0.7 collective-permute-start.21
  179.5 1.3 collective-permute-start.19
  180.9 23.4 %collective-permute-done.23 = bf16[68,4224]{1,0:T(8,128)(2,1)S(1)} collective-permute-done((bf16[68,4224]{1,0:T(8,128)(2,1)S(1)}, bf16[68,4224]{1,0:T(8,128)(2,1)S(1)}, u32[]{:S(2)}, u32[]{:S(2)}) %collective-permute-start.23) | collective-permute-done | bytes 574496 | tf_op jit(solution)/shard_map/ppermute | solution.py:42
  204.3 0.8 collective-permute-done.22
  205.4 1.1 copy-done.9
  206.5 10.5 %weight_work.3 = (bf16[1024,768]{1,0:T(8,128)(2,1)}, bf16[384,1024]{1,0:T(8,128)(2,1)}, bf16[1024,768]{1,0:T(8,128)(2,1)}, bf16[384,1024]{1,0:T(8,128)(2,1)}) custom-call(s32[3]{0:T(128)} %pad_add_fusion.place, bf16[144,5248]{1,0:T(8,128)(2,1)} %get-tuple-element.64.refs_0_, bf16[144,5248]{1,0:T(8,128)(2,1)} %copy-done.8, ...), custom_call_target="tpu_custom_call" | custom-call | tf_op jit(solution)/shard_map/weight_work/pallas_call | solution.py:256
  217.1 0.5 collective-permute-start.25
  217.6 4.5 %collective-permute-done.21 = bf16[68,4224]{1,0:T(8,128)(2,1)S(1)} collective-permute-done((bf16[68,4224]{1,0:T(8,128)(2,1)S(1)}, bf16[68,4224]{1,0:T(8,128)(2,1)S(1)}, u32[]{:S(2)}, u32[]{:S(2)}) %collective-permute-start.21) | collective-permute-done | bytes 574496 | tf_op jit(solution)/shard_map/ppermute | solution.py:31
  222.2 2.5 %collective-permute-done.19 = bf16[68,4224]{1,0:T(8,128)(2,1)S(1)} collective-permute-done((bf16[68,4224]{1,0:T(8,128)(2,1)S(1)}, bf16[68,4224]{1,0:T(8,128)(2,1)S(1)}, u32[]{:S(2)}, u32[]{:S(2)}) %collective-permute-start.19) | collective-permute-done | bytes 574496 | tf_op jit(solution)/shard_map/ppermute | solution.py:31
  225.0 0.7 fusion.7
  225.7 1.5 convolution_convert_fusion
  227.2 1.2 fusion.8
  228.4 0.5 copy-done.7
  228.9 0.5 add_convert_fusion
  229.3 1.3 slice_bitcast_fusion
  (70 shorter events, 3.1 us)
Async XLA Ops:
  0.6 1.6 copy-start
  3.4 5.4 %copy-start.5 = (bf16[128,4096]{1,0:T(8,128)(2,1)S(1)}, bf16[128,4096]{1,0:T(8,128)(2,1)}, u32[]{:S(2)}) copy-start(bf16[128,4096]{1,0:T(8,128)(2,1)} %param.8) | copy-start | bytes 3145732
  3.4 5.4 %copy-start.22 = (bf16[128]{0:T(256)(128)(2,1)S(1)}, bf16[128]{0:T(256)(128)(2,1)}, u32[]{:S(2)}) copy-start(bf16[128]{0:T(256)(128)(2,1)} %param.9) | copy-start | bytes 772
  3.4 15.3 %collective-permute-start = (bf16[68,4096]{1,0:T(8,128)(2,1)}, bf16[68,4096]{1,0:T(8,128)(2,1)S(1)}, u32[]{:S(2)}, u32[]{:S(2)}) collective-permute-start(bf16[68,4096]{1,0:T(8,128)(2,1)} %convolution_convert_fusion.3), channel_id=1, source_target_pairs={{0,4},{4,0},{1,5},{5,1},{2,6},{6,2},{3,7},{7,3},{8,12},{12,8},{9,1... | collective-permute-start | bytes 1671176 | tf_op jit(solution)/shard_map/ppermute | solution.py:31
  5.3 29.1 %collective-permute-start.5 = (bf16[68,4096]{1,0:T(8,128)(2,1)S(1)}, bf16[68,4096]{1,0:T(8,128)(2,1)}, u32[]{:S(2)}, u32[]{:S(2)}) collective-permute-start(bf16[68,4096]{1,0:T(8,128)(2,1)S(1)} %convolution_convert_fusion.4), channel_id=1, source_target_pairs={{1,2},{2,1},{5,6},{6,5},{9,10},{10,9},{13,14},{14,13},{17,18},{18,... | collective-permute-start | bytes 1671176 | tf_op jit(solution)/shard_map/ppermute | solution.py:339
  8.8 29.6 %collective-permute-start.1 = (bf16[68,4096]{1,0:T(8,128)(2,1)S(1)}, bf16[68,4096]{1,0:T(8,128)(2,1)}, u32[]{:S(2)}, u32[]{:S(2)}) collective-permute-start(bf16[68,4096]{1,0:T(8,128)(2,1)S(1)} %convolution_convert_fusion.4), channel_id=1, source_target_pairs={{0,1},{1,0},{2,3},{3,2},{4,5},{5,4},{6,7},{7,6},{8,9},{9,8},{10,11... | collective-permute-start | bytes 1671176 | tf_op jit(solution)/shard_map/ppermute | solution.py:31
  18.7 14.5 %collective-permute-start.3 = (bf16[68,4096]{1,0:T(8,128)(2,1)}, bf16[68,4096]{1,0:T(8,128)(2,1)S(1)}, u32[]{:S(2)}, u32[]{:S(2)}) collective-permute-start(bf16[68,4096]{1,0:T(8,128)(2,1)} %convolution_convert_fusion.1), channel_id=1, source_target_pairs={{0,4},{4,0},{1,5},{5,1},{2,6},{6,2},{3,7},{7,3},{8,12},{12,8},{9,1... | collective-permute-start | bytes 1671176 | tf_op jit(solution)/shard_map/ppermute | solution.py:31
  21.2 15.9 %collective-permute-start.6 = (bf16[68,4096]{1,0:T(8,128)(2,1)S(1)}, bf16[68,4096]{1,0:T(8,128)(2,1)S(1)}, u32[]{:S(2)}, u32[]{:S(2)}) collective-permute-start(bf16[68,4096]{1,0:T(8,128)(2,1)S(1)} %collective-permute-done), channel_id=1, source_target_pairs={{1,2},{2,1},{5,6},{6,5},{9,10},{10,9},{13,14},{14,13},{17,18},{18,... | collective-permute-start | bytes 1671176 | tf_op jit(solution)/shard_map/ppermute | solution.py:341
  24.7 16.3 %collective-permute-start.2 = (bf16[68,4096]{1,0:T(8,128)(2,1)S(1)}, bf16[68,4096]{1,0:T(8,128)(2,1)S(1)}, u32[]{:S(2)}, u32[]{:S(2)}) collective-permute-start(bf16[68,4096]{1,0:T(8,128)(2,1)S(1)} %collective-permute-done), channel_id=1, source_target_pairs={{0,1},{1,0},{2,3},{3,2},{4,5},{5,4},{6,7},{7,6},{8,9},{9,8},{10,11... | collective-permute-start | bytes 1671176 | tf_op jit(solution)/shard_map/ppermute | solution.py:31
  33.4 13.5 %copy-start.3 = (bf16[136,4096]{1,0:T(8,128)(2,1)}, bf16[136,4096]{1,0:T(8,128)(2,1)S(1)}, u32[]{:S(2)}) copy-start(bf16[136,4096]{1,0:T(8,128)(2,1)S(1)} %pad_maximum_fusion.1.refs_2_) | copy-start | bytes 3342340
  33.4 29.0 %collective-permute-start.4 = (bf16[136,4096]{1,0:T(8,128)(2,1)S(1)}, bf16[136,4096]{1,0:T(8,128)(2,1)S(1)}, u32[]{:S(2)}, u32[]{:S(2)}) collective-permute-start(bf16[136,4096]{1,0:T(8,128)(2,1)S(1)} %pad_maximum_fusion.1.refs_2_), channel_id=1, source_target_pairs={{0,1},{1,0},{2,3},{3,2},{4,5},{5,4},{6,7},{7,6},{8,9},{9,8},{10,11... | collective-permute-start | bytes 3342344 | tf_op jit(solution)/shard_map/ppermute | solution.py:31
  34.4 43.3 %collective-permute-start.13 = (bf16[144,4096]{1,0:T(8,128)(2,1)S(1)}, bf16[144,4096]{1,0:T(8,128)(2,1)S(1)}, u32[]{:S(2)}, u32[]{:S(2)}) collective-permute-start(bf16[144,4096]{1,0:T(8,128)(2,1)S(1)} %fusion.2), channel_id=1, source_target_pairs={{0,16},{8,24},{16,0},{24,8},{1,17},{9,25},{17,1},{25,9},{2,18},{10... | collective-permute-start | bytes 3538952 | tf_op jit(solution)/shard_map/ppermute | solution.py:31
  38.4 13.3 %copy-start.2 = (bf16[136,4096]{1,0:T(8,128)(2,1)}, bf16[136,4096]{1,0:T(8,128)(2,1)S(1)}, u32[]{:S(2)}) copy-start(bf16[136,4096]{1,0:T(8,128)(2,1)S(1)} %pad_maximum_fusion.3.refs_1_) | copy-start | bytes 3342340
  42.3 21.2 %copy-start.4 = (bf16[136,4096]{1,0:T(8,128)(2,1)}, bf16[136,4096]{1,0:T(8,128)(2,1)S(1)}, u32[]{:S(2)}) copy-start(bf16[136,4096]{1,0:T(8,128)(2,1)S(1)} %pad_maximum_fusion.2.refs_1_) | copy-start | bytes 3342340
  42.3 52.8 %collective-permute-start.7 = (bf16[136,4096]{1,0:T(8,128)(2,1)S(1)}, bf16[136,4096]{1,0:T(8,128)(2,1)}, u32[]{:S(2)}, u32[]{:S(2)}) collective-permute-start(bf16[136,4096]{1,0:T(8,128)(2,1)S(1)} %pad_maximum_fusion.2.refs_1_), channel_id=1, source_target_pairs={{1,2},{2,1},{5,6},{6,5},{9,10},{10,9},{13,14},{14,13},{17,18},{18,... | collective-permute-start | bytes 3342344 | tf_op jit(solution)/shard_map/ppermute | solution.py:353
  44.7 50.5 %collective-permute-start.8 = (bf16[136,4096]{1,0:T(8,128)(2,1)S(1)}, bf16[136,4096]{1,0:T(8,128)(2,1)}, u32[]{:S(2)}, u32[]{:S(2)}) collective-permute-start(bf16[136,4096]{1,0:T(8,128)(2,1)S(1)} %pad_maximum_fusion.3.refs_1_), channel_id=1, source_target_pairs={{1,0},{2,3},{5,4},{6,7},{9,8},{10,11},{13,12},{14,15},{17,16},{18,... | collective-permute-start | bytes 3342344 | tf_op jit(solution)/shard_map/ppermute | solution.py:354
  47.0 43.3 %collective-permute-start.10 = (bf16[136,4096]{1,0:T(8,128)(2,1)S(1)}, bf16[136,4096]{1,0:T(8,128)(2,1)}, u32[]{:S(2)}, u32[]{:S(2)}) collective-permute-start(bf16[136,4096]{1,0:T(8,128)(2,1)S(1)} %pad_maximum_fusion.1.refs_2_), channel_id=1, source_target_pairs={{1,2},{2,1},{5,6},{6,5},{9,10},{10,9},{13,14},{14,13},{17,18},{18,... | collective-permute-start | bytes 3342344 | tf_op jit(solution)/shard_map/ppermute | solution.py:343
  62.4 1.0 copy-start.14
  63.4 28.2 %copy-start.15 = (bf16[136,4096]{1,0:T(8,128)(2,1)S(1)}, bf16[136,4096]{1,0:T(8,128)(2,1)}, u32[]{:S(2)}) copy-start(bf16[136,4096]{1,0:T(8,128)(2,1)} %copy-done.14) | copy-start | bytes 3342340
  77.7 1.0 copy-start.11
  78.8 49.3 %collective-permute-start.14 = (bf16[144,6400]{1,0:T(8,128)(2,1)}, bf16[144,6400]{1,0:T(8,128)(2,1)S(1)}, u32[]{:S(2)}, u32[]{:S(2)}) collective-permute-start(bf16[144,6400]{1,0:T(8,128)(2,1)} %get-tuple-element.53), channel_id=1, source_target_pairs={{0,16},{8,24},{16,0},{24,8},{1,17},{9,25},{17,1},{25,9},{2,18},{10... | collective-permute-start | bytes 5529608 | tf_op jit(solution)/shard_map/ppermute | solution.py:31
  90.2 26.6 %collective-permute-start.11 = (bf16[136,4096]{1,0:T(8,128)(2,1)}, bf16[136,4096]{1,0:T(8,128)(2,1)S(1)}, u32[]{:S(2)}, u32[]{:S(2)}) collective-permute-start(bf16[136,4096]{1,0:T(8,128)(2,1)} %collective-permute-done.10.refs_3_), channel_id=1, source_target_pairs={{1,0},{2,3},{5,4},{6,7},{9,8},{10,11},{13,12},{14,15},{17,16},{18,... | collective-permute-start | bytes 3342344 | tf_op jit(solution)/shard_map/ppermute | solution.py:356
  91.6 25.2 %collective-permute-start.12 = (bf16[136,4096]{1,0:T(8,128)(2,1)S(1)}, bf16[136,4096]{1,0:T(8,128)(2,1)S(1)}, u32[]{:S(2)}, u32[]{:S(2)}) collective-permute-start(bf16[136,4096]{1,0:T(8,128)(2,1)S(1)} %copy-done.15), channel_id=1, source_target_pairs={{1,2},{2,1},{5,6},{6,5},{9,10},{10,9},{13,14},{14,13},{17,18},{18,... | collective-permute-start | bytes 3342344 | tf_op jit(solution)/shard_map/ppermute | solution.py:355
  95.1 43.8 %collective-permute-start.9 = (bf16[136,4096]{1,0:T(8,128)(2,1)}, bf16[136,4096]{1,0:T(8,128)(2,1)}, u32[]{:S(2)}, u32[]{:S(2)}) collective-permute-start(bf16[136,4096]{1,0:T(8,128)(2,1)} %collective-permute-done.7.refs_1_), channel_id=1, source_target_pairs={{1,0},{2,3},{5,4},{6,7},{9,8},{10,11},{13,12},{14,15},{17,16},{18,... | collective-permute-start | bytes 3342344 | tf_op jit(solution)/shard_map/ppermute | solution.py:358
  116.8 1.0 copy-start.18
  117.8 1.0 copy-start.16
  128.1 1.6 copy-start.6
  128.1 27.8 %collective-permute-start.15 = (bf16[144,5248]{1,0:T(8,128)(2,1)}, bf16[144,5248]{1,0:T(8,128)(2,1)S(1)}, u32[]{:S(2)}, u32[]{:S(2)}) collective-permute-start(bf16[144,5248]{1,0:T(8,128)(2,1)} %get-tuple-element.54), channel_id=1, source_target_pairs={{0,16},{8,24},{16,0},{24,8},{1,17},{9,25},{17,1},{25,9},{2,18},{10... | collective-permute-start | bytes 4534280 | tf_op jit(solution)/shard_map/ppermute | solution.py:31
  129.6 12.8 %copy-start.17 = (bf16[136,4096]{1,0:T(8,128)(2,1)S(1)}, bf16[136,4096]{1,0:T(8,128)(2,1)}, u32[]{:S(2)}) copy-start(bf16[136,4096]{1,0:T(8,128)(2,1)} %copy-done.16) | copy-start | bytes 3342340
  129.7 15.4 %copy-start.10 = (bf16[136,4224]{1,0:T(8,128)(2,1)S(1)}, bf16[136,4224]{1,0:T(8,128)(2,1)}, u32[]{:S(2)}) copy-start(bf16[136,4224]{1,0:T(8,128)(2,1)} %get-tuple-element.43) | copy-start | bytes 3446788
  139.0 30.6 %collective-permute-start.18 = (bf16[136,4224]{1,0:T(8,128)(2,1)}, bf16[136,4224]{1,0:T(8,128)(2,1)S(1)}, u32[]{:S(2)}, u32[]{:S(2)}) collective-permute-start(bf16[136,4224]{1,0:T(8,128)(2,1)} %get-tuple-element.63), channel_id=1, source_target_pairs={{1,2},{2,1},{5,6},{6,5},{9,10},{10,9},{13,14},{14,13},{17,18},{18,... | collective-permute-start | bytes 3446792 | tf_op jit(solution)/shard_map/ppermute | solution.py:379
  142.5 17.8 %collective-permute-start.17 = (bf16[136,4096]{1,0:T(8,128)(2,1)S(1)}, bf16[136,4096]{1,0:T(8,128)(2,1)}, u32[]{:S(2)}, u32[]{:S(2)}) collective-permute-start(bf16[136,4096]{1,0:T(8,128)(2,1)S(1)} %copy-done.17), channel_id=1, source_target_pairs={{1,0},{2,3},{5,4},{6,7},{9,8},{10,11},{13,12},{14,15},{17,16},{18,... | collective-permute-start | bytes 3342344 | tf_op jit(solution)/shard_map/ppermute | solution.py:359
  145.2 24.4 %copy-start.12 = (bf16[136,4224]{1,0:T(8,128)(2,1)S(1)}, bf16[136,4224]{1,0:T(8,128)(2,1)}, u32[]{:S(2)}) copy-start(bf16[136,4224]{1,0:T(8,128)(2,1)} %get-tuple-element.58) | copy-start | bytes 3446788
  145.2 10.1 %collective-permute-start.16 = (bf16[68,4224]{1,0:T(8,128)(2,1)S(1)}, bf16[68,4224]{1,0:T(8,128)(2,1)S(1)}, u32[]{:S(2)}, u32[]{:S(2)}) collective-permute-start(bf16[68,4224]{1,0:T(8,128)(2,1)S(1)} %slice.50), channel_id=1, source_target_pairs={{0,4},{4,0},{1,5},{5,1},{2,6},{6,2},{3,7},{7,3},{8,12},{12,8},{9,1... | collective-permute-start | bytes 1723400 | tf_op jit(solution)/shard_map/ppermute | solution.py:31
  145.9 24.2 %collective-permute-start.20 = (bf16[136,4224]{1,0:T(8,128)(2,1)}, bf16[136,4224]{1,0:T(8,128)(2,1)S(1)}, u32[]{:S(2)}, u32[]{:S(2)}) collective-permute-start(bf16[136,4224]{1,0:T(8,128)(2,1)} %get-tuple-element.63), channel_id=1, source_target_pairs={{0,1},{3,2},{4,5},{7,6},{8,9},{11,10},{12,13},{15,14},{16,17},{19,... | collective-permute-start | bytes 3446792 | tf_op jit(solution)/shard_map/ppermute | solution.py:380
  155.3 0.8 copy-start.20
  156.2 13.4 %copy-start.8 = (bf16[144,5248]{1,0:T(8,128)(2,1)}, bf16[144,5248]{1,0:T(8,128)(2,1)S(1)}, u32[]{:S(2)}) copy-start(bf16[144,5248]{1,0:T(8,128)(2,1)S(1)} %collective-permute-done.15.refs_1_) | copy-start | bytes 4534276
  169.9 1.3 copy-start.13
  171.4 6.0 %copy-start.23 = (bf16[144,5248]{1,0:T(8,128)(2,1)S(1)}, bf16[144,5248]{1,0:T(8,128)(2,1)}, u32[]{:S(2)}) copy-start(bf16[144,5248]{1,0:T(8,128)(2,1)} %get-tuple-element.67) | copy-start | bytes 4534276
  171.4 33.7 %copy-start.21 = (bf16[68,4224]{1,0:T(8,128)(2,1)S(1)}, bf16[68,4224]{1,0:T(8,128)(2,1)}, u32[]{:S(2)}) copy-start(bf16[68,4224]{1,0:T(8,128)(2,1)} %copy-done.20) | copy-start | bytes 1723396
  171.6 32.7 %collective-permute-start.23 = (bf16[68,4224]{1,0:T(8,128)(2,1)S(1)}, bf16[68,4224]{1,0:T(8,128)(2,1)S(1)}, u32[]{:S(2)}, u32[]{:S(2)}) collective-permute-start(bf16[68,4224]{1,0:T(8,128)(2,1)S(1)} %get-tuple-element.79), channel_id=1, source_target_pairs={{0,7},{1,6},{2,5},{3,4},{4,3},{5,2},{6,1},{7,0},{8,15},{9,14},{10,... | collective-permute-start | bytes 1723400 | tf_op jit(solution)/shard_map/ppermute | solution.py:42
  175.2 29.9 %collective-permute-start.22 = (bf16[68,4224]{1,0:T(8,128)(2,1)S(1)}, bf16[68,4224]{1,0:T(8,128)(2,1)S(1)}, u32[]{:S(2)}, u32[]{:S(2)}) collective-permute-start(bf16[68,4224]{1,0:T(8,128)(2,1)S(1)} %get-tuple-element.77), channel_id=1, source_target_pairs={{0,5},{1,4},{2,7},{3,6},{4,1},{5,0},{6,3},{7,2},{8,13},{9,12},{10,... | collective-permute-start | bytes 1723400 | tf_op jit(solution)/shard_map/ppermute | solution.py:42
  177.4 28.0 %collective-permute-start.24 = (bf16[144,5248]{1,0:T(8,128)(2,1)S(1)}, bf16[144,5248]{1,0:T(8,128)(2,1)S(1)}, u32[]{:S(2)}, u32[]{:S(2)}) collective-permute-start(bf16[144,5248]{1,0:T(8,128)(2,1)S(1)} %copy-done.23), channel_id=1, source_target_pairs={{0,16},{8,24},{16,0},{24,8},{1,17},{9,25},{17,1},{25,9},{2,18},{10... | collective-permute-start | bytes 4534280 | tf_op jit(solution)/shard_map/ppermute | solution.py:31
  178.9 43.3 %collective-permute-start.21 = (bf16[68,4224]{1,0:T(8,128)(2,1)S(1)}, bf16[68,4224]{1,0:T(8,128)(2,1)S(1)}, u32[]{:S(2)}, u32[]{:S(2)}) collective-permute-start(bf16[68,4224]{1,0:T(8,128)(2,1)S(1)} %get-tuple-element.80), channel_id=1, source_target_pairs={{0,3},{1,2},{2,1},{3,0},{4,7},{5,6},{6,5},{7,4},{8,11},{9,10},{10,... | collective-permute-start | bytes 1723400 | tf_op jit(solution)/shard_map/ppermute | solution.py:31
  179.5 45.2 %collective-permute-start.19 = (bf16[68,4224]{1,0:T(8,128)(2,1)S(1)}, bf16[68,4224]{1,0:T(8,128)(2,1)S(1)}, u32[]{:S(2)}, u32[]{:S(2)}) collective-permute-start(bf16[68,4224]{1,0:T(8,128)(2,1)S(1)} %get-tuple-element.78), channel_id=1, source_target_pairs={{0,1},{1,0},{2,3},{3,2},{4,5},{5,4},{6,7},{7,6},{8,9},{9,8},{10,11... | collective-permute-start | bytes 1723400 | tf_op jit(solution)/shard_map/ppermute | solution.py:31
  205.4 1.1 copy-start.9
  217.1 10.1 %collective-permute-start.26 = (bf16[384,1024]{1,0:T(8,128)(2,1)}, bf16[384,1024]{1,0:T(8,128)(2,1)S(1)}, u32[]{:S(2)}, u32[]{:S(2)}) collective-permute-start(bf16[384,1024]{1,0:T(8,128)(2,1)} %get-tuple-element.74), channel_id=1, source_target_pairs={{0,8},{8,0},{16,24},{24,16},{1,9},{9,1},{17,25},{25,17},{2,10},{10... | collective-permute-start | bytes 2359304 | tf_op jit(solution)/shard_map/ppermute | solution.py:31
  217.1 11.2 %collective-permute-start.25 = (bf16[1024,768]{1,0:T(8,128)(2,1)}, bf16[1024,768]{1,0:T(8,128)(2,1)S(1)}, u32[]{:S(2)}, u32[]{:S(2)}) collective-permute-start(bf16[1024,768]{1,0:T(8,128)(2,1)} %get-tuple-element.72), channel_id=1, source_target_pairs={{0,8},{8,0},{16,24},{24,16},{1,9},{9,1},{17,25},{25,17},{2,10},{10... | collective-permute-start | bytes 4718600 | tf_op jit(solution)/shard_map/ppermute | solution.py:31
  225.7 1.5 copy-start.19
  227.2 1.7 copy-start.7
  228.9 1.8 copy-start.1

commit v5 on v4

--- a/solution.py
+++ b/solution.py
@@ -183,7 +183,7 @@
             pltpu.SemaphoreType.DMA((3 + 2 * count, blocks)),
             pltpu.SemaphoreType.DMA((1 + count + count * blocks,)),
         ],
-        compiler_params=pltpu.CompilerParams(vmem_limit_bytes=56 * 1024 * 1024),
+        compiler_params=pltpu.CompilerParams(vmem_limit_bytes=32 * 1024 * 1024),
         name="slot_work",
     )(place, *sum(xs, []), *sum(dys, []), gate_local, up_local, down_local)
     return outs[:count], outs[count], outs[count + 1 :]
@@ -265,9 +265,36 @@
             pltpu.SemaphoreType.DMA((sum(len(pieces) for pieces in cuts),)),
             pltpu.SemaphoreType.DMA((4,)),
         ],
-        compiler_params=pltpu.CompilerParams(vmem_limit_bytes=56 * 1024 * 1024),
+        compiler_params=pltpu.CompilerParams(vmem_limit_bytes=32 * 1024 * 1024),
         name="weight_work",
     )(place, *arrays, *before)
+
+
+def final_kernel(keep_gu, keep_d, came_gu, came_d, gate, up, down):
+    width = gate.shape[1]
+    gate_up = keep_gu[...].astype(F32) + came_gu[...].astype(F32)
+    gate[...] = gate_up[:, :width].astype(BF)
+    up[...] = gate_up[:, width:].astype(BF)
+    down[...] = (keep_d[...].astype(F32) + came_d[...].astype(F32)).astype(BF)
+
+
+def final_sums(keep_gu, keep_d, came_gu, came_d):
+    quarter, width = keep_d.shape[1], keep_d.shape[0]
+    steps = 4
+    high = quarter // steps
+    tall = [pl.BlockSpec((high, 2 * width), lambda i: (i, 0))]
+    wide = [pl.BlockSpec((width, high), lambda i: (0, i))]
+    thin = [pl.BlockSpec((high, width), lambda i: (i, 0))]
+    shapes = [(quarter, width), (quarter, width), (width, quarter)]
+    return pl.pallas_call(
+        final_kernel,
+        grid=(steps,),
+        out_shape=[jax.ShapeDtypeStruct(shape, BF) for shape in shapes],
+        in_specs=(tall + wide) * 2,
+        out_specs=thin * 2 + wide,
+        compiler_params=pltpu.CompilerParams(vmem_limit_bytes=32 * 1024 * 1024),
+        name="final_sums",
+    )(keep_gu, keep_d, came_gu, came_d)
 
 
 def body(tokens, out_grad, gate_prob, expert_ids, w_gate, w_up, w_down):
@@ -406,9 +433,9 @@
     home_x = jnp.concatenate(homes, axis=0)
 
     keep_gu, keep_d, give_gu, give_d = sums
-    gate_up = (keep_gu.astype(F32) + send_xor(give_gu, "dp", 1).astype(F32)).astype(BF)
-    down_w_grad = (keep_d.astype(F32) + send_xor(give_d, "dp", 1).astype(F32)).astype(BF)
-    gate_w_grad, up_w_grad = gate_up[:, :width], gate_up[:, width:]
+    gate_w_grad, up_w_grad, down_w_grad = final_sums(
+        keep_gu, keep_d, send_xor(give_gu, "dp", 1), send_xor(give_d, "dp", 1)
+    )
 
     placer = placer_of(0, expert_count)
     placer = placer.astype(BF)

time: 232 us -> 230 us (level)
  waiting for transfers between devices: 105 us -> 114 us
  Pallas kernels: 52.5 us -> 45.2 us
    pallas_call x2, Pallas kernels: 19.9 us -> 12.3 us  [weight_work(): pl.pallas_call(functools.partial(weight_kernel, cuts, bool(before), width...]
    ppermute x14, waiting for transfers between devices: 45.9 us -> 51.8 us  [send_xor(): return lax.ppermute(value, axis, [(i, i ^ mask) for i in range(size)])]
    ppermute x2, waiting for transfers between devices: 24.3 us -> 27.3 us  [send_home(): lax.ppermute(value, ('expert', 'seq'), [(i, i ^ mask) for i in range(tota...]
    unnamed x48 -> x56, local copies, waits for them, and re-layouts: 7.09 us -> 7.65 us
  transfers between devices with their start and end apart: 27 -> 27, of which waited for: 14 -> 13; matrix products, arithmetic and copies ran while one was open for 5% -> 5% of each run, Pallas kernels for 23% -> 19%
where the time goes in v5:
time: 230 us; the launch traced here: 229 us
  waiting for transfers between devices  114 us (50%)
  starting transfers between devices  48 us (21%)
  Pallas kernels  45.2 us (20%)
  local copies, waits for them, and re-layouts  8.07 us (4%)
  other arithmetic  7.56 us (3%)
  matrix products  5.29 us (2%)
    ppermute x14, waiting for transfers between devices, send_xor(): return lax.ppermute(value, axis, [(i, i ^ mask) for i in range(size)])  51.8 us
    pallas_call x3, Pallas kernels, slot_work(): pl.pallas_call(functools.partial(slot_kernel, blocks, count, choices), ou...  30.8 us
    ppermute x2, waiting for transfers between devices, send_home(): lax.ppermute(value, ('expert', 'seq'), [(i, i ^ mask) for i in range(tota...  27.3 us
    ppermute x1, waiting for transfers between devices, body(): dy_near = lax.ppermute(after(dy_across, dy_first), 'seq', OUTWARD)  18.9 us
    ppermute x14, starting transfers between devices, send_xor(): return lax.ppermute(value, axis, [(i, i ^ mask) for i in range(size)])  14.5 us
    pallas_call x2, Pallas kernels, weight_work(): pl.pallas_call(functools.partial(weight_kernel, cuts, bool(before), width...  12.3 us
    ppermute x1, waiting for transfers between devices, body(): dy_across = lax.ppermute(after(slot_dy[0], across_far), 'seq', MIDDLE)  10.3 us
    unnamed x56, local copies, waits for them, and re-layouts  7.65 us
  transfers between devices with their start and end apart: 27, of which 13 were waited for; matrix products, arithmetic and copies ran while one was open for 5% of the time, Pallas kernels for 19%

profile of v5, /device:TPU:8, one launch (start us, length us, event | category | flops | bytes accessed | tf_op | source)
XLA Modules:
  0.0 229.3 jit_solution(15998593862385765013)
XLA Ops:
  0.7 0.9 fusion.5
  1.6 0.7 convert_add_fusion
  2.3 0.4 convolution_convert_fusion.3
  2.6 1.6 collective-permute-start
  4.2 0.3 convolution_convert_fusion.4
  4.6 3.6 %collective-permute-start.5 = (bf16[68,4096]{1,0:T(8,128)(2,1)S(1)}, bf16[68,4096]{1,0:T(8,128)(2,1)}, u32[]{:S(2)}, u32[]{:S(2)}) collective-permute-start(bf16[68,4096]{1,0:T(8,128)(2,1)S(1)} %convolution_convert_fusion.4), channel_id=1, source_target_pairs={{1,2},{2,1},{5,6},{6,5},{9,10},{10,9},{13,14},{14,13},{17,18},{18,... | collective-permute-start | bytes 1671176 | tf_op jit(solution)/shard_map/ppermute | solution.py:366
  8.3 1.2 convolution_convert_fusion.1
  9.5 8.4 %collective-permute-done = bf16[68,4096]{1,0:T(8,128)(2,1)} collective-permute-done((bf16[68,4096]{1,0:T(8,128)(2,1)S(1)}, bf16[68,4096]{1,0:T(8,128)(2,1)}, u32[]{:S(2)}, u32[]{:S(2)}) %collective-permute-start) | collective-permute-done | bytes 557088 | tf_op jit(solution)/shard_map/ppermute | solution.py:31
  17.9 1.5 collective-permute-start.3
  19.5 0.3 convolution_convert_fusion.2
  19.8 3.5 %collective-permute-start.6 = (bf16[68,4096]{1,0:T(8,128)(2,1)}, bf16[68,4096]{1,0:T(8,128)(2,1)S(1)}, u32[]{:S(2)}, u32[]{:S(2)}) collective-permute-start(bf16[68,4096]{1,0:T(8,128)(2,1)} %collective-permute-done), channel_id=1, source_target_pairs={{1,2},{2,1},{5,6},{6,5},{9,10},{10,9},{13,14},{14,13},{17,18},{18,... | collective-permute-start | bytes 1671176 | tf_op jit(solution)/shard_map/ppermute | solution.py:368
  23.4 1.3 fusion.12
  24.7 7.6 %collective-permute-done.3 = bf16[68,4096]{1,0:T(8,128)(2,1)S(1)} collective-permute-done((bf16[68,4096]{1,0:T(8,128)(2,1)}, bf16[68,4096]{1,0:T(8,128)(2,1)S(1)}, u32[]{:S(2)}, u32[]{:S(2)}) %collective-permute-start.3) | collective-permute-done | bytes 557088 | tf_op jit(solution)/shard_map/ppermute | solution.py:31
  32.5 0.6 collective-permute-start.4
  33.5 1.5 collective-permute-start.13
  34.9 0.9 collective-permute-done.6
  35.8 1.4 pad_maximum_fusion.3.refs_1_
  37.2 2.6 %collective-permute-done.2 = bf16[68,4096]{1,0:T(8,128)(2,1)S(1)} collective-permute-done((bf16[68,4096]{1,0:T(8,128)(2,1)}, bf16[68,4096]{1,0:T(8,128)(2,1)S(1)}, u32[]{:S(2)}, u32[]{:S(2)}) %collective-permute-start.2) | collective-permute-done | bytes 557088 | tf_op jit(solution)/shard_map/ppermute | solution.py:31
  39.8 1.4 pad_maximum_fusion.2.refs_1_
  41.2 2.4 %collective-permute-start.7 = (bf16[136,4096]{1,0:T(8,128)(2,1)S(1)}, bf16[136,4096]{1,0:T(8,128)(2,1)S(1)}, u32[]{:S(2)}, u32[]{:S(2)}) collective-permute-start(bf16[136,4096]{1,0:T(8,128)(2,1)S(1)} %pad_maximum_fusion.2.refs_1_), channel_id=1, source_target_pairs={{1,2},{2,1},{5,6},{6,5},{9,10},{10,9},{13,14},{14,13},{17,18},{18,... | collective-permute-start | bytes 3342344 | tf_op jit(solution)/shard_map/ppermute | solution.py:380
  43.6 1.4 collective-permute-start.8
  45.0 3.7 %collective-permute-start.10 = (bf16[136,4096]{1,0:T(8,128)(2,1)S(1)}, bf16[136,4096]{1,0:T(8,128)(2,1)S(1)}, u32[]{:S(2)}, u32[]{:S(2)}) collective-permute-start(bf16[136,4096]{1,0:T(8,128)(2,1)S(1)} %pad_maximum_fusion.1.refs_2_), channel_id=1, source_target_pairs={{1,2},{2,1},{5,6},{6,5},{9,10},{10,9},{13,14},{14,13},{17,18},{18,... | collective-permute-start | bytes 3342344 | tf_op jit(solution)/shard_map/ppermute | solution.py:370
  48.6 1.2 pad_maximum_fusion.refs_0_
  49.9 11.4 %collective-permute-done.4.refs_3_ = bf16[136,4096]{1,0:T(8,128)(2,1)S(1)} collective-permute-done((bf16[136,4096]{1,0:T(8,128)(2,1)S(1)}, bf16[136,4096]{1,0:T(8,128)(2,1)S(1)}, u32[]{:S(2)}, u32[]{:S(2)}) %collective-permute-start.4) | collective-permute-done | bytes 1114144 | tf_op jit(solution)/shard_map/ppermute | solution.py:31
  61.3 13.5 %slot_work.3 = (bf16[136,4224]{1,0:T(8,128)(2,1)S(1)}, bf16[136,4224]{1,0:T(8,128)(2,1)S(1)}, bf16[144,6400]{1,0:T(8,128)(2,1)S(1)}, bf16[144,5248]{1,0:T(8,128)(2,1)S(1)}, bf16[144,5248]{1,0:T(8,128)(2,1)S(1)}) custom-call(s32[3]{0:T(128)S(1)} %pad_add_fusion.place, bf16[136,4096]{1,0:T(8,128)(2,1)S(1)} %pad_maximum_fusion.refs_0_, ...), custom_call_target="tpu_custom_call" | custom-call | tf_op jit(solution)/shard_map/slot_work/pallas_call | solution.py:167
  74.7 1.0 copy-done.13
  75.8 1.1 copy-done.11
  76.8 1.5 collective-permute-start.14
  78.3 10.3 %collective-permute-done.10.refs_3_ = bf16[136,4096]{1,0:T(8,128)(2,1)S(1)} collective-permute-done((bf16[136,4096]{1,0:T(8,128)(2,1)S(1)}, bf16[136,4096]{1,0:T(8,128)(2,1)S(1)}, u32[]{:S(2)}, u32[]{:S(2)}) %collective-permute-start.10) | collective-permute-done | bytes 1114144 | tf_op jit(solution)/shard_map/ppermute | solution.py:370
  88.6 1.3 collective-permute-start.11
  90.0 1.1 copy-done.15
  91.0 3.5 %collective-permute-start.12 = (bf16[136,4096]{1,0:T(8,128)(2,1)S(1)}, bf16[136,4096]{1,0:T(8,128)(2,1)S(1)}, u32[]{:S(2)}, u32[]{:S(2)}) collective-permute-start(bf16[136,4096]{1,0:T(8,128)(2,1)S(1)} %collective-permute-done.4.refs_3_), channel_id=1, source_target_pairs={{1,2},{2,1},{5,6},{6,5},{9,10},{10,9},{13,14},{14,13},{17,18},{18,... | collective-permute-start | bytes 3342344 | tf_op jit(solution)/shard_map/ppermute | solution.py:382
  94.6 1.5 collective-permute-start.9
  96.1 18.9 %collective-permute-done.11.refs_2_ = bf16[136,4096]{1,0:T(8,128)(2,1)S(1)} collective-permute-done((bf16[136,4096]{1,0:T(8,128)(2,1)S(1)}, bf16[136,4096]{1,0:T(8,128)(2,1)S(1)}, u32[]{:S(2)}, u32[]{:S(2)}) %collective-permute-start.11) | collective-permute-done | bytes 1114144 | tf_op jit(solution)/shard_map/ppermute | solution.py:383
  114.9 8.4 %slot_work.4 = (bf16[136,4224]{1,0:T(8,128)(2,1)}, bf16[144,5248]{1,0:T(8,128)(2,1)S(1)}, bf16[144,5248]{1,0:T(8,128)(2,1)S(1)}) custom-call(s32[3]{0:T(128)S(1)} %pad_add_fusion.place, bf16[136,4096]{1,0:T(8,128)(2,1)S(1)} %collective-permute-done.8.refs_0_, bf16[136,4096]{1,0:T(8,128)(2,1)S(1)} %collective-permute-done.7.refs_1_, ...), custom_call_target="tpu_custom_call" | custom-call | tf_op jit(solution)/shard_map/slot_work/pallas_call | solution.py:167
  123.4 1.6 collective-permute-start.15
  125.0 1.4 copy-done.6
  126.3 5.7 %weight_work.2 = (bf16[1024,768]{1,0:T(8,128)(2,1)S(1)}, bf16[384,1024]{1,0:T(8,128)(2,1)S(1)}, bf16[1024,768]{1,0:T(8,128)(2,1)S(1)}, bf16[384,1024]{1,0:T(8,128)(2,1)S(1)}) custom-call(s32[3]{0:T(128)S(1)} %pad_add_fusion.place, bf16[144,5248]{1,0:T(8,128)(2,1)S(1)} %get-tuple-element.63.refs_0_, bf16[144,5248]{1,0:T(8,128)(2,1)S(1)} %copy-done.6, ...), custom_call_target="tpu_custom_call" | custom-call | tf_op jit(solution)/shard_map/weight_work/pallas_call | solution.py:256
  132.1 0.9 copy-done.21
  133.0 0.9 copy-done.23
  133.9 3.6 %collective-permute-start.18 = (bf16[136,4224]{1,0:T(8,128)(2,1)}, bf16[136,4224]{1,0:T(8,128)(2,1)S(1)}, u32[]{:S(2)}, u32[]{:S(2)}) collective-permute-start(bf16[136,4224]{1,0:T(8,128)(2,1)} %get-tuple-element.66), channel_id=1, source_target_pairs={{1,2},{2,1},{5,6},{6,5},{9,10},{10,9},{13,14},{14,13},{17,18},{18,... | collective-permute-start | bytes 3446792 | tf_op jit(solution)/shard_map/ppermute | solution.py:406
  137.5 1.7 collective-permute-start.17
  139.4 1.8 collective-permute-start.16
  141.2 1.3 collective-permute-start.20
  142.4 8.2 %collective-permute-done.16 = bf16[68,4224]{1,0:T(8,128)(2,1)S(1)} collective-permute-done((bf16[68,4224]{1,0:T(8,128)(2,1)S(1)}, bf16[68,4224]{1,0:T(8,128)(2,1)S(1)}, u32[]{:S(2)}, u32[]{:S(2)}) %collective-permute-start.16) | collective-permute-done | bytes 574496 | tf_op jit(solution)/shard_map/ppermute | solution.py:31
  150.7 1.7 collective-permute-done.15.refs_1_
  152.4 4.6 %collective-permute-done.17.refs_2_ = bf16[136,4096]{1,0:T(8,128)(2,1)S(1)} collective-permute-done((bf16[136,4096]{1,0:T(8,128)(2,1)S(1)}, bf16[136,4096]{1,0:T(8,128)(2,1)S(1)}, u32[]{:S(2)}, u32[]{:S(2)}) %collective-permute-start.17) | collective-permute-done | bytes 1114144 | tf_op jit(solution)/shard_map/ppermute | solution.py:386
  157.0 1.2 copy-done.20
  158.3 8.9 %slot_work.5 = (bf16[136,4224]{1,0:T(8,128)(2,1)S(1)}, bf16[144,5248]{1,0:T(8,128)(2,1)S(1)}, bf16[144,5248]{1,0:T(8,128)(2,1)S(1)}) custom-call(s32[3]{0:T(128)S(1)} %pad_add_fusion.place, bf16[136,4096]{1,0:T(8,128)(2,1)S(1)} %copy-done.20, bf16[136,4096]{1,0:T(8,128)(2,1)S(1)} %pad_maximum_fusion.3.refs_1_, ...), custom_call_target="tpu_custom_call" | custom-call | tf_op jit(solution)/shard_map/slot_work/pallas_call | solution.py:167
  167.2 0.3 add_convert_fusion.1
  167.7 0.3 add_convert_fusion
  168.1 5.1 %collective-permute-start.23 = (bf16[68,4224]{1,0:T(8,128)(2,1)S(1)}, bf16[68,4224]{1,0:T(8,128)(2,1)S(1)}, u32[]{:S(2)}, u32[]{:S(2)}) collective-permute-start(bf16[68,4224]{1,0:T(8,128)(2,1)S(1)} %get-tuple-element.83), channel_id=1, source_target_pairs={{0,7},{1,6},{2,5},{3,4},{4,3},{5,2},{6,1},{7,0},{8,15},{9,14},{10,... | collective-permute-start | bytes 1723400 | tf_op jit(solution)/shard_map/ppermute | solution.py:42
  173.3 1.0 collective-permute-start.22
  174.3 1.5 collective-permute-start.24
  175.9 2.2 collective-permute-start.19
  178.0 27.3 %collective-permute-done.23 = bf16[68,4224]{1,0:T(8,128)(2,1)S(1)} collective-permute-done((bf16[68,4224]{1,0:T(8,128)(2,1)S(1)}, bf16[68,4224]{1,0:T(8,128)(2,1)S(1)}, u32[]{:S(2)}, u32[]{:S(2)}) %collective-permute-start.23) | collective-permute-done | bytes 574496 | tf_op jit(solution)/shard_map/ppermute | solution.py:42
  205.4 0.2 add_convert_fusion.2
  205.7 6.5 %weight_work.3 = (bf16[1024,768]{1,0:T(8,128)(2,1)S(1)}, bf16[384,1024]{1,0:T(8,128)(2,1)S(1)}, bf16[1024,768]{1,0:T(8,128)(2,1)S(1)}, bf16[384,1024]{1,0:T(8,128)(2,1)S(1)}) custom-call(s32[3]{0:T(128)S(1)} %pad_add_fusion.place, bf16[144,5248]{1,0:T(8,128)(2,1)S(1)} %copy-done.8, bf16[144,5248]{1,0:T(8,128)(2,1)S(1)} %copy-done.10, ...), custom_call_target="tpu_custom_call" | custom-call | tf_op jit(solution)/shard_map/weight_work/pallas_call | solution.py:256
  212.3 0.5 collective-permute-start.25
  212.8 8.3 %collective-permute-done.21 = bf16[68,4224]{1,0:T(8,128)(2,1)S(1)} collective-permute-done((bf16[68,4224]{1,0:T(8,128)(2,1)S(1)}, bf16[68,4224]{1,0:T(8,128)(2,1)S(1)}, u32[]{:S(2)}, u32[]{:S(2)}) %collective-permute-start.21) | collective-permute-done | bytes 574496 | tf_op jit(solution)/shard_map/ppermute | solution.py:31
  221.1 3.6 %collective-permute-done.19 = bf16[68,4224]{1,0:T(8,128)(2,1)S(1)} collective-permute-done((bf16[68,4224]{1,0:T(8,128)(2,1)S(1)}, bf16[68,4224]{1,0:T(8,128)(2,1)S(1)}, u32[]{:S(2)}, u32[]{:S(2)}) %collective-permute-start.19) | collective-permute-done | bytes 574496 | tf_op jit(solution)/shard_map/ppermute | solution.py:31
  224.9 0.7 fusion.7
  225.6 1.5 convolution_convert_fusion
  227.1 2.2 final_sums.1
  (76 shorter events, 1.7 us)
Async XLA Ops:
  0.6 1.6 copy-start
  2.6 5.7 %copy-start.25 = (bf16[128,4096]{1,0:T(8,128)(2,1)S(1)}, bf16[128,4096]{1,0:T(8,128)(2,1)}, u32[]{:S(2)}) copy-start(bf16[128,4096]{1,0:T(8,128)(2,1)} %param.8) | copy-start | bytes 3145732
  2.6 5.7 %copy-start.27 = (bf16[128]{0:T(256)(128)(2,1)S(1)}, bf16[128]{0:T(256)(128)(2,1)}, u32[]{:S(2)}) copy-start(bf16[128]{0:T(256)(128)(2,1)} %param.9) | copy-start | bytes 772
  2.6 15.2 %collective-permute-start = (bf16[68,4096]{1,0:T(8,128)(2,1)S(1)}, bf16[68,4096]{1,0:T(8,128)(2,1)}, u32[]{:S(2)}, u32[]{:S(2)}) collective-permute-start(bf16[68,4096]{1,0:T(8,128)(2,1)S(1)} %convolution_convert_fusion.3), channel_id=1, source_target_pairs={{0,4},{4,0},{1,5},{5,1},{2,6},{6,2},{3,7},{7,3},{8,12},{12,8},{9,1... | collective-permute-start | bytes 1671176 | tf_op jit(solution)/shard_map/ppermute | solution.py:31
  4.6 14.9 %copy-start.26 = (bf16[128,4096]{1,0:T(8,128)(2,1)S(1)}, bf16[128,4096]{1,0:T(8,128)(2,1)}, u32[]{:S(2)}) copy-start(bf16[128,4096]{1,0:T(8,128)(2,1)} %param.8) | copy-start | bytes 3145732
  4.6 28.9 %collective-permute-start.5 = (bf16[68,4096]{1,0:T(8,128)(2,1)S(1)}, bf16[68,4096]{1,0:T(8,128)(2,1)}, u32[]{:S(2)}, u32[]{:S(2)}) collective-permute-start(bf16[68,4096]{1,0:T(8,128)(2,1)S(1)} %convolution_convert_fusion.4), channel_id=1, source_target_pairs={{1,2},{2,1},{5,6},{6,5},{9,10},{10,9},{13,14},{14,13},{17,18},{18,... | collective-permute-start | bytes 1671176 | tf_op jit(solution)/shard_map/ppermute | solution.py:366
  8.2 29.0 %collective-permute-start.1 = (bf16[68,4096]{1,0:T(8,128)(2,1)S(1)}, bf16[68,4096]{1,0:T(8,128)(2,1)}, u32[]{:S(2)}, u32[]{:S(2)}) collective-permute-start(bf16[68,4096]{1,0:T(8,128)(2,1)S(1)} %convolution_convert_fusion.4), channel_id=1, source_target_pairs={{0,1},{1,0},{2,3},{3,2},{4,5},{5,4},{6,7},{7,6},{8,9},{9,8},{10,11... | collective-permute-start | bytes 1671176 | tf_op jit(solution)/shard_map/ppermute | solution.py:31
  17.9 14.4 %collective-permute-start.3 = (bf16[68,4096]{1,0:T(8,128)(2,1)}, bf16[68,4096]{1,0:T(8,128)(2,1)S(1)}, u32[]{:S(2)}, u32[]{:S(2)}) collective-permute-start(bf16[68,4096]{1,0:T(8,128)(2,1)} %convolution_convert_fusion.1), channel_id=1, source_target_pairs={{0,4},{4,0},{1,5},{5,1},{2,6},{6,2},{3,7},{7,3},{8,12},{12,8},{9,1... | collective-permute-start | bytes 1671176 | tf_op jit(solution)/shard_map/ppermute | solution.py:31
  19.8 16.0 %collective-permute-start.6 = (bf16[68,4096]{1,0:T(8,128)(2,1)}, bf16[68,4096]{1,0:T(8,128)(2,1)S(1)}, u32[]{:S(2)}, u32[]{:S(2)}) collective-permute-start(bf16[68,4096]{1,0:T(8,128)(2,1)} %collective-permute-done), channel_id=1, source_target_pairs={{1,2},{2,1},{5,6},{6,5},{9,10},{10,9},{13,14},{14,13},{17,18},{18,... | collective-permute-start | bytes 1671176 | tf_op jit(solution)/shard_map/ppermute | solution.py:368
  23.3 16.5 %collective-permute-start.2 = (bf16[68,4096]{1,0:T(8,128)(2,1)}, bf16[68,4096]{1,0:T(8,128)(2,1)S(1)}, u32[]{:S(2)}, u32[]{:S(2)}) collective-permute-start(bf16[68,4096]{1,0:T(8,128)(2,1)} %collective-permute-done), channel_id=1, source_target_pairs={{0,1},{1,0},{2,3},{3,2},{4,5},{5,4},{6,7},{7,6},{8,9},{9,8},{10,11... | collective-permute-start | bytes 1671176 | tf_op jit(solution)/shard_map/ppermute | solution.py:31
  32.5 28.8 %collective-permute-start.4 = (bf16[136,4096]{1,0:T(8,128)(2,1)S(1)}, bf16[136,4096]{1,0:T(8,128)(2,1)S(1)}, u32[]{:S(2)}, u32[]{:S(2)}) collective-permute-start(bf16[136,4096]{1,0:T(8,128)(2,1)S(1)} %pad_maximum_fusion.1.refs_2_), channel_id=1, source_target_pairs={{0,1},{1,0},{2,3},{3,2},{4,5},{5,4},{6,7},{7,6},{8,9},{9,8},{10,11... | collective-permute-start | bytes 3342344 | tf_op jit(solution)/shard_map/ppermute | solution.py:31
  33.1 28.2 %copy-start.4 = (bf16[1,384,4096]{2,1,0:T(8,128)(2,1)S(1)}, bf16[1,384,4096]{2,1,0:T(8,128)(2,1)}, u32[]{:S(2)}) copy-start(bf16[1,384,4096]{2,1,0:T(8,128)(2,1)} %param.13) | copy-start | bytes 9437188
  33.5 42.3 %collective-permute-start.13 = (bf16[144,4096]{1,0:T(8,128)(2,1)S(1)}, bf16[144,4096]{1,0:T(8,128)(2,1)S(1)}, u32[]{:S(2)}, u32[]{:S(2)}) collective-permute-start(bf16[144,4096]{1,0:T(8,128)(2,1)S(1)} %fusion.2), channel_id=1, source_target_pairs={{0,16},{8,24},{16,0},{24,8},{1,17},{9,25},{17,1},{25,9},{2,18},{10... | collective-permute-start | bytes 3538952 | tf_op jit(solution)/shard_map/ppermute | solution.py:31
  35.8 25.4 %copy-start.3 = (bf16[1,4096,384]{2,1,0:T(8,128)(2,1)S(1)}, bf16[1,4096,384]{2,1,0:T(8,128)(2,1)}, u32[]{:S(2)}) copy-start(bf16[1,4096,384]{2,1,0:T(8,128)(2,1)} %param.12) | copy-start | bytes 9437188
  39.8 21.4 %copy-start.2 = (bf16[1,4096,384]{2,1,0:T(8,128)(2,1)S(1)}, bf16[1,4096,384]{2,1,0:T(8,128)(2,1)}, u32[]{:S(2)}) copy-start(bf16[1,4096,384]{2,1,0:T(8,128)(2,1)} %param.11) | copy-start | bytes 9437188
  41.2 53.3 %collective-permute-start.7 = (bf16[136,4096]{1,0:T(8,128)(2,1)S(1)}, bf16[136,4096]{1,0:T(8,128)(2,1)S(1)}, u32[]{:S(2)}, u32[]{:S(2)}) collective-permute-start(bf16[136,4096]{1,0:T(8,128)(2,1)S(1)} %pad_maximum_fusion.2.refs_1_), channel_id=1, source_target_pairs={{1,2},{2,1},{5,6},{6,5},{9,10},{10,9},{13,14},{14,13},{17,18},{18,... | collective-permute-start | bytes 3342344 | tf_op jit(solution)/shard_map/ppermute | solution.py:380
  43.6 51.0 %collective-permute-start.8 = (bf16[136,4096]{1,0:T(8,128)(2,1)S(1)}, bf16[136,4096]{1,0:T(8,128)(2,1)S(1)}, u32[]{:S(2)}, u32[]{:S(2)}) collective-permute-start(bf16[136,4096]{1,0:T(8,128)(2,1)S(1)} %pad_maximum_fusion.3.refs_1_), channel_id=1, source_target_pairs={{1,0},{2,3},{5,4},{6,7},{9,8},{10,11},{13,12},{14,15},{17,16},{18,... | collective-permute-start | bytes 3342344 | tf_op jit(solution)/shard_map/ppermute | solution.py:381
  45.0 43.7 %collective-permute-start.10 = (bf16[136,4096]{1,0:T(8,128)(2,1)S(1)}, bf16[136,4096]{1,0:T(8,128)(2,1)S(1)}, u32[]{:S(2)}, u32[]{:S(2)}) collective-permute-start(bf16[136,4096]{1,0:T(8,128)(2,1)S(1)} %pad_maximum_fusion.1.refs_2_), channel_id=1, source_target_pairs={{1,2},{2,1},{5,6},{6,5},{9,10},{10,9},{13,14},{14,13},{17,18},{18,... | collective-permute-start | bytes 3342344 | tf_op jit(solution)/shard_map/ppermute | solution.py:370
  74.7 1.0 copy-start.13
  75.8 47.6 %copy-start.5 = (bf16[144,5248]{1,0:T(8,128)(2,1)}, bf16[144,5248]{1,0:T(8,128)(2,1)S(1)}, u32[]{:S(2)}) copy-start(bf16[144,5248]{1,0:T(8,128)(2,1)S(1)} %get-tuple-element.64.refs_1_) | copy-start | bytes 4534276
  75.8 1.1 copy-start.11
  76.8 46.5 %collective-permute-start.14 = (bf16[144,6400]{1,0:T(8,128)(2,1)S(1)}, bf16[144,6400]{1,0:T(8,128)(2,1)S(1)}, u32[]{:S(2)}, u32[]{:S(2)}) collective-permute-start(bf16[144,6400]{1,0:T(8,128)(2,1)S(1)} %get-tuple-element.56), channel_id=1, source_target_pairs={{0,16},{8,24},{16,0},{24,8},{1,17},{9,25},{17,1},{25,9},{2,18},{10... | collective-permute-start | bytes 5529608 | tf_op jit(solution)/shard_map/ppermute | solution.py:31
  88.6 26.3 %collective-permute-start.11 = (bf16[136,4096]{1,0:T(8,128)(2,1)S(1)}, bf16[136,4096]{1,0:T(8,128)(2,1)S(1)}, u32[]{:S(2)}, u32[]{:S(2)}) collective-permute-start(bf16[136,4096]{1,0:T(8,128)(2,1)S(1)} %collective-permute-done.10.refs_3_), channel_id=1, source_target_pairs={{1,0},{2,3},{5,4},{6,7},{9,8},{10,11},{13,12},{14,15},{17,16},{18,... | collective-permute-start | bytes 3342344 | tf_op jit(solution)/shard_map/ppermute | solution.py:383
  90.0 1.1 copy-start.15
  91.0 23.9 %collective-permute-start.12 = (bf16[136,4096]{1,0:T(8,128)(2,1)S(1)}, bf16[136,4096]{1,0:T(8,128)(2,1)S(1)}, u32[]{:S(2)}, u32[]{:S(2)}) collective-permute-start(bf16[136,4096]{1,0:T(8,128)(2,1)S(1)} %collective-permute-done.4.refs_3_), channel_id=1, source_target_pairs={{1,2},{2,1},{5,6},{6,5},{9,10},{10,9},{13,14},{14,13},{17,18},{18,... | collective-permute-start | bytes 3342344 | tf_op jit(solution)/shard_map/ppermute | solution.py:382
  94.6 30.4 %copy-start.12 = (bf16[144,4096]{1,0:T(8,128)(2,1)S(1)}, bf16[144,4096]{1,0:T(8,128)(2,1)}, u32[]{:S(2)}) copy-start(bf16[144,4096]{1,0:T(8,128)(2,1)} %copy-done.11) | copy-start | bytes 3538948
  94.6 39.3 %collective-permute-start.9 = (bf16[136,4096]{1,0:T(8,128)(2,1)S(1)}, bf16[136,4096]{1,0:T(8,128)(2,1)S(1)}, u32[]{:S(2)}, u32[]{:S(2)}) collective-permute-start(bf16[136,4096]{1,0:T(8,128)(2,1)S(1)} %collective-permute-done.7.refs_1_), channel_id=1, source_target_pairs={{1,0},{2,3},{5,4},{6,7},{9,8},{10,11},{13,12},{14,15},{17,16},{18,... | collective-permute-start | bytes 3342344 | tf_op jit(solution)/shard_map/ppermute | solution.py:385
  114.9 8.4 %copy-start.17 = (bf16[136,4096]{1,0:T(8,128)(2,1)}, bf16[136,4096]{1,0:T(8,128)(2,1)S(1)}, u32[]{:S(2)}) copy-start(bf16[136,4096]{1,0:T(8,128)(2,1)S(1)} %collective-permute-done.12.refs_3_) | copy-start | bytes 3342340
  123.4 8.7 %copy-start.7 = (bf16[144,5248]{1,0:T(8,128)(2,1)}, bf16[144,5248]{1,0:T(8,128)(2,1)S(1)}, u32[]{:S(2)}) copy-start(bf16[144,5248]{1,0:T(8,128)(2,1)S(1)} %get-tuple-element.67.refs_0_) | copy-start | bytes 4534276
  123.4 29.0 %collective-permute-start.15 = (bf16[144,5248]{1,0:T(8,128)(2,1)S(1)}, bf16[144,5248]{1,0:T(8,128)(2,1)S(1)}, u32[]{:S(2)}, u32[]{:S(2)}) collective-permute-start(bf16[144,5248]{1,0:T(8,128)(2,1)S(1)} %get-tuple-element.57), channel_id=1, source_target_pairs={{0,16},{8,24},{16,0},{24,8},{1,17},{9,25},{17,1},{25,9},{2,18},{10... | collective-permute-start | bytes 4534280 | tf_op jit(solution)/shard_map/ppermute | solution.py:31
  124.9 1.4 copy-start.6
  126.3 11.1 %copy-start.18 = (bf16[136,4096]{1,0:T(8,128)(2,1)S(1)}, bf16[136,4096]{1,0:T(8,128)(2,1)}, u32[]{:S(2)}) copy-start(bf16[136,4096]{1,0:T(8,128)(2,1)} %copy-done.17) | copy-start | bytes 3342340
  132.1 0.9 copy-start.21
  133.0 0.9 copy-start.23
  133.9 23.2 %copy-start.16 = (bf16[136,4096]{1,0:T(8,128)(2,1)S(1)}, bf16[136,4096]{1,0:T(8,128)(2,1)}, u32[]{:S(2)}) copy-start(bf16[136,4096]{1,0:T(8,128)(2,1)} %copy-done.15) | copy-start | bytes 3342340
  133.9 18.5 %copy-start.19 = (bf16[136,4096]{1,0:T(8,128)(2,1)}, bf16[136,4096]{1,0:T(8,128)(2,1)S(1)}, u32[]{:S(2)}) copy-start(bf16[136,4096]{1,0:T(8,128)(2,1)S(1)} %collective-permute-done.9.refs_0_) | copy-start | bytes 3342340
  133.9 33.3 %collective-permute-start.18 = (bf16[136,4224]{1,0:T(8,128)(2,1)}, bf16[136,4224]{1,0:T(8,128)(2,1)S(1)}, u32[]{:S(2)}, u32[]{:S(2)}) collective-permute-start(bf16[136,4224]{1,0:T(8,128)(2,1)} %get-tuple-element.66), channel_id=1, source_target_pairs={{1,2},{2,1},{5,6},{6,5},{9,10},{10,9},{13,14},{14,13},{17,18},{18,... | collective-permute-start | bytes 3446792 | tf_op jit(solution)/shard_map/ppermute | solution.py:406
  137.5 19.6 %collective-permute-start.17 = (bf16[136,4096]{1,0:T(8,128)(2,1)S(1)}, bf16[136,4096]{1,0:T(8,128)(2,1)S(1)}, u32[]{:S(2)}, u32[]{:S(2)}) collective-permute-start(bf16[136,4096]{1,0:T(8,128)(2,1)S(1)} %copy-done.18), channel_id=1, source_target_pairs={{1,0},{2,3},{5,4},{6,7},{9,8},{10,11},{13,12},{14,15},{17,16},{18,... | collective-permute-start | bytes 3342344 | tf_op jit(solution)/shard_map/ppermute | solution.py:386
  139.3 27.9 %copy-start.14 = (bf16[136,4224]{1,0:T(8,128)(2,1)S(1)}, bf16[136,4224]{1,0:T(8,128)(2,1)}, u32[]{:S(2)}) copy-start(bf16[136,4224]{1,0:T(8,128)(2,1)} %copy-done.13) | copy-start | bytes 3446788
  139.4 11.3 %collective-permute-start.16 = (bf16[68,4224]{1,0:T(8,128)(2,1)S(1)}, bf16[68,4224]{1,0:T(8,128)(2,1)S(1)}, u32[]{:S(2)}, u32[]{:S(2)}) collective-permute-start(bf16[68,4224]{1,0:T(8,128)(2,1)S(1)} %slice.44), channel_id=1, source_target_pairs={{0,4},{4,0},{1,5},{5,1},{2,6},{6,2},{3,7},{7,3},{8,12},{12,8},{9,1... | collective-permute-start | bytes 1723400 | tf_op jit(solution)/shard_map/ppermute | solution.py:31
  141.2 26.5 %collective-permute-start.20 = (bf16[136,4224]{1,0:T(8,128)(2,1)}, bf16[136,4224]{1,0:T(8,128)(2,1)S(1)}, u32[]{:S(2)}, u32[]{:S(2)}) collective-permute-start(bf16[136,4224]{1,0:T(8,128)(2,1)} %get-tuple-element.66), channel_id=1, source_target_pairs={{0,1},{3,2},{4,5},{7,6},{8,9},{11,10},{12,13},{15,14},{16,17},{19,... | collective-permute-start | bytes 3446792 | tf_op jit(solution)/shard_map/ppermute | solution.py:407
  152.4 14.8 %copy-start.9 = (bf16[144,5248]{1,0:T(8,128)(2,1)}, bf16[144,5248]{1,0:T(8,128)(2,1)S(1)}, u32[]{:S(2)}) copy-start(bf16[144,5248]{1,0:T(8,128)(2,1)S(1)} %collective-permute-done.15.refs_1_) | copy-start | bytes 4534276
  157.0 1.2 copy-start.20
  167.9 37.7 %copy-start.10 = (bf16[144,5248]{1,0:T(8,128)(2,1)S(1)}, bf16[144,5248]{1,0:T(8,128)(2,1)}, u32[]{:S(2)}) copy-start(bf16[144,5248]{1,0:T(8,128)(2,1)} %copy-done.9) | copy-start | bytes 4534276
  167.9 37.7 %copy-start.24 = (bf16[384,1024]{1,0:T(8,128)(2,1)S(1)}, bf16[384,1024]{1,0:T(8,128)(2,1)}, u32[]{:S(2)}) copy-start(bf16[384,1024]{1,0:T(8,128)(2,1)} %copy-done.23) | copy-start | bytes 2359300
  168.1 37.3 %collective-permute-start.23 = (bf16[68,4224]{1,0:T(8,128)(2,1)S(1)}, bf16[68,4224]{1,0:T(8,128)(2,1)S(1)}, u32[]{:S(2)}, u32[]{:S(2)}) collective-permute-start(bf16[68,4224]{1,0:T(8,128)(2,1)S(1)} %get-tuple-element.83), channel_id=1, source_target_pairs={{0,7},{1,6},{2,5},{3,4},{4,3},{5,2},{6,1},{7,0},{8,15},{9,14},{10,... | collective-permute-start | bytes 1723400 | tf_op jit(solution)/shard_map/ppermute | solution.py:42
  173.3 32.1 %collective-permute-start.22 = (bf16[68,4224]{1,0:T(8,128)(2,1)S(1)}, bf16[68,4224]{1,0:T(8,128)(2,1)S(1)}, u32[]{:S(2)}, u32[]{:S(2)}) collective-permute-start(bf16[68,4224]{1,0:T(8,128)(2,1)S(1)} %get-tuple-element.81), channel_id=1, source_target_pairs={{0,5},{1,4},{2,7},{3,6},{4,1},{5,0},{6,3},{7,2},{8,13},{9,12},{10,... | collective-permute-start | bytes 1723400 | tf_op jit(solution)/shard_map/ppermute | solution.py:42
  174.3 31.3 %collective-permute-start.24 = (bf16[144,5248]{1,0:T(8,128)(2,1)S(1)}, bf16[144,5248]{1,0:T(8,128)(2,1)S(1)}, u32[]{:S(2)}, u32[]{:S(2)}) collective-permute-start(bf16[144,5248]{1,0:T(8,128)(2,1)S(1)} %get-tuple-element.70), channel_id=1, source_target_pairs={{0,16},{8,24},{16,0},{24,8},{1,17},{9,25},{17,1},{25,9},{2,18},{10... | collective-permute-start | bytes 4534280 | tf_op jit(solution)/shard_map/ppermute | solution.py:31
  175.8 45.3 %collective-permute-start.21 = (bf16[68,4224]{1,0:T(8,128)(2,1)S(1)}, bf16[68,4224]{1,0:T(8,128)(2,1)S(1)}, u32[]{:S(2)}, u32[]{:S(2)}) collective-permute-start(bf16[68,4224]{1,0:T(8,128)(2,1)S(1)} %get-tuple-element.84), channel_id=1, source_target_pairs={{0,3},{1,2},{2,1},{3,0},{4,7},{5,6},{6,5},{7,4},{8,11},{9,10},{10,... | collective-permute-start | bytes 1723400 | tf_op jit(solution)/shard_map/ppermute | solution.py:31
  175.9 29.8 %copy-start.8 = (bf16[144,5248]{1,0:T(8,128)(2,1)S(1)}, bf16[144,5248]{1,0:T(8,128)(2,1)}, u32[]{:S(2)}) copy-start(bf16[144,5248]{1,0:T(8,128)(2,1)} %copy-done.7) | copy-start | bytes 4534276
  175.9 29.8 %copy-start.22 = (bf16[384,1024]{1,0:T(8,128)(2,1)S(1)}, bf16[384,1024]{1,0:T(8,128)(2,1)}, u32[]{:S(2)}) copy-start(bf16[384,1024]{1,0:T(8,128)(2,1)} %copy-done.21) | copy-start | bytes 2359300
  175.9 48.8 %collective-permute-start.19 = (bf16[68,4224]{1,0:T(8,128)(2,1)S(1)}, bf16[68,4224]{1,0:T(8,128)(2,1)S(1)}, u32[]{:S(2)}, u32[]{:S(2)}) collective-permute-start(bf16[68,4224]{1,0:T(8,128)(2,1)S(1)} %get-tuple-element.82), channel_id=1, source_target_pairs={{0,1},{1,0},{2,3},{3,2},{4,5},{5,4},{6,7},{7,6},{8,9},{9,8},{10,11... | collective-permute-start | bytes 1723400 | tf_op jit(solution)/shard_map/ppermute | solution.py:31
  212.2 14.9 %collective-permute-start.26 = (bf16[384,1024]{1,0:T(8,128)(2,1)S(1)}, bf16[384,1024]{1,0:T(8,128)(2,1)S(1)}, u32[]{:S(2)}, u32[]{:S(2)}) collective-permute-start(bf16[384,1024]{1,0:T(8,128)(2,1)S(1)} %get-tuple-element.77), channel_id=1, source_target_pairs={{0,8},{8,0},{16,24},{24,16},{1,9},{9,1},{17,25},{25,17},{2,10},{10... | collective-permute-start | bytes 2359304 | tf_op jit(solution)/shard_map/ppermute | solution.py:31
  212.3 14.8 %collective-permute-start.25 = (bf16[1024,768]{1,0:T(8,128)(2,1)S(1)}, bf16[1024,768]{1,0:T(8,128)(2,1)S(1)}, u32[]{:S(2)}, u32[]{:S(2)}) collective-permute-start(bf16[1024,768]{1,0:T(8,128)(2,1)S(1)} %get-tuple-element.76), channel_id=1, source_target_pairs={{0,8},{8,0},{16,24},{24,16},{1,9},{9,1},{17,25},{25,17},{2,10},{10... | collective-permute-start | bytes 4718600 | tf_op jit(solution)/shard_map/ppermute | solution.py:31
  227.1 2.2 copy-start.1

commit v6 on v5

--- a/solution.py
+++ b/solution.py
@@ -183,7 +183,7 @@
             pltpu.SemaphoreType.DMA((3 + 2 * count, blocks)),
             pltpu.SemaphoreType.DMA((1 + count + count * blocks,)),
         ],
-        compiler_params=pltpu.CompilerParams(vmem_limit_bytes=32 * 1024 * 1024),
+        compiler_params=pltpu.CompilerParams(vmem_limit_bytes=28 * 1024 * 1024),
         name="slot_work",
     )(place, *sum(xs, []), *sum(dys, []), gate_local, up_local, down_local)
     return outs[:count], outs[count], outs[count + 1 :]
@@ -265,7 +265,7 @@
             pltpu.SemaphoreType.DMA((sum(len(pieces) for pieces in cuts),)),
             pltpu.SemaphoreType.DMA((4,)),
         ],
-        compiler_params=pltpu.CompilerParams(vmem_limit_bytes=32 * 1024 * 1024),
+        compiler_params=pltpu.CompilerParams(vmem_limit_bytes=28 * 1024 * 1024),
         name="weight_work",
     )(place, *arrays, *before)
 
@@ -292,7 +292,7 @@
         out_shape=[jax.ShapeDtypeStruct(shape, BF) for shape in shapes],
         in_specs=(tall + wide) * 2,
         out_specs=thin * 2 + wide,
-        compiler_params=pltpu.CompilerParams(vmem_limit_bytes=32 * 1024 * 1024),
+        compiler_params=pltpu.CompilerParams(vmem_limit_bytes=28 * 1024 * 1024),
         name="final_sums",
     )(keep_gu, keep_d, came_gu, came_d)
 

time: 230 us -> 229 us (level)
  local copies, waits for them, and re-layouts: 8.07 us -> 1.5 us
  waiting for transfers between devices: 114 us -> 118 us
    unnamed x56 -> x24, local copies, waits for them, and re-layouts: 7.65 us -> 1.07 us
  transfers between devices with their start and end apart: 27 -> 27, of which waited for: 13 -> 14; matrix products, arithmetic and copies ran while one was open for 5% -> 5% of each run, Pallas kernels for 19% -> 19%
where the time goes in v6:
time: 229 us; the launch traced here: 228 us
  waiting for transfers between devices  118 us (52%)
  starting transfers between devices  49 us (21%)
  Pallas kernels  45.2 us (20%)
  other arithmetic  7.59 us (3%)
  matrix products  5.28 us (2%)
    ppermute x14, waiting for transfers between devices, send_xor(): return lax.ppermute(value, axis, [(i, i ^ mask) for i in range(size)])  50.9 us
    pallas_call x3, Pallas kernels, slot_work(): pl.pallas_call(functools.partial(slot_kernel, blocks, count, choices), ou...  30.7 us
    ppermute x2, waiting for transfers between devices, send_home(): lax.ppermute(value, ('expert', 'seq'), [(i, i ^ mask) for i in range(tota...  27.7 us
    ppermute x1, waiting for transfers between devices, body(): dy_near = lax.ppermute(after(dy_across, dy_first), 'seq', OUTWARD)  20 us
    ppermute x14, starting transfers between devices, send_xor(): return lax.ppermute(value, axis, [(i, i ^ mask) for i in range(size)])  14.9 us
    pallas_call x2, Pallas kernels, weight_work(): pl.pallas_call(functools.partial(weight_kernel, cuts, bool(before), width...  12.3 us
    ppermute x1, waiting for transfers between devices, body(): dy_across = lax.ppermute(after(slot_dy[0], across_far), 'seq', MIDDLE)  11.4 us
    ppermute x2, starting transfers between devices, send_home(): lax.ppermute(value, ('expert', 'seq'), [(i, i ^ mask) for i in range(tota...  6.33 us
  transfers between devices with their start and end apart: 27, of which 14 were waited for; matrix products, arithmetic and copies ran while one was open for 5% of the time, Pallas kernels for 19%

profile of v6, /device:TPU:8, one launch (start us, length us, event | category | flops | bytes accessed | tf_op | source)
XLA Modules:
  0.0 228.1 jit_solution(16148620603372671427)
XLA Ops:
  0.7 0.9 fusion.5
  1.6 0.7 convert_add_fusion
  2.3 0.4 convolution_convert_fusion.3
  2.6 1.6 collective-permute-start
  4.2 0.3 convolution_convert_fusion.4
  4.6 3.6 %collective-permute-start.5 = (bf16[68,4096]{1,0:T(8,128)(2,1)S(1)}, bf16[68,4096]{1,0:T(8,128)(2,1)}, u32[]{:S(2)}, u32[]{:S(2)}) collective-permute-start(bf16[68,4096]{1,0:T(8,128)(2,1)S(1)} %convolution_convert_fusion.4), channel_id=1, source_target_pairs={{1,2},{2,1},{5,6},{6,5},{9,10},{10,9},{13,14},{14,13},{17,18},{18,... | collective-permute-start | bytes 1671176 | tf_op jit(solution)/shard_map/ppermute | solution.py:366
  8.3 1.2 convolution_convert_fusion.1
  9.5 8.4 %collective-permute-done = bf16[68,4096]{1,0:T(8,128)(2,1)} collective-permute-done((bf16[68,4096]{1,0:T(8,128)(2,1)S(1)}, bf16[68,4096]{1,0:T(8,128)(2,1)}, u32[]{:S(2)}, u32[]{:S(2)}) %collective-permute-start) | collective-permute-done | bytes 557088 | tf_op jit(solution)/shard_map/ppermute | solution.py:31
  17.9 1.5 collective-permute-start.3
  19.5 0.3 convolution_convert_fusion.2
  19.8 3.5 %collective-permute-start.6 = (bf16[68,4096]{1,0:T(8,128)(2,1)}, bf16[68,4096]{1,0:T(8,128)(2,1)S(1)}, u32[]{:S(2)}, u32[]{:S(2)}) collective-permute-start(bf16[68,4096]{1,0:T(8,128)(2,1)} %collective-permute-done), channel_id=1, source_target_pairs={{1,2},{2,1},{5,6},{6,5},{9,10},{10,9},{13,14},{14,13},{17,18},{18,... | collective-permute-start | bytes 1671176 | tf_op jit(solution)/shard_map/ppermute | solution.py:368
  23.4 1.3 fusion.12
  24.7 7.6 %collective-permute-done.3 = bf16[68,4096]{1,0:T(8,128)(2,1)S(1)} collective-permute-done((bf16[68,4096]{1,0:T(8,128)(2,1)}, bf16[68,4096]{1,0:T(8,128)(2,1)S(1)}, u32[]{:S(2)}, u32[]{:S(2)}) %collective-permute-start.3) | collective-permute-done | bytes 557088 | tf_op jit(solution)/shard_map/ppermute | solution.py:31
  32.3 0.2 pad_maximum_fusion.1.refs_2_
  32.5 0.6 collective-permute-start.4
  33.1 0.2 fusion.9
  33.5 1.5 collective-permute-start.13
  34.9 0.9 collective-permute-done.6
  35.8 1.4 pad_maximum_fusion.3.refs_1_
  37.2 2.6 %collective-permute-done.2 = bf16[68,4096]{1,0:T(8,128)(2,1)S(1)} collective-permute-done((bf16[68,4096]{1,0:T(8,128)(2,1)}, bf16[68,4096]{1,0:T(8,128)(2,1)S(1)}, u32[]{:S(2)}, u32[]{:S(2)}) %collective-permute-start.2) | collective-permute-done | bytes 557088 | tf_op jit(solution)/shard_map/ppermute | solution.py:31
  39.8 1.4 pad_maximum_fusion.2.refs_1_
  41.2 2.4 %collective-permute-start.7 = (bf16[136,4096]{1,0:T(8,128)(2,1)S(1)}, bf16[136,4096]{1,0:T(8,128)(2,1)S(1)}, u32[]{:S(2)}, u32[]{:S(2)}) collective-permute-start(bf16[136,4096]{1,0:T(8,128)(2,1)S(1)} %pad_maximum_fusion.2.refs_1_), channel_id=1, source_target_pairs={{1,2},{2,1},{5,6},{6,5},{9,10},{10,9},{13,14},{14,13},{17,18},{18,... | collective-permute-start | bytes 3342344 | tf_op jit(solution)/shard_map/ppermute | solution.py:380
  43.6 1.4 collective-permute-start.8
  45.0 3.7 %collective-permute-start.10 = (bf16[136,4096]{1,0:T(8,128)(2,1)S(1)}, bf16[136,4096]{1,0:T(8,128)(2,1)S(1)}, u32[]{:S(2)}, u32[]{:S(2)}) collective-permute-start(bf16[136,4096]{1,0:T(8,128)(2,1)S(1)} %pad_maximum_fusion.1.refs_2_), channel_id=1, source_target_pairs={{1,2},{2,1},{5,6},{6,5},{9,10},{10,9},{13,14},{14,13},{17,18},{18,... | collective-permute-start | bytes 3342344 | tf_op jit(solution)/shard_map/ppermute | solution.py:370
  48.6 1.2 pad_maximum_fusion.refs_0_
  49.9 11.4 %collective-permute-done.4.refs_3_ = bf16[136,4096]{1,0:T(8,128)(2,1)S(1)} collective-permute-done((bf16[136,4096]{1,0:T(8,128)(2,1)S(1)}, bf16[136,4096]{1,0:T(8,128)(2,1)S(1)}, u32[]{:S(2)}, u32[]{:S(2)}) %collective-permute-start.4) | collective-permute-done | bytes 1114144 | tf_op jit(solution)/shard_map/ppermute | solution.py:31
  61.2 13.5 %slot_work.3 = (bf16[136,4224]{1,0:T(8,128)(2,1)S(1)}, bf16[136,4224]{1,0:T(8,128)(2,1)S(1)}, bf16[144,6400]{1,0:T(8,128)(2,1)S(1)}, bf16[144,5248]{1,0:T(8,128)(2,1)S(1)}, bf16[144,5248]{1,0:T(8,128)(2,1)S(1)}) custom-call(s32[3]{0:T(128)S(1)} %pad_add_fusion.place, bf16[136,4096]{1,0:T(8,128)(2,1)S(1)} %pad_maximum_fusion.refs_0_, ...), custom_call_target="tpu_custom_call" | custom-call | tf_op jit(solution)/shard_map/slot_work/pallas_call | solution.py:167
  74.7 1.0 copy-done.5
  75.7 1.5 collective-permute-start.14
  77.2 11.4 %collective-permute-done.10.refs_3_ = bf16[136,4096]{1,0:T(8,128)(2,1)S(1)} collective-permute-done((bf16[136,4096]{1,0:T(8,128)(2,1)S(1)}, bf16[136,4096]{1,0:T(8,128)(2,1)S(1)}, u32[]{:S(2)}, u32[]{:S(2)}) %collective-permute-start.10) | collective-permute-done | bytes 1114144 | tf_op jit(solution)/shard_map/ppermute | solution.py:370
  88.6 1.3 collective-permute-start.11
  90.0 3.5 %collective-permute-start.12 = (bf16[136,4096]{1,0:T(8,128)(2,1)S(1)}, bf16[136,4096]{1,0:T(8,128)(2,1)S(1)}, u32[]{:S(2)}, u32[]{:S(2)}) collective-permute-start(bf16[136,4096]{1,0:T(8,128)(2,1)S(1)} %collective-permute-done.4.refs_3_), channel_id=1, source_target_pairs={{1,2},{2,1},{5,6},{6,5},{9,10},{10,9},{13,14},{14,13},{17,18},{18,... | collective-permute-start | bytes 3342344 | tf_op jit(solution)/shard_map/ppermute | solution.py:382
  93.5 1.4 collective-permute-start.9
  94.9 20.0 %collective-permute-done.11.refs_2_ = bf16[136,4096]{1,0:T(8,128)(2,1)S(1)} collective-permute-done((bf16[136,4096]{1,0:T(8,128)(2,1)S(1)}, bf16[136,4096]{1,0:T(8,128)(2,1)S(1)}, u32[]{:S(2)}, u32[]{:S(2)}) %collective-permute-start.11) | collective-permute-done | bytes 1114144 | tf_op jit(solution)/shard_map/ppermute | solution.py:383
  114.9 8.4 %slot_work.4 = (bf16[136,4224]{1,0:T(8,128)(2,1)}, bf16[144,5248]{1,0:T(8,128)(2,1)S(1)}, bf16[144,5248]{1,0:T(8,128)(2,1)S(1)}) custom-call(s32[3]{0:T(128)S(1)} %pad_add_fusion.place, bf16[136,4096]{1,0:T(8,128)(2,1)S(1)} %collective-permute-done.8.refs_0_, bf16[136,4096]{1,0:T(8,128)(2,1)S(1)} %collective-permute-done.7.refs_1_, ...), custom_call_target="tpu_custom_call" | custom-call | tf_op jit(solution)/shard_map/slot_work/pallas_call | solution.py:167
  123.3 1.6 collective-permute-start.15
  124.9 5.7 %weight_work.2 = (bf16[1024,768]{1,0:T(8,128)(2,1)S(1)}, bf16[384,1024]{1,0:T(8,128)(2,1)S(1)}, bf16[1024,768]{1,0:T(8,128)(2,1)S(1)}, bf16[384,1024]{1,0:T(8,128)(2,1)S(1)}) custom-call(s32[3]{0:T(128)S(1)} %pad_add_fusion.place, bf16[144,5248]{1,0:T(8,128)(2,1)S(1)} %get-tuple-element.63.refs_0_, bf16[144,5248]{1,0:T(8,128)(2,1)S(1)} %get-tuple-element.64.refs_1_, ...), custom_call_target="tpu_custom_call" | custom-call | tf_op jit(solution)/shard_map/weight_work/pallas_call | solution.py:256
  130.7 1.9 collective-permute-done.9.refs_0_
  132.5 4.4 %collective-permute-start.18 = (bf16[136,4224]{1,0:T(8,128)(2,1)}, bf16[136,4224]{1,0:T(8,128)(2,1)S(1)}, u32[]{:S(2)}, u32[]{:S(2)}) collective-permute-start(bf16[136,4224]{1,0:T(8,128)(2,1)} %get-tuple-element.66), channel_id=1, source_target_pairs={{1,2},{2,1},{5,6},{6,5},{9,10},{10,9},{13,14},{14,13},{17,18},{18,... | collective-permute-start | bytes 3446792 | tf_op jit(solution)/shard_map/ppermute | solution.py:406
  136.9 1.4 collective-permute-start.17
  138.4 2.7 %collective-permute-start.16 = (bf16[68,4224]{1,0:T(8,128)(2,1)S(1)}, bf16[68,4224]{1,0:T(8,128)(2,1)S(1)}, u32[]{:S(2)}, u32[]{:S(2)}) collective-permute-start(bf16[68,4224]{1,0:T(8,128)(2,1)S(1)} %slice.44), channel_id=1, source_target_pairs={{0,4},{4,0},{1,5},{5,1},{2,6},{6,2},{3,7},{7,3},{8,12},{12,8},{9,1... | collective-permute-start | bytes 1723400 | tf_op jit(solution)/shard_map/ppermute | solution.py:31
  141.1 1.3 collective-permute-start.20
  142.4 8.2 %collective-permute-done.16 = bf16[68,4224]{1,0:T(8,128)(2,1)S(1)} collective-permute-done((bf16[68,4224]{1,0:T(8,128)(2,1)S(1)}, bf16[68,4224]{1,0:T(8,128)(2,1)S(1)}, u32[]{:S(2)}, u32[]{:S(2)}) %collective-permute-start.16) | collective-permute-done | bytes 574496 | tf_op jit(solution)/shard_map/ppermute | solution.py:31
  150.6 0.7 collective-permute-done.15.refs_1_
  151.3 5.6 %collective-permute-done.17.refs_2_ = bf16[136,4096]{1,0:T(8,128)(2,1)S(1)} collective-permute-done((bf16[136,4096]{1,0:T(8,128)(2,1)S(1)}, bf16[136,4096]{1,0:T(8,128)(2,1)S(1)}, u32[]{:S(2)}, u32[]{:S(2)}) %collective-permute-start.17) | collective-permute-done | bytes 1114144 | tf_op jit(solution)/shard_map/ppermute | solution.py:386
  156.9 8.9 %slot_work.5 = (bf16[136,4224]{1,0:T(8,128)(2,1)S(1)}, bf16[144,5248]{1,0:T(8,128)(2,1)S(1)}, bf16[144,5248]{1,0:T(8,128)(2,1)S(1)}) custom-call(s32[3]{0:T(128)S(1)} %pad_add_fusion.place, bf16[136,4096]{1,0:T(8,128)(2,1)S(1)} %collective-permute-done.9.refs_0_, bf16[136,4096]{1,0:T(8,128)(2,1)S(1)} %pad_maximum_fusion.3.refs_1_, ...), custom_call_target="tpu_custom_call" | custom-call | tf_op jit(solution)/shard_map/slot_work/pallas_call | solution.py:167
  165.8 0.3 add_convert_fusion.1
  166.2 0.1 fusion.37
  166.3 0.3 add_convert_fusion
  166.6 0.1 fusion.38
  166.8 5.2 %collective-permute-start.23 = (bf16[68,4224]{1,0:T(8,128)(2,1)S(1)}, bf16[68,4224]{1,0:T(8,128)(2,1)S(1)}, u32[]{:S(2)}, u32[]{:S(2)}) collective-permute-start(bf16[68,4224]{1,0:T(8,128)(2,1)S(1)} %get-tuple-element.83), channel_id=1, source_target_pairs={{0,7},{1,6},{2,5},{3,4},{4,3},{5,2},{6,1},{7,0},{8,15},{9,14},{10,... | collective-permute-start | bytes 1723400 | tf_op jit(solution)/shard_map/ppermute | solution.py:42
  172.0 1.1 collective-permute-start.22
  173.1 1.5 collective-permute-start.24
  174.6 1.8 collective-permute-start.19
  176.4 27.7 %collective-permute-done.23 = bf16[68,4224]{1,0:T(8,128)(2,1)S(1)} collective-permute-done((bf16[68,4224]{1,0:T(8,128)(2,1)S(1)}, bf16[68,4224]{1,0:T(8,128)(2,1)S(1)}, u32[]{:S(2)}, u32[]{:S(2)}) %collective-permute-start.23) | collective-permute-done | bytes 574496 | tf_op jit(solution)/shard_map/ppermute | solution.py:42
  204.1 0.2 add_convert_fusion.2
  204.4 6.6 %weight_work.3 = (bf16[1024,768]{1,0:T(8,128)(2,1)S(1)}, bf16[384,1024]{1,0:T(8,128)(2,1)S(1)}, bf16[1024,768]{1,0:T(8,128)(2,1)S(1)}, bf16[384,1024]{1,0:T(8,128)(2,1)S(1)}) custom-call(s32[3]{0:T(128)S(1)} %pad_add_fusion.place, bf16[144,5248]{1,0:T(8,128)(2,1)S(1)} %get-tuple-element.67.refs_0_, bf16[144,5248]{1,0:T(8,128)(2,1)S(1)} %collective-permute-done.15.refs_1_, ...), custom_call_target="tpu_custom_call" | custom-call | tf_op jit(solution)/shard_map/weight_work/pallas_call | solution.py:256
  211.0 0.5 collective-permute-start.25
  211.5 8.3 %collective-permute-done.21 = bf16[68,4224]{1,0:T(8,128)(2,1)S(1)} collective-permute-done((bf16[68,4224]{1,0:T(8,128)(2,1)S(1)}, bf16[68,4224]{1,0:T(8,128)(2,1)S(1)}, u32[]{:S(2)}, u32[]{:S(2)}) %collective-permute-start.21) | collective-permute-done | bytes 574496 | tf_op jit(solution)/shard_map/ppermute | solution.py:31
  219.8 3.7 %collective-permute-done.19 = bf16[68,4224]{1,0:T(8,128)(2,1)S(1)} collective-permute-done((bf16[68,4224]{1,0:T(8,128)(2,1)S(1)}, bf16[68,4224]{1,0:T(8,128)(2,1)S(1)}, u32[]{:S(2)}, u32[]{:S(2)}) %collective-permute-start.19) | collective-permute-done | bytes 574496 | tf_op jit(solution)/shard_map/ppermute | solution.py:31
  223.5 0.2 add_convert_fusion.3
  223.7 0.7 fusion.7
  224.4 1.5 convolution_convert_fusion
  225.9 2.2 final_sums.1
  (44 shorter events, 0.7 us)
Async XLA Ops:
  0.6 1.6 copy-start
  2.6 5.7 %copy-start.9 = (bf16[128,4096]{1,0:T(8,128)(2,1)S(1)}, bf16[128,4096]{1,0:T(8,128)(2,1)}, u32[]{:S(2)}) copy-start(bf16[128,4096]{1,0:T(8,128)(2,1)} %param.8) | copy-start | bytes 3145732
  2.6 5.7 %copy-start.11 = (bf16[128]{0:T(256)(128)(2,1)S(1)}, bf16[128]{0:T(256)(128)(2,1)}, u32[]{:S(2)}) copy-start(bf16[128]{0:T(256)(128)(2,1)} %param.9) | copy-start | bytes 772
  2.6 15.2 %collective-permute-start = (bf16[68,4096]{1,0:T(8,128)(2,1)S(1)}, bf16[68,4096]{1,0:T(8,128)(2,1)}, u32[]{:S(2)}, u32[]{:S(2)}) collective-permute-start(bf16[68,4096]{1,0:T(8,128)(2,1)S(1)} %convolution_convert_fusion.3), channel_id=1, source_target_pairs={{0,4},{4,0},{1,5},{5,1},{2,6},{6,2},{3,7},{7,3},{8,12},{12,8},{9,1... | collective-permute-start | bytes 1671176 | tf_op jit(solution)/shard_map/ppermute | solution.py:31
  4.6 14.9 %copy-start.10 = (bf16[128,4096]{1,0:T(8,128)(2,1)S(1)}, bf16[128,4096]{1,0:T(8,128)(2,1)}, u32[]{:S(2)}) copy-start(bf16[128,4096]{1,0:T(8,128)(2,1)} %param.8) | copy-start | bytes 3145732
  4.6 28.9 %collective-permute-start.5 = (bf16[68,4096]{1,0:T(8,128)(2,1)S(1)}, bf16[68,4096]{1,0:T(8,128)(2,1)}, u32[]{:S(2)}, u32[]{:S(2)}) collective-permute-start(bf16[68,4096]{1,0:T(8,128)(2,1)S(1)} %convolution_convert_fusion.4), channel_id=1, source_target_pairs={{1,2},{2,1},{5,6},{6,5},{9,10},{10,9},{13,14},{14,13},{17,18},{18,... | collective-permute-start | bytes 1671176 | tf_op jit(solution)/shard_map/ppermute | solution.py:366
  8.2 29.0 %collective-permute-start.1 = (bf16[68,4096]{1,0:T(8,128)(2,1)S(1)}, bf16[68,4096]{1,0:T(8,128)(2,1)}, u32[]{:S(2)}, u32[]{:S(2)}) collective-permute-start(bf16[68,4096]{1,0:T(8,128)(2,1)S(1)} %convolution_convert_fusion.4), channel_id=1, source_target_pairs={{0,1},{1,0},{2,3},{3,2},{4,5},{5,4},{6,7},{7,6},{8,9},{9,8},{10,11... | collective-permute-start | bytes 1671176 | tf_op jit(solution)/shard_map/ppermute | solution.py:31
  17.9 14.4 %collective-permute-start.3 = (bf16[68,4096]{1,0:T(8,128)(2,1)}, bf16[68,4096]{1,0:T(8,128)(2,1)S(1)}, u32[]{:S(2)}, u32[]{:S(2)}) collective-permute-start(bf16[68,4096]{1,0:T(8,128)(2,1)} %convolution_convert_fusion.1), channel_id=1, source_target_pairs={{0,4},{4,0},{1,5},{5,1},{2,6},{6,2},{3,7},{7,3},{8,12},{12,8},{9,1... | collective-permute-start | bytes 1671176 | tf_op jit(solution)/shard_map/ppermute | solution.py:31
  19.8 16.0 %collective-permute-start.6 = (bf16[68,4096]{1,0:T(8,128)(2,1)}, bf16[68,4096]{1,0:T(8,128)(2,1)S(1)}, u32[]{:S(2)}, u32[]{:S(2)}) collective-permute-start(bf16[68,4096]{1,0:T(8,128)(2,1)} %collective-permute-done), channel_id=1, source_target_pairs={{1,2},{2,1},{5,6},{6,5},{9,10},{10,9},{13,14},{14,13},{17,18},{18,... | collective-permute-start | bytes 1671176 | tf_op jit(solution)/shard_map/ppermute | solution.py:368
  23.3 16.5 %collective-permute-start.2 = (bf16[68,4096]{1,0:T(8,128)(2,1)}, bf16[68,4096]{1,0:T(8,128)(2,1)S(1)}, u32[]{:S(2)}, u32[]{:S(2)}) collective-permute-start(bf16[68,4096]{1,0:T(8,128)(2,1)} %collective-permute-done), channel_id=1, source_target_pairs={{0,1},{1,0},{2,3},{3,2},{4,5},{5,4},{6,7},{7,6},{8,9},{9,8},{10,11... | collective-permute-start | bytes 1671176 | tf_op jit(solution)/shard_map/ppermute | solution.py:31
  32.5 28.8 %collective-permute-start.4 = (bf16[136,4096]{1,0:T(8,128)(2,1)S(1)}, bf16[136,4096]{1,0:T(8,128)(2,1)S(1)}, u32[]{:S(2)}, u32[]{:S(2)}) collective-permute-start(bf16[136,4096]{1,0:T(8,128)(2,1)S(1)} %pad_maximum_fusion.1.refs_2_), channel_id=1, source_target_pairs={{0,1},{1,0},{2,3},{3,2},{4,5},{5,4},{6,7},{7,6},{8,9},{9,8},{10,11... | collective-permute-start | bytes 3342344 | tf_op jit(solution)/shard_map/ppermute | solution.py:31
  33.1 28.2 %copy-start.4 = (bf16[1,384,4096]{2,1,0:T(8,128)(2,1)S(1)}, bf16[1,384,4096]{2,1,0:T(8,128)(2,1)}, u32[]{:S(2)}) copy-start(bf16[1,384,4096]{2,1,0:T(8,128)(2,1)} %param.13) | copy-start | bytes 9437188
  33.5 42.3 %collective-permute-start.13 = (bf16[144,4096]{1,0:T(8,128)(2,1)S(1)}, bf16[144,4096]{1,0:T(8,128)(2,1)S(1)}, u32[]{:S(2)}, u32[]{:S(2)}) collective-permute-start(bf16[144,4096]{1,0:T(8,128)(2,1)S(1)} %fusion.2), channel_id=1, source_target_pairs={{0,16},{8,24},{16,0},{24,8},{1,17},{9,25},{17,1},{25,9},{2,18},{10... | collective-permute-start | bytes 3538952 | tf_op jit(solution)/shard_map/ppermute | solution.py:31
  35.8 25.4 %copy-start.3 = (bf16[1,4096,384]{2,1,0:T(8,128)(2,1)S(1)}, bf16[1,4096,384]{2,1,0:T(8,128)(2,1)}, u32[]{:S(2)}) copy-start(bf16[1,4096,384]{2,1,0:T(8,128)(2,1)} %param.12) | copy-start | bytes 9437188
  39.8 21.4 %copy-start.2 = (bf16[1,4096,384]{2,1,0:T(8,128)(2,1)S(1)}, bf16[1,4096,384]{2,1,0:T(8,128)(2,1)}, u32[]{:S(2)}) copy-start(bf16[1,4096,384]{2,1,0:T(8,128)(2,1)} %param.11) | copy-start | bytes 9437188
  41.2 52.3 %collective-permute-start.7 = (bf16[136,4096]{1,0:T(8,128)(2,1)S(1)}, bf16[136,4096]{1,0:T(8,128)(2,1)S(1)}, u32[]{:S(2)}, u32[]{:S(2)}) collective-permute-start(bf16[136,4096]{1,0:T(8,128)(2,1)S(1)} %pad_maximum_fusion.2.refs_1_), channel_id=1, source_target_pairs={{1,2},{2,1},{5,6},{6,5},{9,10},{10,9},{13,14},{14,13},{17,18},{18,... | collective-permute-start | bytes 3342344 | tf_op jit(solution)/shard_map/ppermute | solution.py:380
  43.6 49.9 %collective-permute-start.8 = (bf16[136,4096]{1,0:T(8,128)(2,1)S(1)}, bf16[136,4096]{1,0:T(8,128)(2,1)S(1)}, u32[]{:S(2)}, u32[]{:S(2)}) collective-permute-start(bf16[136,4096]{1,0:T(8,128)(2,1)S(1)} %pad_maximum_fusion.3.refs_1_), channel_id=1, source_target_pairs={{1,0},{2,3},{5,4},{6,7},{9,8},{10,11},{13,12},{14,15},{17,16},{18,... | collective-permute-start | bytes 3342344 | tf_op jit(solution)/shard_map/ppermute | solution.py:381
  45.0 43.7 %collective-permute-start.10 = (bf16[136,4096]{1,0:T(8,128)(2,1)S(1)}, bf16[136,4096]{1,0:T(8,128)(2,1)S(1)}, u32[]{:S(2)}, u32[]{:S(2)}) collective-permute-start(bf16[136,4096]{1,0:T(8,128)(2,1)S(1)} %pad_maximum_fusion.1.refs_2_), channel_id=1, source_target_pairs={{1,2},{2,1},{5,6},{6,5},{9,10},{10,9},{13,14},{14,13},{17,18},{18,... | collective-permute-start | bytes 3342344 | tf_op jit(solution)/shard_map/ppermute | solution.py:370
  74.7 1.0 copy-start.5
  75.7 47.6 %collective-permute-start.14 = (bf16[144,6400]{1,0:T(8,128)(2,1)S(1)}, bf16[144,6400]{1,0:T(8,128)(2,1)S(1)}, u32[]{:S(2)}, u32[]{:S(2)}) collective-permute-start(bf16[144,6400]{1,0:T(8,128)(2,1)S(1)} %get-tuple-element.56), channel_id=1, source_target_pairs={{0,16},{8,24},{16,0},{24,8},{1,17},{9,25},{17,1},{25,9},{2,18},{10... | collective-permute-start | bytes 5529608 | tf_op jit(solution)/shard_map/ppermute | solution.py:31
  88.6 34.7 %copy-start.7 = (bf16[136,4096]{1,0:T(8,128)(2,1)}, bf16[136,4096]{1,0:T(8,128)(2,1)S(1)}, u32[]{:S(2)}) copy-start(bf16[136,4096]{1,0:T(8,128)(2,1)S(1)} %collective-permute-done.10.refs_3_) | copy-start | bytes 3342340
  88.6 26.3 %collective-permute-start.11 = (bf16[136,4096]{1,0:T(8,128)(2,1)S(1)}, bf16[136,4096]{1,0:T(8,128)(2,1)S(1)}, u32[]{:S(2)}, u32[]{:S(2)}) collective-permute-start(bf16[136,4096]{1,0:T(8,128)(2,1)S(1)} %collective-permute-done.10.refs_3_), channel_id=1, source_target_pairs={{1,0},{2,3},{5,4},{6,7},{9,8},{10,11},{13,12},{14,15},{17,16},{18,... | collective-permute-start | bytes 3342344 | tf_op jit(solution)/shard_map/ppermute | solution.py:383
  90.0 24.9 %collective-permute-start.12 = (bf16[136,4096]{1,0:T(8,128)(2,1)S(1)}, bf16[136,4096]{1,0:T(8,128)(2,1)S(1)}, u32[]{:S(2)}, u32[]{:S(2)}) collective-permute-start(bf16[136,4096]{1,0:T(8,128)(2,1)S(1)} %collective-permute-done.4.refs_3_), channel_id=1, source_target_pairs={{1,2},{2,1},{5,6},{6,5},{9,10},{10,9},{13,14},{14,13},{17,18},{18,... | collective-permute-start | bytes 3342344 | tf_op jit(solution)/shard_map/ppermute | solution.py:382
  93.5 39.0 %collective-permute-start.9 = (bf16[136,4096]{1,0:T(8,128)(2,1)S(1)}, bf16[136,4096]{1,0:T(8,128)(2,1)S(1)}, u32[]{:S(2)}, u32[]{:S(2)}) collective-permute-start(bf16[136,4096]{1,0:T(8,128)(2,1)S(1)} %collective-permute-done.7.refs_1_), channel_id=1, source_target_pairs={{1,0},{2,3},{5,4},{6,7},{9,8},{10,11},{13,12},{14,15},{17,16},{18,... | collective-permute-start | bytes 3342344 | tf_op jit(solution)/shard_map/ppermute | solution.py:385
  123.3 28.0 %collective-permute-start.15 = (bf16[144,5248]{1,0:T(8,128)(2,1)S(1)}, bf16[144,5248]{1,0:T(8,128)(2,1)S(1)}, u32[]{:S(2)}, u32[]{:S(2)}) collective-permute-start(bf16[144,5248]{1,0:T(8,128)(2,1)S(1)} %get-tuple-element.57), channel_id=1, source_target_pairs={{0,16},{8,24},{16,0},{24,8},{1,17},{9,25},{17,1},{25,9},{2,18},{10... | collective-permute-start | bytes 4534280 | tf_op jit(solution)/shard_map/ppermute | solution.py:31
  130.6 26.3 %copy-start.8 = (bf16[136,4096]{1,0:T(8,128)(2,1)S(1)}, bf16[136,4096]{1,0:T(8,128)(2,1)}, u32[]{:S(2)}) copy-start(bf16[136,4096]{1,0:T(8,128)(2,1)} %copy-done.7) | copy-start | bytes 3342340
  132.5 33.3 %collective-permute-start.18 = (bf16[136,4224]{1,0:T(8,128)(2,1)}, bf16[136,4224]{1,0:T(8,128)(2,1)S(1)}, u32[]{:S(2)}, u32[]{:S(2)}) collective-permute-start(bf16[136,4224]{1,0:T(8,128)(2,1)} %get-tuple-element.66), channel_id=1, source_target_pairs={{1,2},{2,1},{5,6},{6,5},{9,10},{10,9},{13,14},{14,13},{17,18},{18,... | collective-permute-start | bytes 3446792 | tf_op jit(solution)/shard_map/ppermute | solution.py:406
  136.9 20.0 %collective-permute-start.17 = (bf16[136,4096]{1,0:T(8,128)(2,1)S(1)}, bf16[136,4096]{1,0:T(8,128)(2,1)S(1)}, u32[]{:S(2)}, u32[]{:S(2)}) collective-permute-start(bf16[136,4096]{1,0:T(8,128)(2,1)S(1)} %collective-permute-done.12.refs_3_), channel_id=1, source_target_pairs={{1,0},{2,3},{5,4},{6,7},{9,8},{10,11},{13,12},{14,15},{17,16},{18,... | collective-permute-start | bytes 3342344 | tf_op jit(solution)/shard_map/ppermute | solution.py:386
  138.4 27.4 %copy-start.6 = (bf16[136,4224]{1,0:T(8,128)(2,1)S(1)}, bf16[136,4224]{1,0:T(8,128)(2,1)}, u32[]{:S(2)}) copy-start(bf16[136,4224]{1,0:T(8,128)(2,1)} %copy-done.5) | copy-start | bytes 3446788
  138.4 12.2 %collective-permute-start.16 = (bf16[68,4224]{1,0:T(8,128)(2,1)S(1)}, bf16[68,4224]{1,0:T(8,128)(2,1)S(1)}, u32[]{:S(2)}, u32[]{:S(2)}) collective-permute-start(bf16[68,4224]{1,0:T(8,128)(2,1)S(1)} %slice.44), channel_id=1, source_target_pairs={{0,4},{4,0},{1,5},{5,1},{2,6},{6,2},{3,7},{7,3},{8,12},{12,8},{9,1... | collective-permute-start | bytes 1723400 | tf_op jit(solution)/shard_map/ppermute | solution.py:31
  141.1 25.2 %collective-permute-start.20 = (bf16[136,4224]{1,0:T(8,128)(2,1)}, bf16[136,4224]{1,0:T(8,128)(2,1)S(1)}, u32[]{:S(2)}, u32[]{:S(2)}) collective-permute-start(bf16[136,4224]{1,0:T(8,128)(2,1)} %get-tuple-element.66), channel_id=1, source_target_pairs={{0,1},{3,2},{4,5},{7,6},{8,9},{11,10},{12,13},{15,14},{16,17},{19,... | collective-permute-start | bytes 3446792 | tf_op jit(solution)/shard_map/ppermute | solution.py:407
  166.8 37.3 %collective-permute-start.23 = (bf16[68,4224]{1,0:T(8,128)(2,1)S(1)}, bf16[68,4224]{1,0:T(8,128)(2,1)S(1)}, u32[]{:S(2)}, u32[]{:S(2)}) collective-permute-start(bf16[68,4224]{1,0:T(8,128)(2,1)S(1)} %get-tuple-element.83), channel_id=1, source_target_pairs={{0,7},{1,6},{2,5},{3,4},{4,3},{5,2},{6,1},{7,0},{8,15},{9,14},{10,... | collective-permute-start | bytes 1723400 | tf_op jit(solution)/shard_map/ppermute | solution.py:42
  172.0 32.1 %collective-permute-start.22 = (bf16[68,4224]{1,0:T(8,128)(2,1)S(1)}, bf16[68,4224]{1,0:T(8,128)(2,1)S(1)}, u32[]{:S(2)}, u32[]{:S(2)}) collective-permute-start(bf16[68,4224]{1,0:T(8,128)(2,1)S(1)} %get-tuple-element.81), channel_id=1, source_target_pairs={{0,5},{1,4},{2,7},{3,6},{4,1},{5,0},{6,3},{7,2},{8,13},{9,12},{10,... | collective-permute-start | bytes 1723400 | tf_op jit(solution)/shard_map/ppermute | solution.py:42
  173.1 31.2 %collective-permute-start.24 = (bf16[144,5248]{1,0:T(8,128)(2,1)S(1)}, bf16[144,5248]{1,0:T(8,128)(2,1)S(1)}, u32[]{:S(2)}, u32[]{:S(2)}) collective-permute-start(bf16[144,5248]{1,0:T(8,128)(2,1)S(1)} %get-tuple-element.70), channel_id=1, source_target_pairs={{0,16},{8,24},{16,0},{24,8},{1,17},{9,25},{17,1},{25,9},{2,18},{10... | collective-permute-start | bytes 4534280 | tf_op jit(solution)/shard_map/ppermute | solution.py:31
  174.6 45.2 %collective-permute-start.21 = (bf16[68,4224]{1,0:T(8,128)(2,1)S(1)}, bf16[68,4224]{1,0:T(8,128)(2,1)S(1)}, u32[]{:S(2)}, u32[]{:S(2)}) collective-permute-start(bf16[68,4224]{1,0:T(8,128)(2,1)S(1)} %get-tuple-element.84), channel_id=1, source_target_pairs={{0,3},{1,2},{2,1},{3,0},{4,7},{5,6},{6,5},{7,4},{8,11},{9,10},{10,... | collective-permute-start | bytes 1723400 | tf_op jit(solution)/shard_map/ppermute | solution.py:31
  174.6 48.8 %collective-permute-start.19 = (bf16[68,4224]{1,0:T(8,128)(2,1)S(1)}, bf16[68,4224]{1,0:T(8,128)(2,1)S(1)}, u32[]{:S(2)}, u32[]{:S(2)}) collective-permute-start(bf16[68,4224]{1,0:T(8,128)(2,1)S(1)} %get-tuple-element.82), channel_id=1, source_target_pairs={{0,1},{1,0},{2,3},{3,2},{4,5},{5,4},{6,7},{7,6},{8,9},{9,8},{10,11... | collective-permute-start | bytes 1723400 | tf_op jit(solution)/shard_map/ppermute | solution.py:31
  210.9 15.0 %collective-permute-start.26 = (bf16[384,1024]{1,0:T(8,128)(2,1)S(1)}, bf16[384,1024]{1,0:T(8,128)(2,1)S(1)}, u32[]{:S(2)}, u32[]{:S(2)}) collective-permute-start(bf16[384,1024]{1,0:T(8,128)(2,1)S(1)} %get-tuple-element.77), channel_id=1, source_target_pairs={{0,8},{8,0},{16,24},{24,16},{1,9},{9,1},{17,25},{25,17},{2,10},{10... | collective-permute-start | bytes 2359304 | tf_op jit(solution)/shard_map/ppermute | solution.py:31
  211.0 14.9 %collective-permute-start.25 = (bf16[1024,768]{1,0:T(8,128)(2,1)S(1)}, bf16[1024,768]{1,0:T(8,128)(2,1)S(1)}, u32[]{:S(2)}, u32[]{:S(2)}) collective-permute-start(bf16[1024,768]{1,0:T(8,128)(2,1)S(1)} %get-tuple-element.76), channel_id=1, source_target_pairs={{0,8},{8,0},{16,24},{24,16},{1,9},{9,1},{17,25},{25,17},{2,10},{10... | collective-permute-start | bytes 4718600 | tf_op jit(solution)/shard_map/ppermute | solution.py:31
  225.9 2.2 copy-start.1
